TPU v7x, 32 devices: a whole 2x2x4 slice. The times are simulated.
32 devices in a mesh: dp: 16 (over z, y, x), mp: 2 (over core).
Axes of the slice: x: 2, y: 2, z: 4, core: 2. Of those that a mesh axis runs over, the one named last changes fastest.
Arguments:
- acoustic: bfloat16 [4096, 512], P('dp'), may hold values from -6 to 6
- memory: bfloat16 [32768, 512], P('dp'), may hold values from -6 to 6
- embedding: bfloat16 [8404, 512], replicated, may hold values from -6 to 6
- w_query: bfloat16 [512, 512], P(None, 'mp'), may hold values from -0.25 to 0.25
- w_key: bfloat16 [512, 512], P(None, 'mp'), may hold values from -0.25 to 0.25
- w_value: bfloat16 [512, 512], P(None, 'mp'), may hold values from -0.25 to 0.25
- w_out: bfloat16 [512, 512], P('mp'), may hold values from -2 to 2
- w_in: bfloat16 [512, 2048], P(None, 'mp'), may hold values from -0.25 to 0.25
- w_back: bfloat16 [2048, 512], P('mp'), may hold values from -0.1875 to 0.1875
- w_vocab: bfloat16 [512, 8404], P(None, 'mp'), may hold values from -0.25 to 0.25
- gain_one: float32 [512], replicated, may hold values from 0.5 to 1.5
- bias_one: float32 [512], replicated, may hold values from -3 to 3
- gain_two: float32 [512], replicated, may hold values from 0.5 to 1.5
- bias_two: float32 [512], replicated, may hold values from -3 to 3
- fsmn_kernel: float32 [11, 512], replicated, may hold values from -1.75 to 1.75
- rate_table: float32 [2, 512], replicated, may hold values from -3 to 3
- token_lengths: int32 [32], P('dp'), may hold values from 1 to 128, 3072 in all
- memory_lengths: int32 [32], P('dp'), may hold values from 1 to 1024, 24576 in all
- rate_groups: int32 [32], P('dp'), may hold values from 0 to 1
- glance_mask: int32 [4096], P('dp'), may hold values 0 or 1
- targets: int32 [4096], P('dp'), may hold values from 0 to 8403
Outputs:
- token_loss: float32 [4096], P('dp')
- grad_acoustic: float32 [4096, 512], P('dp')
- grad_memory: float32 [32768, 512], P('dp', 'mp')
- grad_embedding: float32 [8404, 512], P(None, 'dp')
- grad_query: float32 [512, 512], P('dp', 'mp')
- grad_key: float32 [512, 512], P('dp', 'mp')
- grad_value: float32 [512, 512], P('dp', 'mp')
- grad_out: float32 [512, 512], P('mp', 'dp')
- grad_in: float32 [512, 2048], P('dp', 'mp')
- grad_back: float32 [2048, 512], P('mp', 'dp')
- grad_vocab: float32 [512, 8404], P('dp', 'mp')
- grad_gain_one: float32 [512], P('dp')
- grad_bias_one: float32 [512], P('dp')
- grad_gain_two: float32 [512], P('dp')
- grad_bias_two: float32 [512], P('dp')
- grad_kernel: float32 [11, 512], P(None, 'dp')
- grad_rate: float32 [2, 512], replicated
Inputs may be any that keep to these rules, and one draw needn't show every extreme that they name: Utterance u occupies the first token_lengths[u] of its 128 token slots. Utterance u occupies the first memory_lengths[u] of its 1024 frame slots.
All inputs are finite; a program needn't handle non-finite values. No bound on the sum of `token_lengths` or of `memory_lengths` or of `glance_mask` on one device may be relied on, other than what follows from the above.
Results may differ from a plain program's by a relative error of at most 0.025.
Values sent between devices are 32-bit elements; how exact they have to be, the bound alone decides.
A program may use at most 192 MiB of HBM per device.

v0:
```python
from functools import partial
import math

import jax
import jax.numpy as jnp
from jax import lax
from jax.sharding import PartitionSpec as P

HD = 128
V = 8404


EPSILON = 1e-05


def norm_rows(row_values, gain_vector, bias_vector):
    average = jnp.mean(row_values, axis=-1, keepdims=True)
    centred = row_values - average
    variance = jnp.mean(centred * centred, axis=-1, keepdims=True)
    return centred * lax.rsqrt(variance + EPSILON) * gain_vector + bias_vector


def memory_block(activations, kernel, valid_mask):
    half_width = kernel.shape[0] // 2
    token_slots = activations.shape[1]
    padded = jnp.pad(activations * valid_mask, ((0, 0), (half_width, half_width), (0, 0)))
    summed = jnp.zeros_like(activations)
    for position in range(kernel.shape[0]):
        summed = summed + kernel[position] * padded[:, position : position + token_slots]
    return summed * valid_mask


def product(left_side, right_side):
    return jnp.dot(left_side, right_side, preferred_element_type=jnp.float32)


def product_left(left_side, right_side):
    return lax.dot_general(
        left_side, right_side, (((0,), (0,)), ((), ())), preferred_element_type=jnp.float32
    )


def product_right(left_side, right_side):
    return lax.dot_general(
        left_side, right_side, (((1,), (1,)), ((), ())), preferred_element_type=jnp.float32
    )


def logit_stats(logits, target_ids, offset):
    vocab_ids = offset + lax.broadcasted_iota(jnp.int32, logits.shape, 1)
    onehot = (vocab_ids == target_ids[:, None]).astype(jnp.float32)
    picked = jnp.sum(onehot * logits, axis=1)
    local_top = jnp.max(logits, axis=1)
    top_value = lax.pmax(local_top, "mp")
    denominator, picked = lax.psum(
        (jnp.sum(jnp.exp(logits - top_value[:, None]), axis=1), picked), "mp"
    )
    return (top_value + jnp.log(denominator), picked, onehot)


def attention_scores(query_rows, key_rows, valid_mem, score_scale):
    scores = (
        jnp.einsum("uthd,umhd->uhtm", query_rows, key_rows, preferred_element_type=jnp.float32)
        * score_scale
    )
    return jnp.where(valid_mem[:, None, None, :], scores, -1e30)


def per_device(
    acoustic,
    memory,
    embedding,
    w_query,
    w_key,
    w_value,
    w_out,
    w_in,
    w_back,
    w_vocab,
    gain_one,
    bias_one,
    gain_two,
    bias_two,
    fsmn_kernel,
    rate_table,
    token_lengths,
    memory_lengths,
    rate_groups,
    glance_mask,
    targets,
):
    utterances = token_lengths.shape[0]
    tok_rows, model_width = acoustic.shape
    token_slots = tok_rows // utterances
    frames = memory.shape[0] // utterances
    heads_here = w_query.shape[1] // HD
    offset = lax.axis_index("mp") * w_vocab.shape[1]
    score_scale = 1.0 / math.sqrt(HD)
    valid_tok = (
        lax.broadcasted_iota(jnp.int32, (utterances, token_slots), 1) < token_lengths[:, None]
    ).astype(jnp.float32)
    valid_mem = lax.broadcasted_iota(jnp.int32, (utterances, frames), 1) < memory_lengths[:, None]
    valid_rows = valid_tok.reshape(tok_rows)
    rate_rows = jnp.where(rate_groups[:, None, None] == 1, rate_table[1], rate_table[0])
    mem_low = (
        (memory.astype(jnp.float32).reshape(utterances, frames, model_width) + rate_rows)
        .astype(jnp.bfloat16)
        .reshape(utterances * frames, model_width)
    )
    key_rows = (
        product(mem_low, w_key).astype(jnp.bfloat16).reshape(utterances, frames, heads_here, HD)
    )
    value_rows = (
        product(mem_low, w_value).astype(jnp.bfloat16).reshape(utterances, frames, heads_here, HD)
    )

    def conv_rows(activations, kernel):
        shaped = activations.reshape(utterances, token_slots, model_width)
        return memory_block(shaped, kernel, valid_tok[:, :, None]).reshape(tok_rows, model_width)

    def decoder_pass(stream_in):
        norm_one, back_one = jax.vjp(norm_rows, stream_in, gain_one, bias_one)
        convolved, back_conv = jax.vjp(conv_rows, norm_one, fsmn_kernel)
        stream_one = stream_in + convolved
        stream_low = stream_one.astype(jnp.bfloat16)
        query_rows = (
            product(stream_low, w_query)
            .astype(jnp.bfloat16)
            .reshape(utterances, token_slots, heads_here, HD)
        )
        scores = attention_scores(query_rows, key_rows, valid_mem, score_scale)
        score_top = jnp.max(scores, axis=-1, keepdims=True)
        raised = jnp.exp(scores - score_top)
        score_sum = jnp.sum(raised, axis=-1, keepdims=True)
        probs_low = (raised / score_sum).astype(jnp.bfloat16)
        mixed_heads = (
            jnp.einsum("uhtm,umhd->uthd", probs_low, value_rows, preferred_element_type=jnp.float32)
            .astype(jnp.bfloat16)
            .reshape(tok_rows, heads_here * HD)
        )
        stream_two = stream_one + lax.psum(product(mixed_heads, w_out), "mp")
        norm_two, back_two = jax.vjp(norm_rows, stream_two, gain_two, bias_two)
        norm_low = norm_two.astype(jnp.bfloat16)
        activated, back_act = jax.vjp(
            partial(jax.nn.gelu, approximate=False), product(norm_low, w_in)
        )
        hidden = activated.astype(jnp.bfloat16)
        stream_three = stream_two + lax.psum(product(hidden, w_back), "mp")
        top_low = stream_three.astype(jnp.bfloat16)
        logits = product(top_low, w_vocab)
        log_total, picked, onehot = logit_stats(logits, targets, offset)
        token_loss = (log_total - picked) * valid_rows
        saved_state = (
            back_one,
            back_conv,
            stream_low,
            query_rows,
            score_top + jnp.log(score_sum),
            mixed_heads,
            back_two,
            norm_low,
            back_act,
            hidden,
            top_low,
            logits,
            log_total,
            onehot,
        )
        return (token_loss, saved_state)

    acoustic_wide = acoustic.astype(jnp.float32)
    first_loss, unused = decoder_pass(acoustic_wide)
    blend_weight = (
        glance_mask.astype(jnp.float32) * valid_rows * jax.nn.sigmoid(first_loss - math.log(V))
    )
    rows_taken = embedding[targets].astype(jnp.float32)
    stream_in = acoustic_wide + blend_weight[:, None] * (rows_taken - acoustic_wide)
    token_loss, saved_state = decoder_pass(stream_in)
    (
        back_one,
        back_conv,
        stream_low,
        query_rows,
        score_log,
        mixed_heads,
        back_two,
        norm_low,
        back_act,
        hidden,
        top_low,
        logits,
        log_total,
        onehot,
    ) = saved_state
    grad_logits = ((jnp.exp(logits - log_total[:, None]) - onehot) * valid_rows[:, None]).astype(
        jnp.bfloat16
    )
    grad_vocab = product_left(top_low, grad_logits)
    grad_three = lax.psum(product_right(grad_logits, w_vocab), "mp")
    grad_branch = grad_three.astype(jnp.bfloat16)
    grad_back = product_left(hidden, grad_branch)
    grad_pre = back_act(product_right(grad_branch, w_back))[0].astype(jnp.bfloat16)
    grad_in = product_left(norm_low, grad_pre)
    grad_norm_two = lax.psum(product_right(grad_pre, w_in), "mp")
    grad_two_norm, grad_gain_two, grad_bias_two = back_two(grad_norm_two)
    grad_two = grad_three + grad_two_norm
    grad_attended = grad_two.astype(jnp.bfloat16)
    grad_out = product_left(mixed_heads, grad_attended)
    grad_mixed = (
        product_right(grad_attended, w_out)
        .astype(jnp.bfloat16)
        .reshape(utterances, token_slots, heads_here, HD)
    )
    scores = attention_scores(query_rows, key_rows, valid_mem, score_scale)
    attention_probs = jnp.exp(scores - score_log)
    probs_low = attention_probs.astype(jnp.bfloat16)
    grad_probs = jnp.einsum(
        "uthd,umhd->uhtm", grad_mixed, value_rows, preferred_element_type=jnp.float32
    )
    grad_values = (
        jnp.einsum("uhtm,uthd->umhd", probs_low, grad_mixed, preferred_element_type=jnp.float32)
        .astype(jnp.bfloat16)
        .reshape(utterances * frames, heads_here * HD)
    )
    grad_scores = (
        attention_probs
        * (grad_probs - jnp.sum(attention_probs * grad_probs, axis=-1, keepdims=True))
    ).astype(jnp.bfloat16)
    grad_queries = (
        (
            jnp.einsum("uhtm,umhd->uthd", grad_scores, key_rows, preferred_element_type=jnp.float32)
            * score_scale
        )
        .astype(jnp.bfloat16)
        .reshape(tok_rows, heads_here * HD)
    )
    grad_keys = (
        (
            jnp.einsum(
                "uhtm,uthd->umhd", grad_scores, query_rows, preferred_element_type=jnp.float32
            )
            * score_scale
        )
        .astype(jnp.bfloat16)
        .reshape(utterances * frames, heads_here * HD)
    )
    grad_query = product_left(stream_low, grad_queries)
    grad_one = grad_two + lax.psum(product_right(grad_queries, w_query), "mp")
    grad_key = product_left(mem_low, grad_keys)
    grad_value = product_left(mem_low, grad_values)
    grad_mem_part = product_right(grad_keys, w_key) + product_right(grad_values, w_value)
    grad_memory = lax.psum_scatter(grad_mem_part, "mp", scatter_dimension=1, tiled=True)
    utterance_sums = jnp.sum(grad_mem_part.reshape(utterances, frames, model_width), axis=1)
    group_one = (rate_groups == 1).astype(jnp.float32)[:, None]
    rate_part = jnp.stack(
        [
            jnp.sum((1.0 - group_one) * utterance_sums, axis=0),
            jnp.sum(group_one * utterance_sums, axis=0),
        ]
    )
    grad_rate = lax.psum(rate_part, ("dp", "mp"))
    grad_norm_one, grad_kernel = back_conv(grad_one)
    grad_zero_norm, grad_gain_one, grad_bias_one = back_one(grad_norm_one)
    grad_zero = grad_one + grad_zero_norm
    grad_acoustic = grad_zero - blend_weight[:, None] * grad_zero
    table_terms = blend_weight[:, None] * grad_zero
    group_size = lax.axis_size("dp")
    id_columns = jnp.broadcast_to(targets.astype(jnp.float32)[:, None], (tok_rows, group_size))
    arrived_rows, arrived_ids = (
        lax.all_to_all(table_terms, "dp", split_axis=1, concat_axis=0, tiled=True),
        lax.all_to_all(id_columns, "dp", split_axis=1, concat_axis=0, tiled=True),
    )
    grad_embedding = jax.ops.segment_sum(
        arrived_rows, arrived_ids[:, 0].astype(jnp.int32), num_segments=embedding.shape[0]
    )
    summed_grads = (
        lax.psum_scatter(grad_query, "dp", scatter_dimension=0, tiled=True),
        lax.psum_scatter(grad_key, "dp", scatter_dimension=0, tiled=True),
        lax.psum_scatter(grad_value, "dp", scatter_dimension=0, tiled=True),
        lax.psum_scatter(grad_out, "dp", scatter_dimension=1, tiled=True),
        lax.psum_scatter(grad_in, "dp", scatter_dimension=0, tiled=True),
        lax.psum_scatter(grad_back, "dp", scatter_dimension=1, tiled=True),
        lax.psum_scatter(grad_vocab, "dp", scatter_dimension=0, tiled=True),
        lax.psum_scatter(grad_kernel, "dp", scatter_dimension=1, tiled=True),
        lax.psum_scatter(grad_gain_one, "dp", scatter_dimension=0, tiled=True),
        lax.psum_scatter(grad_bias_one, "dp", scatter_dimension=0, tiled=True),
        lax.psum_scatter(grad_gain_two, "dp", scatter_dimension=0, tiled=True),
        lax.psum_scatter(grad_bias_two, "dp", scatter_dimension=0, tiled=True),
    )
    (
        grad_query,
        grad_key,
        grad_value,
        grad_out,
        grad_in,
        grad_back,
        grad_vocab,
        grad_kernel,
        grad_gain_one,
        grad_bias_one,
        grad_gain_two,
        grad_bias_two,
    ) = summed_grads
    return (
        token_loss,
        grad_acoustic,
        grad_memory,
        grad_embedding,
        grad_query,
        grad_key,
        grad_value,
        grad_out,
        grad_in,
        grad_back,
        grad_vocab,
        grad_gain_one,
        grad_bias_one,
        grad_gain_two,
        grad_bias_two,
        grad_kernel,
        grad_rate,
    )


def solution(mesh):
    return jax.shard_map(
        per_device,
        mesh=mesh,
        in_specs=(
            P("dp", None),
            P("dp", None),
            P(),
            P(None, "mp"),
            P(None, "mp"),
            P(None, "mp"),
            P("mp", None),
            P(None, "mp"),
            P("mp", None),
            P(None, "mp"),
            P(),
            P(),
            P(),
            P(),
            P(),
            P(),
            P("dp"),
            P("dp"),
            P("dp"),
            P("dp"),
            P("dp"),
        ),
        out_specs=(
            P("dp"),
            P("dp", None),
            P("dp", "mp"),
            P(None, "dp"),
            P("dp", "mp"),
            P("dp", "mp"),
            P("dp", "mp"),
            P("mp", "dp"),
            P("dp", "mp"),
            P("mp", "dp"),
            P("dp", "mp"),
            P("dp"),
            P("dp"),
            P("dp"),
            P("dp"),
            P(None, "dp"),
            P(),
        ),
        check_vma=False,
    )
```

profile of v0, /device:TPU:0, one launch (start us, length us, event | category | flops | bytes accessed | tf_op | source)
XLA Modules:
  0.0 1008.7 jit_solution(17247975809619713009)
XLA Ops:
  17.2 2.0 fusion.6
  22.4 2.4 copy.118
  24.9 3.6 convolution_convert_fusion.1
  28.5 2.2 reshape.375
  30.7 2.1 fusion.190
  32.8 2.6 fusion.16
  36.7 21.5 %all-reduce.39.cloned.1.call-done = f32[256,512]{1,0:T(8,128)} async-done(((f32[256,512]{1,0:T(8,128)}), f32[256,512]{1,0:T(8,128)}) %all-reduce.39.cloned.1.call-update) | async-done | bytes 524304 | tf_op jit(solution)/shard_map/psum | solution.py:141
  59.6 5.0 fusion.83
  65.5 5.8 gather_fusion
  71.3 13.4 %all-reduce.41.cloned.1.call-done = f32[256,512]{1,0:T(8,128)} async-done(((f32[256,512]{1,0:T(8,128)}), f32[256,512]{1,0:T(8,128)}) %all-reduce.41.cloned.1.call-update) | async-done | bytes 524304 | tf_op jit(solution)/shard_map/psum | solution.py:148
  84.7 5.7 fusion.193
  90.4 2.4 pmax.14
  92.9 4.0 exponential_reduce_fusion.1
  97.0 2.5 all-reduce.30
  103.8 1.9 fusion.194
  106.3 1.4 fusion.17
  107.7 1.7 copy.115
  109.4 2.0 fusion.105
  111.5 20.0 %all-reduce.43.cloned.1.call-done = f32[256,512]{1,0:T(8,128)} async-done(((f32[256,512]{1,0:T(8,128)}), f32[256,512]{1,0:T(8,128)}) %all-reduce.43.cloned.1.call-update) | async-done | bytes 524304 | tf_op jit(solution)/shard_map/psum | solution.py:141
  131.6 1.6 fusion.183
  134.0 4.4 multiply_convert_fusion.2
  140.6 20.0 %all-reduce.45.cloned.1.call-done = f32[256,512]{1,0:T(8,128)} async-done(((f32[256,512]{1,0:T(8,128)}), f32[256,512]{1,0:T(8,128)}) %all-reduce.45.cloned.1.call-update) | async-done | bytes 524304 | tf_op jit(solution)/shard_map/psum | solution.py:148
  161.9 6.2 fusion.195
  168.1 3.3 pmax.15
  171.4 4.4 fusion.2
  175.8 3.1 all-reduce.29
  180.9 6.4 fusion.176
  187.4 20.0 %all-reduce.47.cloned.1.call-done = f32[256,512]{1,0:T(8,128)} async-done(((f32[256,512]{1,0:T(8,128)}), f32[256,512]{1,0:T(8,128)}) %all-reduce.47.cloned.1.call-update) | async-done | bytes 524304 | tf_op jit(solution)/shard_map/psum | solution.py:199
  207.4 2.7 add_convert_fusion
  212.9 19.3 %all-reduce.49.cloned.1.call-done = f32[256,512]{1,0:T(8,128)} async-done(((f32[256,512]{1,0:T(8,128)}), f32[256,512]{1,0:T(8,128)}) %all-reduce.49.cloned.1.call-update) | async-done | bytes 524304 | tf_op jit(solution)/shard_map/psum | solution.py:204
  232.2 2.0 multiply_reduce_fusion.12
  235.0 1.5 fusion.181
  238.1 2.0 multiply_reduce_fusion
  243.8 2.1 fusion.101
  245.9 20.0 %all-reduce.51.cloned.1.call-done = f32[256,512]{1,0:T(8,128)} async-done(((f32[256,512]{1,0:T(8,128)}), f32[256,512]{1,0:T(8,128)}) %all-reduce.51.cloned.1.call-update) | async-done | bytes 524304 | tf_op jit(solution)/shard_map/psum | solution.py:248
  265.9 1.5 multiply_reduce_fusion.6
  267.5 5.7 multiply_reduce_fusion.11
  273.9 1.6 copy.129
  275.6 2.0 fusion.103
  277.6 2.4 fusion.12
  280.0 2.4 copy.123
  282.5 3.2 fusion.23
  285.8 1.4 fusion.13
  287.2 2.4 copy.121
  289.7 3.2 fusion.26
  293.0 2.1 fusion.99
  295.2 3.0 fusion.171
  299.2 2.8 fusion.114
  303.7 2.7 bitcast_reduce_fusion
  307.4 6.8 fusion.174
  315.4 6.7 all-to-all-start
  327.8 1.7 all-to-all-done
  329.5 5.3 all-to-all-start.1
  336.2 41.1 %psum.95 = f32[2,512]{1,0:T(2,128)} all-reduce(f32[2,512]{1,0:T(2,128)S(1)} %pad_maximum_fusion), channel_id=1, replica_groups=mesh['dp'=16,'mp'=2] {'dp','mp'}, use_global_device_ids=true, to_apply=%region_68.69 | all-reduce | flops 1024 | bytes 8192 | tf_op jit(solution)/shard_map/psum | solution.py:261
  377.3 41.0 %all-reduce.28 = (f32[512]{0:T(512)S(1)}, f32[512]{0:T(512)S(1)}, f32[512]{0:T(512)S(1)}, f32[512]{0:T(512)S(1)}) all-reduce(f32[512]{0:T(512)S(1)} %get-tuple-element.89, f32[512]{0:T(512)S(1)} %get-tuple-element.116, f32[512]{0:T(512)S(1)} %copy-done.91, f32[512]{0:T(512)S(1)} %copy-done.92), channel_id=10, replica_groups=mesh['dp'=16,'mp'=2] {'dp'}, use_global_device_ids=true, to_apply=%region_46.47.clone | all-reduce | flops 2048 | bytes 16384
  422.6 24.6 %scatter_custom_fusion = f32[8404,32]{1,0:T(8,128)} fusion(s32[4096]{0:T(1024)S(1)} %bitcast.240, f32[4096,32]{1,0:T(8,128)S(1)} %bitcast.197, f32[]{:T(128)} %constant.43.clone.1), kind=kCustom, calls=%fused_computation.19 | custom fusion | flops 131072 | bytes 1075716 | tf_op jit(solution)/shard_map/scatter-add | solution.py:273
  447.2 3.7 copy.127
  450.9 54.3 %reduce-scatter.18.cloned.1.call-done = f32[32,256]{1,0:T(8,128)} async-done(((f32[512,256]{1,0:T(8,128)}), f32[32,256]{1,0:T(8,128)}) %reduce-scatter.18.cloned.1.call-update) | async-done | bytes 32784 | tf_op jit(solution)/shard_map/reduce_scatter | solution.py:279
  505.1 75.8 %reduce-scatter.16.cloned.1.call-done = f32[32,256]{1,0:T(8,128)} async-done(((f32[512,256]{1,0:T(8,128)}), f32[32,256]{1,0:T(8,128)}) %reduce-scatter.16.cloned.1.call-update) | async-done | bytes 32784 | tf_op jit(solution)/shard_map/reduce_scatter | solution.py:278
  580.9 75.7 %reduce-scatter.14.cloned.1.call-done = f32[32,256]{1,0:T(8,128)} async-done(((f32[512,256]{1,0:T(8,128)}), f32[32,256]{1,0:T(8,128)}) %reduce-scatter.14.cloned.1.call-update) | async-done | bytes 32784 | tf_op jit(solution)/shard_map/reduce_scatter | solution.py:277
  656.6 79.6 %reduce-scatter.22.cloned.1.call-done = f32[32,1024]{1,0:T(8,128)} async-done(((f32[512,1024]{1,0:T(8,128)}), f32[32,1024]{1,0:T(8,128)}) %reduce-scatter.22.cloned.1.call-update) | async-done | bytes 131088 | tf_op jit(solution)/shard_map/reduce_scatter | solution.py:281
  736.2 80.7 %reduce-scatter.24.cloned.1.call-done = f32[1024,32]{0,1:T(8,128)} async-done(((f32[1024,512]{0,1:T(8,128)}), f32[1024,32]{0,1:T(8,128)}) %reduce-scatter.24.cloned.1.call-update) | async-done | bytes 131088 | tf_op jit(solution)/shard_map/reduce_scatter | solution.py:282
  816.9 11.6 %reduce-scatter.12.cloned.1.call-done = f32[2048,256]{1,0:T(8,128)} async-done(((f32[2048,512]{1,0:T(8,128)}), f32[2048,256]{1,0:T(8,128)}) %reduce-scatter.12.cloned.1.call-update) | async-done | bytes 2097168 | tf_op jit(solution)/shard_map/reduce_scatter | solution.py:252
  828.5 173.2 %reduce-scatter.26.cloned.1.call-done = f32[32,4202]{1,0:T(8,128)} async-done(((f32[512,4202]{1,0:T(8,128)}), f32[32,4202]{1,0:T(8,128)}) %reduce-scatter.26.cloned.1.call-update) | async-done | bytes 537872 | tf_op jit(solution)/shard_map/reduce_scatter | solution.py:283
  (321 shorter events, 52.4 us)
Async XLA Ops:
  7.2 52.4 %copy-start = (bf16[512,1024]{1,0:T(8,128)(2,1)S(1)}, bf16[512,1024]{1,0:T(8,128)(2,1)}, u32[]{:S(2)}) copy-start(bf16[512,1024]{1,0:T(8,128)(2,1)} %param.28) | copy-start | bytes 3145732
  7.2 9.5 copy-start.2
  7.2 51.0 %all-reduce.39.cloned.1.call-start = ((), (), s32[]{:S(2)}) async-start(), calls=%async_computation.11 | async-start | bytes 1048576 | tf_op jit(solution)/shard_map/psum | solution.py:141
  9.6 7.1 copy-start.21
  24.9 5.8 copy-start.7
  35.4 24.2 %copy-start.77 = (f32[512]{0:T(512)S(1)}, f32[512]{0:T(512)}, u32[]{:S(2)}) copy-start(f32[512]{0:T(512)} %param.33) | copy-start | bytes 6148
  35.4 24.2 %copy-start.98 = (f32[512]{0:T(512)S(1)}, f32[512]{0:T(512)}, u32[]{:S(2)}) copy-start(f32[512]{0:T(512)} %param.34) | copy-start | bytes 6148
  36.6 48.1 %all-reduce.41.cloned.1.call-start = ((), (), s32[]{:S(2)}) async-start(), calls=%async_computation.12 | async-start | bytes 1048576 | tf_op jit(solution)/shard_map/psum | solution.py:148
  59.6 5.3 copy-start.83
  64.6 66.9 %all-reduce.43.cloned.1.call-start = ((), (), s32[]{:S(2)}) async-start(), calls=%async_computation.13 | async-start | bytes 1048576 | tf_op jit(solution)/shard_map/psum | solution.py:141
  71.2 30.9 %copy-start.5 = (bf16[256,512]{1,0:T(8,128)(2,1)}, bf16[256,512]{1,0:T(8,128)(2,1)S(1)}, u32[]{:S(2)}) copy-start(bf16[256,512]{1,0:T(8,128)(2,1)S(1)} %gather_fusion) | copy-start | bytes 786436
  71.3 21.6 %copy-start.38 = (s32[4202]{0:T(1024)}, s32[4202]{0:T(1024)S(1)}, u32[]{:S(2)}) copy-start(s32[4202]{0:T(1024)S(1)} %iota_add_fusion) | copy-start | bytes 50428
  92.9 6.6 copy-start.94
  92.9 6.6 copy-start.99
  92.9 7.3 copy-start.57
  92.9 7.3 copy-start.90
  96.9 4.5 copy-start.45
  96.9 4.5 copy-start.48
  96.9 4.4 copy-start.50
  96.9 4.4 copy-start.52
  97.0 4.4 copy-start.54
  97.0 4.4 copy-start.56
  97.0 4.4 copy-start.60
  97.0 4.4 copy-start.63
  111.5 49.1 %all-reduce.45.cloned.1.call-start = ((), (), s32[]{:S(2)}) async-start(), calls=%async_computation.14 | async-start | bytes 1048576 | tf_op jit(solution)/shard_map/psum | solution.py:148
  133.1 5.3 copy-start.3
  133.2 5.2 copy-start.73
  134.0 4.5 copy-start.80
  134.0 5.3 copy-start.37
  140.5 66.9 %all-reduce.47.cloned.1.call-start = ((), (), s32[]{:S(2)}) async-start(), calls=%async_computation.15 | async-start | bytes 1048576 | tf_op jit(solution)/shard_map/psum | solution.py:199
  161.9 6.2 copy-start.19
  161.9 9.6 copy-start.84
  187.4 44.9 %all-reduce.49.cloned.1.call-start = ((), (), s32[]{:S(2)}) async-start(), calls=%async_computation.16 | async-start | bytes 1048576 | tf_op jit(solution)/shard_map/psum | solution.py:204
  212.2 53.7 %all-reduce.51.cloned.1.call-start = ((), (), s32[]{:S(2)}) async-start(), calls=%async_computation.17 | async-start | bytes 1048576 | tf_op jit(solution)/shard_map/psum | solution.py:248
  212.9 27.2 %copy-start.71 = (f32[2,2,128]{2,1,0:T(2,128)}, f32[2,2,128]{2,1,0:T(2,128)S(1)}, u32[]{:S(2)}) copy-start(f32[2,2,128]{2,1,0:T(2,128)S(1)} %log_add_fusion) | copy-start | bytes 6148
  212.9 24.7 %copy-start.18 = (bf16[256,512]{1,0:T(8,128)(2,1)S(1)}, bf16[256,512]{1,0:T(8,128)(2,1)}, u32[]{:S(2)}) copy-start(bf16[256,512]{1,0:T(8,128)(2,1)} %param.27) | copy-start | bytes 786436
  242.7 24.7 %copy-start.46 = (f32[1,512]{1,0:T(1,128)S(1)}, f32[1,512]{1,0:T(1,128)}, u32[]{:S(2)}) copy-start(f32[1,512]{1,0:T(1,128)} %copy-done.44) | copy-start | bytes 6148
  243.8 23.7 %copy-start.34 = (bf16[2,128,2,128]{3,2,1,0:T(2,128)(2,1)}, bf16[2,128,2,128]{3,2,1,0:T(2,128)(2,1)S(1)}, u32[]{:S(2)}) copy-start(bf16[2,128,2,128]{3,2,1,0:T(2,128)(2,1)S(1)} %copy.119) | copy-start | bytes 393220
  245.8 174.8 %reduce-scatter.28.cloned.1.call-start = ((), (), s32[]{:S(2)}) async-start(), calls=%async_computation.26 | async-start | bytes 278528
  267.4 8.1 copy-start.12
  275.5 175.4 %reduce-scatter.20.cloned.1.call-start = ((), (), s32[]{:S(2)}) async-start(), calls=%async_computation.22 | async-start | bytes 557056 | tf_op jit(solution)/shard_map/reduce_scatter | solution.py:280
  277.6 227.6 %reduce-scatter.18.cloned.1.call-start = ((), (), s32[]{:S(2)}) async-start(), calls=%async_computation.21 | async-start | bytes 557056 | tf_op jit(solution)/shard_map/reduce_scatter | solution.py:279
  285.8 295.2 %reduce-scatter.16.cloned.1.call-start = ((), (), s32[]{:S(2)}) async-start(), calls=%async_computation.20 | async-start | bytes 557056 | tf_op jit(solution)/shard_map/reduce_scatter | solution.py:278
  289.7 5.5 copy-start.74
  289.7 5.5 copy-start.78
  292.9 363.7 %reduce-scatter.14.cloned.1.call-start = ((), (), s32[]{:S(2)}) async-start(), calls=%async_computation.19 | async-start | bytes 557056 | tf_op jit(solution)/shard_map/reduce_scatter | solution.py:277
  295.1 441.1 %reduce-scatter.22.cloned.1.call-start = ((), (), s32[]{:S(2)}) async-start(), calls=%async_computation.23 | async-start | bytes 2228224 | tf_op jit(solution)/shard_map/reduce_scatter | solution.py:281
  298.2 518.7 %reduce-scatter.24.cloned.1.call-start = ((), (), s32[]{:S(2)}) async-start(), calls=%async_computation.24 | async-start | bytes 2228224 | tf_op jit(solution)/shard_map/reduce_scatter | solution.py:282
  302.1 526.4 %reduce-scatter.12.cloned.1.call-start = ((), (), s32[]{:S(2)}) async-start(), calls=%async_computation.18 | async-start | bytes 6291456 | tf_op jit(solution)/shard_map/reduce_scatter | solution.py:252
  306.5 695.2 %reduce-scatter.26.cloned.1.call-start = ((), (), s32[]{:S(2)}) async-start(), calls=%async_computation.25 | async-start | bytes 9191424 | tf_op jit(solution)/shard_map/reduce_scatter | solution.py:283
  314.2 8.0 copy-start.61
  314.2 8.0 copy-start.64
  314.2 8.0 copy-start.67
  314.2 8.0 copy-start.70
  314.2 8.3 copy-start.28
  314.2 8.3 copy-start.29
  315.4 14.1 %all-to-all-start = ((f32[256,16,1]{0,2,1:T(1,128)}), f32[256,16,1]{0,2,1:T(1,128)S(1)}, u32[]{:S(2)}, u32[]{:S(2)}) async-start(f32[256,16,1]{0,2,1:T(1,128)} %broadcast_in_dim.149), calls=%async_computation.1 | async-start | bytes 32768 | tf_op jit(solution)/shard_map/all_to_all | solution.py:271
  325.8 8.9 copy-start.102
  325.9 10.2 %copy-start.101 = (s32[2]{0:T(128)S(1)}, s32[2]{0:T(128)}, u32[]{:S(2)}) copy-start(s32[2]{0:T(128)} %param.39) | copy-start | bytes 28
  325.9 10.2 %copy-start.100 = (f32[2]{0:T(128)S(1)}, f32[2]{0:T(128)}, u32[]{:S(2)}) copy-start(f32[2]{0:T(128)} %get-tuple-element.158) | copy-start | bytes 28
  325.9 51.4 %copy-start.91 = (f32[512]{0:T(512)S(1)}, f32[512]{0:T(512)}, u32[]{:S(2)}) copy-start(f32[512]{0:T(512)} %get-tuple-element.101) | copy-start | bytes 6148
  325.9 51.4 %copy-start.92 = (f32[512]{0:T(512)S(1)}, f32[512]{0:T(512)}, u32[]{:S(2)}) copy-start(f32[512]{0:T(512)} %get-tuple-element.103) | copy-start | bytes 6148
  329.5 92.5 %all-to-all-start.1 = ((f32[256,16,32]{0,2,1:T(8,128)}), f32[256,16,32]{0,2,1:T(8,128)S(1)}, u32[]{:S(2)}, u32[]{:S(2)}) async-start(f32[256,16,32]{0,2,1:T(8,128)} %bitcast.28), calls=%async_computation.2 | async-start | bytes 1048576 | tf_op jit(solution)/shard_map/all_to_all | solution.py:270
  422.6 579.1 %copy-start.1 = (bf16[512,1024]{1,0:T(8,128)(2,1)S(1)}, bf16[512,1024]{1,0:T(8,128)(2,1)}, u32[]{:S(2)}) copy-start(bf16[512,1024]{1,0:T(8,128)(2,1)} %param.28) | copy-start | bytes 3145732
  (57 other events, 102.1 us)
Sparse Core Ops, SparseCore 0:
  36.7 21.4 all-reduce.38
  64.8 19.9 all-reduce.40
  111.6 19.8 all-reduce.42
  140.6 19.9 all-reduce.44
  187.5 19.8 all-reduce.46
  212.3 19.9 all-reduce.48
  246.0 19.9 all-reduce.50
  275.6 77.4 reduce-scatter.27
  355.9 73.5 reduce-scatter.19
  432.2 72.8 reduce-scatter.17
  508.0 72.9 reduce-scatter.15
  583.7 72.8 reduce-scatter.13
  659.5 76.6 reduce-scatter.21
  738.9 77.9 reduce-scatter.23
  819.6 8.8 reduce-scatter.11
  835.5 166.1 reduce-scatter.25
where the time goes:
time: 1020 us; the launch traced here: 1010 us
  waiting for transfers between devices  687 us (67%)
  blocking collectives  93.5 us (9%)
  matrix products  84.6 us (8%)
  other arithmetic  68.4 us (7%)
  local copies, waits for them, and re-layouts  45.5 us (4%)
  between operations  16.6 us (2%)
  starting transfers between devices  13.1 us (1%)
    reduce_scatter x1, waiting for transfers between devices, per_device(): lax.psum_scatter(grad_vocab, 'dp', scatter_dimension=0, tiled=True)  173 us
    reduce_scatter x1, waiting for transfers between devices, per_device(): lax.psum_scatter(grad_back, 'dp', scatter_dimension=1, tiled=True)  80.7 us
    reduce_scatter x1, waiting for transfers between devices, per_device(): lax.psum_scatter(grad_in, 'dp', scatter_dimension=0, tiled=True)  79.6 us
    reduce_scatter x1, waiting for transfers between devices, per_device(): lax.psum_scatter(grad_key, 'dp', scatter_dimension=0, tiled=True)  75.8 us
    reduce_scatter x1, waiting for transfers between devices, per_device(): lax.psum_scatter(grad_query, 'dp', scatter_dimension=0, tiled=True)  75.7 us
    reduce_scatter x1, waiting for transfers between devices, per_device(): lax.psum_scatter(grad_value, 'dp', scatter_dimension=0, tiled=True)  54.3 us
    psum x2, waiting for transfers between devices, decoder_pass(): stream_two = stream_one + lax.psum(product(mixed_heads, w_out), 'mp')  41.5 us
    psum x1, blocking collectives, per_device(): grad_rate = lax.psum(rate_part, ('dp', 'mp'))  41.1 us
  transfers between devices with their start and end apart: 18, of which 15 were waited for; matrix products, arithmetic and copies ran while one was open for 8% of the time, Pallas kernels for 0%

commit v1 on v0

--- a/solution.py
+++ b/solution.py
@@ -4,13 +4,246 @@
 import jax
 import jax.numpy as jnp
 from jax import lax
+from jax.experimental import pallas as pl
+from jax.experimental.pallas import tpu as pltpu
 from jax.sharding import PartitionSpec as P
+
+MESH = pl.DeviceIdType.MESH
+VMEM = pl.BlockSpec(memory_space=pltpu.VMEM)
 
 HD = 128
 V = 8404
 
 
 EPSILON = 1e-05
+
+
+def other_core():
+    return {"mp": 1 - lax.axis_index("mp")}
+
+
+def greet_other_core():
+    barrier = pltpu.get_barrier_semaphore()
+    pl.semaphore_signal(barrier, inc=1, device_id=other_core(), device_id_type=MESH)
+    pl.semaphore_wait(barrier, 1)
+
+
+def pair_add_kernel(mine, total, arrived, send_sem, recv_sem):
+    greet_other_core()
+    copy = pltpu.make_async_remote_copy(
+        src_ref=mine, dst_ref=arrived, send_sem=send_sem, recv_sem=recv_sem,
+        device_id=other_core(), device_id_type=MESH,
+    )
+    copy.start()
+    copy.wait()
+    total[...] = mine[...] + arrived[...]
+
+
+def pair_get_kernel(mine, theirs, arrived, send_sem, recv_sem):
+    greet_other_core()
+    copy = pltpu.make_async_remote_copy(
+        src_ref=mine, dst_ref=arrived, send_sem=send_sem, recv_sem=recv_sem,
+        device_id=other_core(), device_id_type=MESH,
+    )
+    copy.start()
+    copy.wait()
+    theirs[...] = arrived[...]
+
+
+def pair_half_kernel(mine, total, arrived, send_sem, recv_sem):
+    greet_other_core()
+    width = total.shape[1]
+    core = lax.axis_index("mp")
+    copy = pltpu.make_async_remote_copy(
+        src_ref=mine.at[:, pl.ds(pl.multiple_of((1 - core) * width, 128), width)],
+        dst_ref=arrived, send_sem=send_sem, recv_sem=recv_sem,
+        device_id=other_core(), device_id_type=MESH,
+    )
+    copy.start()
+    copy.wait()
+    total[...] = mine[:, pl.ds(pl.multiple_of(core * width, 128), width)] + arrived[...]
+
+
+def pair_call(kernel, mine, shape, collective_id):
+    out = jax.ShapeDtypeStruct(shape, jnp.float32)
+    return pl.pallas_call(
+        kernel,
+        out_shape=out,
+        in_specs=[VMEM],
+        out_specs=VMEM,
+        scratch_shapes=[
+            pltpu.VMEM(shape, jnp.float32),
+            pltpu.SemaphoreType.DMA,
+            pltpu.SemaphoreType.DMA,
+        ],
+        compiler_params=pltpu.CompilerParams(
+            collective_id=collective_id, has_side_effects=True, vmem_limit_bytes=32 << 20
+        ),
+    )(mine)
+
+
+def pair_add(mine):
+    return pair_call(pair_add_kernel, mine, mine.shape, 1)
+
+
+def pair_get(mine):
+    return pair_call(pair_get_kernel, mine, mine.shape, 2)
+
+
+def pair_half(mine):
+    return pair_call(pair_half_kernel, mine, (mine.shape[0], mine.shape[1] // 2), 3)
+
+
+def scatter_sum_kernel(bits, low_bits, chunks, shared_rows, n_in, *refs):
+    ins, small = refs[:n_in], refs[n_in]
+    outs, small_out = refs[n_in + 1 : 2 * n_in + 1], refs[2 * n_in + 1]
+    scratch = refs[2 * n_in + 2 :]
+    steps = len(bits)
+    n_chunks = len(chunks)
+    arrived = [scratch[c * steps : (c + 1) * steps] for c in range(n_chunks)]
+    small_arrived, small_sent, send_sem, recv_sem, small_send, small_recv = scratch[n_chunks * steps :]
+    me, core = lax.axis_index("dp"), lax.axis_index("mp")
+    bit_of = {b: lax.rem(me // (1 << b), 2) for b in low_bits + bits}
+    peer_of = {b: {"dp": me + (1 - 2 * bit_of[b]) * (1 << b)} for b in low_bits + bits}
+
+    barrier = pltpu.get_barrier_semaphore()
+    for b in low_bits + bits:
+        pl.semaphore_signal(barrier, inc=1, device_id=peer_of[b], device_id_type=MESH)
+    pl.semaphore_signal(barrier, inc=1, device_id=other_core(), device_id_type=MESH)
+    pl.semaphore_wait(barrier, len(low_bits) + steps + 1)
+
+    def pick(c, step, half):
+        source, start, width, order = chunks[c]
+        rest = sorted([b for b in bits if b not in order[:step]], reverse=True)
+        where = tuple(half if b == order[step] else slice(None) for b in rest)
+        if step == 0:
+            return ins[source], where + (slice(None), pl.ds(start, width))
+        return arrived[c][step - 1], where + (slice(None), slice(None))
+
+    def send(c, step):
+        b = chunks[c][3][step]
+        ref, where = pick(c, step, 1 - bit_of[b])
+        copy = pltpu.make_async_remote_copy(
+            src_ref=ref.at[where], dst_ref=arrived[c][step],
+            send_sem=send_sem.at[c, step], recv_sem=recv_sem.at[c, step],
+            device_id=peer_of[b], device_id_type=MESH,
+        )
+        copy.start()
+        return copy
+
+    def take(c, step, copy):
+        b = chunks[c][3][step]
+        ref, where = pick(c, step, bit_of[b])
+        copy.wait_recv()
+        got = arrived[c][step]
+        if step == steps - 1:
+            source, start, width, _ = chunks[c]
+            outs[source][:, pl.ds(start, width)] = got[...] + ref[where]
+        else:
+            got[...] = got[...] + ref[where]
+
+    small_peers = [peer_of[b] for b in low_bits + bits] + [other_core()]
+    small_sent[0] = small[...]
+
+    def small_send_step(step):
+        copy = pltpu.make_async_remote_copy(
+            src_ref=small_sent.at[step], dst_ref=small_arrived.at[step],
+            send_sem=small_send.at[step], recv_sem=small_recv.at[step],
+            device_id=small_peers[step], device_id_type=MESH,
+        )
+        copy.start()
+        return copy
+
+    def small_take(step, copy):
+        copy.wait_recv()
+        if step + 1 < len(small_peers):
+            small_sent[step + 1] = small_sent[step] + small_arrived[step]
+        else:
+            small_out[...] = small_sent[step]
+            rows = small_out.shape[0] - shared_rows
+            small_out[pl.ds(shared_rows, rows)] = (
+                small_sent[step, pl.ds(shared_rows, rows)]
+                + small_arrived[step, pl.ds(shared_rows, rows)]
+            )
+
+    started = []
+    small_copy = small_send_step(0)
+    small_step = 0
+    started.append(small_copy)
+    flying = {}
+    for c in range(n_chunks):
+        flying[c] = send(c, 0)
+        started.append(flying[c])
+    for wave in range(n_chunks + 2 * (steps - 1)):
+        for step in reversed(range(steps)):
+            c = wave - 2 * step
+            if not 0 <= c < n_chunks:
+                continue
+            take(c, step, flying[c])
+            if step + 1 < steps:
+                flying[c] = send(c, step + 1)
+                started.append(flying[c])
+        if small_step < len(small_peers):
+            small_take(small_step, small_copy)
+            small_step += 1
+            if small_step < len(small_peers):
+                small_copy = small_send_step(small_step)
+                started.append(small_copy)
+    for copy in started:
+        copy.wait_send()
+
+
+def scatter_sum(parts, small, shared_rows, n_dp):
+    nbits = n_dp.bit_length() - 1
+    rows = parts[0].shape[0]
+    steps = nbits
+    while rows >> steps < 8:
+        steps -= 1
+    low_bits, bits = list(range(nbits - steps)), list(range(nbits - steps, nbits))
+    block = rows >> steps
+    shaped = [p.reshape((2,) * steps + (block, p.shape[1])) for p in parts]
+    forward = bits
+    swapped = [bits[1], bits[0]] + bits[2:]
+    chunks = []
+    for i, p in enumerate(parts):
+        width = p.shape[1]
+        pieces = max(1, width // 1024)
+        edges = [width // 128 * k // pieces * 128 for k in range(pieces)] + [width]
+        for k in range(pieces):
+            chunks.append((i, edges[k], edges[k + 1] - edges[k], [forward, swapped][len(chunks) % 2]))
+    scratch = []
+    for _, _, width, _ in chunks:
+        for step in range(steps):
+            scratch.append(pltpu.VMEM((2,) * (steps - 1 - step) + (block, width), jnp.float32))
+    n_small = nbits + 1
+    scratch += [
+        pltpu.VMEM((n_small,) + small.shape, jnp.float32),
+        pltpu.VMEM((n_small,) + small.shape, jnp.float32),
+        pltpu.SemaphoreType.DMA((len(chunks), steps)),
+        pltpu.SemaphoreType.DMA((len(chunks), steps)),
+        pltpu.SemaphoreType.DMA((n_small,)),
+        pltpu.SemaphoreType.DMA((n_small,)),
+    ]
+    out = pl.pallas_call(
+        partial(scatter_sum_kernel, bits, low_bits, chunks, shared_rows, len(parts)),
+        out_shape=[jax.ShapeDtypeStruct((block, p.shape[1]), jnp.float32) for p in parts]
+        + [jax.ShapeDtypeStruct(small.shape, jnp.float32)],
+        in_specs=[VMEM] * (len(parts) + 1),
+        out_specs=[VMEM] * (len(parts) + 1),
+        scratch_shapes=scratch,
+        compiler_params=pltpu.CompilerParams(
+            collective_id=4, has_side_effects=True, vmem_limit_bytes=56 << 20
+        ),
+    )(*shaped, small)
+    summed, small_sum = list(out[:-1]), out[-1]
+    if low_bits:
+        size = 1 << len(low_bits)
+        groups = [list(range(g * size, (g + 1) * size)) for g in range(n_dp // size)]
+        summed = [
+            lax.psum_scatter(s, "dp", scatter_dimension=0, axis_index_groups=groups, tiled=True)
+            for s in summed
+        ]
+    return summed, small_sum
 
 
 def norm_rows(row_values, gain_vector, bias_vector):
@@ -51,11 +284,14 @@
     onehot = (vocab_ids == target_ids[:, None]).astype(jnp.float32)
     picked = jnp.sum(onehot * logits, axis=1)
     local_top = jnp.max(logits, axis=1)
-    top_value = lax.pmax(local_top, "mp")
-    denominator, picked = lax.psum(
-        (jnp.sum(jnp.exp(logits - top_value[:, None]), axis=1), picked), "mp"
-    )
-    return (top_value + jnp.log(denominator), picked, onehot)
+    local_sum = jnp.sum(jnp.exp(logits - local_top[:, None]), axis=1)
+    zeros = jnp.zeros_like(local_top)
+    theirs = pair_get(jnp.stack([local_top, local_sum, picked] + [zeros] * 5))
+    top_value = jnp.maximum(local_top, theirs[0])
+    denominator = local_sum * jnp.exp(local_top - top_value) + theirs[1] * jnp.exp(
+        theirs[0] - top_value
+    )
+    return (top_value + jnp.log(denominator), picked + theirs[2], onehot)
 
 
 def attention_scores(query_rows, key_rows, valid_mem, score_scale):
@@ -89,6 +325,7 @@
     glance_mask,
     targets,
 ):
+    all_targets = lax.all_gather(targets, "dp", tiled=True)
     utterances = token_lengths.shape[0]
     tok_rows, model_width = acoustic.shape
     token_slots = tok_rows // utterances
@@ -138,14 +375,14 @@
             .astype(jnp.bfloat16)
             .reshape(tok_rows, heads_here * HD)
         )
-        stream_two = stream_one + lax.psum(product(mixed_heads, w_out), "mp")
+        stream_two = stream_one + pair_add(product(mixed_heads, w_out))
         norm_two, back_two = jax.vjp(norm_rows, stream_two, gain_two, bias_two)
         norm_low = norm_two.astype(jnp.bfloat16)
         activated, back_act = jax.vjp(
             partial(jax.nn.gelu, approximate=False), product(norm_low, w_in)
         )
         hidden = activated.astype(jnp.bfloat16)
-        stream_three = stream_two + lax.psum(product(hidden, w_back), "mp")
+        stream_three = stream_two + pair_add(product(hidden, w_back))
         top_low = stream_three.astype(jnp.bfloat16)
         logits = product(top_low, w_vocab)
         log_total, picked, onehot = logit_stats(logits, targets, offset)
@@ -195,17 +432,20 @@
     grad_logits = ((jnp.exp(logits - log_total[:, None]) - onehot) * valid_rows[:, None]).astype(
         jnp.bfloat16
     )
-    grad_vocab = product_left(top_low, grad_logits)
-    grad_three = lax.psum(product_right(grad_logits, w_vocab), "mp")
+    vocab_here = grad_logits.shape[1]
+    grad_vocab = product_left(
+        top_low, jnp.pad(grad_logits, ((0, 0), (0, -vocab_here % 128)))
+    )
+    grad_three = pair_add(product_right(grad_logits, w_vocab))
     grad_branch = grad_three.astype(jnp.bfloat16)
-    grad_back = product_left(hidden, grad_branch)
+    grad_back = product_left(grad_branch, hidden)
     grad_pre = back_act(product_right(grad_branch, w_back))[0].astype(jnp.bfloat16)
     grad_in = product_left(norm_low, grad_pre)
-    grad_norm_two = lax.psum(product_right(grad_pre, w_in), "mp")
+    grad_norm_two = pair_add(product_right(grad_pre, w_in))
     grad_two_norm, grad_gain_two, grad_bias_two = back_two(grad_norm_two)
     grad_two = grad_three + grad_two_norm
     grad_attended = grad_two.astype(jnp.bfloat16)
-    grad_out = product_left(mixed_heads, grad_attended)
+    grad_out = product_left(grad_attended, mixed_heads)
     grad_mixed = (
         product_right(grad_attended, w_out)
         .astype(jnp.bfloat16)
@@ -245,11 +485,11 @@
         .reshape(utterances * frames, heads_here * HD)
     )
     grad_query = product_left(stream_low, grad_queries)
-    grad_one = grad_two + lax.psum(product_right(grad_queries, w_query), "mp")
+    grad_one = grad_two + pair_add(product_right(grad_queries, w_query))
     grad_key = product_left(mem_low, grad_keys)
     grad_value = product_left(mem_low, grad_values)
     grad_mem_part = product_right(grad_keys, w_key) + product_right(grad_values, w_value)
-    grad_memory = lax.psum_scatter(grad_mem_part, "mp", scatter_dimension=1, tiled=True)
+    grad_memory = pair_half(grad_mem_part)
     utterance_sums = jnp.sum(grad_mem_part.reshape(utterances, frames, model_width), axis=1)
     group_one = (rate_groups == 1).astype(jnp.float32)[:, None]
     rate_part = jnp.stack(
@@ -258,49 +498,41 @@
             jnp.sum(group_one * utterance_sums, axis=0),
         ]
     )
-    grad_rate = lax.psum(rate_part, ("dp", "mp"))
     grad_norm_one, grad_kernel = back_conv(grad_one)
     grad_zero_norm, grad_gain_one, grad_bias_one = back_one(grad_norm_one)
     grad_zero = grad_one + grad_zero_norm
     grad_acoustic = grad_zero - blend_weight[:, None] * grad_zero
     table_terms = blend_weight[:, None] * grad_zero
     group_size = lax.axis_size("dp")
-    id_columns = jnp.broadcast_to(targets.astype(jnp.float32)[:, None], (tok_rows, group_size))
-    arrived_rows, arrived_ids = (
-        lax.all_to_all(table_terms, "dp", split_axis=1, concat_axis=0, tiled=True),
-        lax.all_to_all(id_columns, "dp", split_axis=1, concat_axis=0, tiled=True),
-    )
+    arrived_rows = lax.all_to_all(table_terms, "dp", split_axis=1, concat_axis=0, tiled=True)
     grad_embedding = jax.ops.segment_sum(
-        arrived_rows, arrived_ids[:, 0].astype(jnp.int32), num_segments=embedding.shape[0]
-    )
-    summed_grads = (
-        lax.psum_scatter(grad_query, "dp", scatter_dimension=0, tiled=True),
-        lax.psum_scatter(grad_key, "dp", scatter_dimension=0, tiled=True),
-        lax.psum_scatter(grad_value, "dp", scatter_dimension=0, tiled=True),
-        lax.psum_scatter(grad_out, "dp", scatter_dimension=1, tiled=True),
-        lax.psum_scatter(grad_in, "dp", scatter_dimension=0, tiled=True),
-        lax.psum_scatter(grad_back, "dp", scatter_dimension=1, tiled=True),
-        lax.psum_scatter(grad_vocab, "dp", scatter_dimension=0, tiled=True),
-        lax.psum_scatter(grad_kernel, "dp", scatter_dimension=1, tiled=True),
-        lax.psum_scatter(grad_gain_one, "dp", scatter_dimension=0, tiled=True),
-        lax.psum_scatter(grad_bias_one, "dp", scatter_dimension=0, tiled=True),
-        lax.psum_scatter(grad_gain_two, "dp", scatter_dimension=0, tiled=True),
-        lax.psum_scatter(grad_bias_two, "dp", scatter_dimension=0, tiled=True),
-    )
-    (
-        grad_query,
-        grad_key,
-        grad_value,
-        grad_out,
-        grad_in,
-        grad_back,
-        grad_vocab,
-        grad_kernel,
-        grad_gain_one,
-        grad_bias_one,
-        grad_gain_two,
-        grad_bias_two,
-    ) = summed_grads
+        arrived_rows, all_targets, num_segments=embedding.shape[0]
+    )
+    grad_kernel = jnp.pad(grad_kernel, ((0, 12 - grad_kernel.shape[0]), (0, 0)))
+    small = jnp.concatenate(
+        [
+            grad_kernel,
+            grad_gain_one[None],
+            grad_bias_one[None],
+            grad_gain_two[None],
+            grad_bias_two[None],
+            rate_part,
+            jnp.zeros((6, model_width), jnp.float32),
+        ]
+    )
+    (grad_vocab, grad_in, grad_back, grad_query, grad_key, grad_value, grad_out), small = scatter_sum(
+        [grad_vocab, grad_in, grad_back, grad_query, grad_key, grad_value, grad_out],
+        small,
+        16,
+        group_size,
+    )
+    grad_vocab = grad_vocab[:, :vocab_here]
+    grad_back, grad_out = grad_back.T, grad_out.T
+    grad_rate = small[16:18]
+    own = model_width // group_size
+    small = lax.dynamic_slice_in_dim(small, lax.axis_index("dp") * own, own, axis=1)
+    grad_kernel = small[: fsmn_kernel.shape[0]]
+    grad_gain_one, grad_bias_one, grad_gain_two, grad_bias_two = (small[12 + i] for i in range(4))
     return (
         token_loss,
         grad_acoustic,

time: 1020 us -> 436 us (0.43)
  waiting for transfers between devices: 687 us -> 0.01 us
  Pallas kernels: 0 us -> 195 us
  blocking collectives: 93.5 us -> 38.5 us
  matrix products: 84.6 us -> 60.9 us
  local copies, waits for them, and re-layouts: 45.5 us -> 65 us
  between operations: 16.6 us -> 2.94 us
  other arithmetic: 68.4 us -> 57.8 us
    reduce_scatter x8 -> x0, waiting for transfers between devices: 551 us -> none  [the longest x1 173 us: per_device(): lax.psum_scatter(grad_vocab, 'dp', scatter_dimension=0, tiled=True)]
    pallas_call x0 -> x11, Pallas kernels: none -> 195 us  [the longest x1 174 us: scatter_sum(): pl.pallas_call(partial(scatter_sum_kernel, bits, low_bits, chunks, shared...]
    psum x7 -> x0, waiting for transfers between devices: 134 us -> none  [the longest x2 41.5 us: decoder_pass(): stream_two = stream_one + lax.psum(product(mixed_heads, w_out), 'mp')]
    psum x3 -> x0, blocking collectives: 46.7 us -> none  [the longest x1 41.1 us: per_device(): grad_rate = lax.psum(rate_part, ('dp', 'mp'))]
    unnamed x1 -> x0, blocking collectives: 41 us -> none
    all_gather x0 -> x1, blocking collectives: none -> 38.5 us  [per_device(): all_targets = lax.all_gather(targets, 'dp', tiled=True)]
    dot_general x11, matrix products: 30.4 us -> 18.4 us  [product(): return jnp.dot(left_side, right_side, preferred_element_type=jnp.float32)]
    unnamed x214 -> x291, local copies, waits for them, and re-layouts: 21.8 us -> 24.1 us
  transfers between devices with their start and end apart: 18 -> 1, of which waited for: 15 -> 0; matrix products, arithmetic and copies ran while one was open for 8% -> 9% of each run, Pallas kernels for 0% -> 42%
where the time goes in v1:
time: 436 us; the launch traced here: 428 us
  Pallas kernels  195 us (45%)
  local copies, waits for them, and re-layouts  65 us (15%)
  matrix products  60.9 us (14%)
  other arithmetic  57.8 us (13%)
  blocking collectives  38.5 us (9%)
  starting transfers between devices  8.57 us (2%)
    pallas_call x1, Pallas kernels, scatter_sum(): pl.pallas_call(partial(scatter_sum_kernel, bits, low_bits, chunks, shared...  174 us
    all_gather x1, blocking collectives, per_device(): all_targets = lax.all_gather(targets, 'dp', tiled=True)  38.5 us
    scatter-add x1, other arithmetic, per_device(): jax.ops.segment_sum(arrived_rows, all_targets, num_segments=embedding.sha...  25.1 us
    unnamed x291, local copies, waits for them, and re-layouts  24.1 us
    pallas_call x10, Pallas kernels, pair_call(): pl.pallas_call(kernel, out_shape=out, in_specs=[VMEM], out_specs=VMEM, sc...  20.8 us
    dot_general x11, matrix products, product(): return jnp.dot(left_side, right_side, preferred_element_type=jnp.float32)  18.4 us
    dot_general x7, matrix products, product_left(): lax.dot_general(left_side, right_side, (((0,), (0,)), ((), ())), preferre...  18.1 us
  transfers between devices with their start and end apart: 1, of which 0 were waited for; matrix products, arithmetic and copies ran while one was open for 9% of the time, Pallas kernels for 42%

profile of v1, /device:TPU:0, one launch (start us, length us, event | category | flops | bytes accessed | tf_op | source)
XLA Modules:
  0.0 428.3 jit_solution(17820102170535400583)
XLA Ops:
  2.5 1.2 fusion.76
  3.7 1.2 fusion.171
  4.9 1.3 bitcast_convert_fusion
  12.7 2.9 copy.121
  16.9 2.0 copy.150
  19.7 1.4 copy-done.36
  23.0 3.7 convolution_convert_fusion.1
  26.7 1.6 reshape.404
  28.3 3.2 fusion.188
  31.4 2.2 fusion.17
  34.1 2.1 shard_map.332
  36.6 3.0 fusion.82.mine
  39.6 2.0 shard_map.333
  41.6 3.6 fusion.191
  45.2 2.2 exponential_reduce_fusion.1
  47.5 1.2 shard_map.334
  48.8 5.8 %gather_fusion = bf16[256,512]{1,0:T(8,128)(2,1)S(1)} fusion(bf16[8404,512]{1,0:T(8,128)(2,1)} %param.23, s32[1024]{0:T(1024)S(1)} %pad_clamp_fusion), kind=kCustom, calls=%fused_computation | custom fusion | bytes 525312 | tf_op jit(solution)/shard_map/gather | solution.py:413
  59.1 1.9 fusion.192
  62.1 1.4 fusion.18
  63.6 1.7 copy.129
  65.3 1.3 fusion.101.mine
  66.6 2.0 shard_map.335
  69.2 3.7 multiply_convert_fusion.2
  74.1 2.0 shard_map.336
  76.3 1.3 fusion.193
  77.7 2.5 fusion.2
  80.9 1.2 shard_map.337
  82.2 1.4 bitcast_select_fusion
  83.5 4.3 %fusion.5 = bf16[256,4202]{0,1:T(8,128)(2,1)S(1)} fusion(f32[256,4202]{0,1:T(8,128)} %copy-done.2, f32[256]{0:T(256)} %get-tuple-element.178, f32[256]{0:T(256)S(1)} %get-tuple-element.133, s32[256]{0:T(256)} %param.41, s32[4202]{0:T(1024)} %copy-done.50), kind=kLoop, calls=%fused_computation.10 | loop fusion | flops 6454272 | bytes 6474152 | tf_op jit(solution)/shard_map/convert_element_type | solution.py:432
  87.9 1.3 copy-done.13
  89.2 3.7 fusion.195.mine
  92.9 2.0 shard_map.338
  96.9 2.0 shard_map.339
  102.6 1.6 reshape.412
  104.2 1.7 copy.136
  105.9 2.1 multiply_reduce_fusion
  110.5 1.7 copy.133
  112.3 1.4 fusion.98.mine
  113.6 2.0 shard_map.340
  115.7 1.4 multiply_reduce_fusion.7
  117.2 1.4 multiply_reduce_fusion.12
  122.2 2.1 copy.138
  124.2 8.6 %all-to-all-start = ((f32[256,16,32]{0,2,1:T(8,128)}), f32[256,16,32]{0,2,1:T(8,128)}, u32[]{:S(2)}, u32[]{:S(2)}) async-start(f32[256,16,32]{0,2,1:T(8,128)} %bitcast.245), calls=%async_computation | async-start | bytes 1048576 | tf_op jit(solution)/shard_map/all_to_all | solution.py:507
  134.1 3.1 fusion.172
  137.2 2.5 fusion.13
  139.7 1.4 fusion.14
  143.0 2.5 copy.135
  145.5 1.5 reshape.447
  147.0 1.5 reshape.448
  148.4 3.6 fusion.31.refs_4_
  152.1 1.5 fusion.29.refs_5_
  156.2 4.4 %shard_map.341 = f32[2048,256]{1,0:T(8,128)S(1)} custom-call(f32[2048,512]{1,0:T(8,128)S(1)} %get-tuple-element.192.mine), custom_call_target="tpu_custom_call" | custom-call | tf_op jit(solution)/shard_map/pallas_call | solution.py:69
  162.8 3.3 concatenate.3.refs_7_
  166.1 3.1 fusion.114
  169.3 4.7 %fusion.6 = f32[512,4224]{1,0:T(8,128)} fusion(bf16[256,512]{1,0:T(8,128)(2,1)S(1)} %copy-done.31, bf16[256,4202]{0,1:T(8,128)(2,1)S(1)} %copy-done.14), kind=kOutput, calls=%fused_computation.18 | convolution fusion | flops 1107296256 | bytes 11064320 | tf_op jit(solution)/shard_map/dot_general | solution.py:271
  174.0 173.8 %shard_map.342 = (f32[32,4224]{1,0:T(8,128)}, f32[32,1024]{1,0:T(8,128)}, f32[32,1024]{1,0:T(8,128)}, f32[32,256]{1,0:T(8,128)}, f32[32,256]{1,0:T(8,128)}, /*in...) custom-call(f32[2,2,2,2,32,4224]{5,4,3,2,1,0:T(8,128)} %bitcast.231, f32[2,2,2,2,32,1024]{5,4,3,2,1,0:T(8,128)} %bitcast.239, ...), custom_call_target="tpu_custom_call" | custom-call | tf_op jit(solution)/shard_map/pallas_call | solution.py:227
  347.8 1.3 slice.199
  349.1 38.5 %all-gather = s32[16,1,256]{2,1,0:T(1,128)S(1)} all-gather(s32[1,1,256]{2,1,0:T(1,128)S(1)} %bitcast.289), channel_id=1, replica_groups=mesh['dp'=16,'mp'=2] {'dp'}, dimensions={0}, use_global_device_ids=true | all-gather | bytes 17408 | tf_op jit(solution)/shard_map/all_gather | solution.py:328
  387.6 1.4 dynamic-slice_bitcast_fusion
  389.0 1.4 constant_dynamic-slice_fusion
  390.4 3.0 copy.148
  393.4 25.1 %scatter_custom_fusion = f32[8404,32]{1,0:T(8,128)} fusion(s32[4096]{0:T(1024)S(1)} %bitcast.290, f32[4096,32]{1,0:T(8,128)} %bitcast.243, f32[]{:T(128)} %constant.47.clone.1), kind=kCustom, calls=%fused_computation.20 | custom fusion | flops 131072 | bytes 1076224 | tf_op jit(solution)/shard_map/scatter-add | solution.py:508
  418.5 3.7 copy.143
  422.2 1.3 copy.204
  (372 shorter events, 44.9 us)
Async XLA Ops:
  0.7 35.9 %copy-start = (bf16[512,1024]{1,0:T(8,128)(2,1)S(1)}, bf16[512,1024]{1,0:T(8,128)(2,1)}, u32[]{:S(2)}) copy-start(bf16[512,1024]{1,0:T(8,128)(2,1)} %param.28) | copy-start | bytes 3145732
  0.7 11.0 %copy-start.3 = (bf16[256,512]{1,0:T(8,128)(2,1)S(1)}, bf16[256,512]{1,0:T(8,128)(2,1)}, u32[]{:S(2)}) copy-start(bf16[256,512]{1,0:T(8,128)(2,1)} %param.21) | copy-start | bytes 786436
  3.7 8.0 %copy-start.32 = (bf16[512,256]{1,0:T(8,128)(2,1)S(1)}, bf16[512,256]{1,0:T(8,128)(2,1)}, u32[]{:S(2)}) copy-start(bf16[512,256]{1,0:T(8,128)(2,1)} %param.24) | copy-start | bytes 786436
  7.0 21.2 %copy-start.57 = (pred[2,1024]{1,0:T(4,128)(4,1)}, pred[2,1024]{1,0:T(4,128)(4,1)S(1)}, u32[]{:S(2)}) copy-start(pred[2,1024]{1,0:T(4,128)(4,1)S(1)} %iota_compare_fusion) | copy-start | bytes 6148
  7.8 37.4 %copy-start.50 = (s32[4202]{0:T(1024)}, s32[4202]{0:T(1024)S(1)}, u32[]{:S(2)}) copy-start(s32[4202]{0:T(1024)S(1)} %iota_add_fusion) | copy-start | bytes 50428
  8.8 47.6 %copy-start.60 = (f32[1,512]{1,0:T(1,128)}, f32[1,512]{1,0:T(1,128)S(1)}, u32[]{:S(2)}) copy-start(f32[1,512]{1,0:T(1,128)S(1)} %get-tuple-element.156) | copy-start | bytes 6148
  8.8 47.6 %copy-start.62 = (f32[1,512]{1,0:T(1,128)}, f32[1,512]{1,0:T(1,128)S(1)}, u32[]{:S(2)}) copy-start(f32[1,512]{1,0:T(1,128)S(1)} %get-tuple-element.158) | copy-start | bytes 6148
  8.8 47.6 %copy-start.64 = (f32[1,512]{1,0:T(1,128)}, f32[1,512]{1,0:T(1,128)S(1)}, u32[]{:S(2)}) copy-start(f32[1,512]{1,0:T(1,128)S(1)} %get-tuple-element.159) | copy-start | bytes 6148
  8.9 47.6 %copy-start.66 = (f32[1,512]{1,0:T(1,128)}, f32[1,512]{1,0:T(1,128)S(1)}, u32[]{:S(2)}) copy-start(f32[1,512]{1,0:T(1,128)S(1)} %get-tuple-element.160) | copy-start | bytes 6148
  8.9 47.6 %copy-start.68 = (f32[1,512]{1,0:T(1,128)}, f32[1,512]{1,0:T(1,128)S(1)}, u32[]{:S(2)}) copy-start(f32[1,512]{1,0:T(1,128)S(1)} %get-tuple-element.161) | copy-start | bytes 6148
  8.9 47.6 %copy-start.70 = (f32[1,512]{1,0:T(1,128)}, f32[1,512]{1,0:T(1,128)S(1)}, u32[]{:S(2)}) copy-start(f32[1,512]{1,0:T(1,128)S(1)} %get-tuple-element.162) | copy-start | bytes 6148
  8.9 47.6 %copy-start.72 = (f32[1,512]{1,0:T(1,128)}, f32[1,512]{1,0:T(1,128)S(1)}, u32[]{:S(2)}) copy-start(f32[1,512]{1,0:T(1,128)S(1)} %get-tuple-element.163) | copy-start | bytes 6148
  8.9 47.6 %copy-start.80 = (f32[1,512]{1,0:T(1,128)}, f32[1,512]{1,0:T(1,128)S(1)}, u32[]{:S(2)}) copy-start(f32[1,512]{1,0:T(1,128)S(1)} %get-tuple-element.157) | copy-start | bytes 6148
  8.9 47.6 %copy-start.82 = (f32[1,512]{1,0:T(1,128)}, f32[1,512]{1,0:T(1,128)S(1)}, u32[]{:S(2)}) copy-start(f32[1,512]{1,0:T(1,128)S(1)} %get-tuple-element.164) | copy-start | bytes 6148
  8.9 47.6 %copy-start.84 = (f32[1,512]{1,0:T(1,128)}, f32[1,512]{1,0:T(1,128)S(1)}, u32[]{:S(2)}) copy-start(f32[1,512]{1,0:T(1,128)S(1)} %get-tuple-element.165) | copy-start | bytes 6148
  8.9 47.6 %copy-start.86 = (f32[1,512]{1,0:T(1,128)}, f32[1,512]{1,0:T(1,128)S(1)}, u32[]{:S(2)}) copy-start(f32[1,512]{1,0:T(1,128)S(1)} %get-tuple-element.166) | copy-start | bytes 6148
  23.0 5.3 %copy-start.9 = (bf16[2,1024,2,128]{1,3,2,0:T(8,128)(2,1)}, bf16[2,1024,2,128]{1,3,2,0:T(8,128)(2,1)S(1)}, u32[]{:S(2)}) copy-start(bf16[2,1024,2,128]{1,3,2,0:T(8,128)(2,1)S(1)} %copy.132) | copy-start | bytes 3145732
  28.3 5.4 %copy-start.25 = (bf16[2,1024,2,128]{3,2,1,0:T(2,128)(2,1)}, bf16[2,1024,2,128]{3,2,1,0:T(2,128)(2,1)S(1)}, u32[]{:S(2)}) copy-start(bf16[2,1024,2,128]{3,2,1,0:T(2,128)(2,1)S(1)} %reshape.404) | copy-start | bytes 3145732
  47.4 7.1 %copy-start.127 = (s32[2]{0:T(128)S(1)}, s32[2]{0:T(128)}, u32[]{:S(2)}) copy-start(s32[2]{0:T(128)} %param.37) | copy-start | bytes 28
  47.4 7.1 %copy-start.132 = (s32[256]{0:T(256)S(1)}, s32[256]{0:T(256)}, u32[]{:S(2)}) copy-start(s32[256]{0:T(256)} %param.40) | copy-start | bytes 3076
  47.4 7.8 %copy-start.74 = (f32[512]{0:T(512)S(1)}, f32[512]{0:T(512)}, u32[]{:S(2)}) copy-start(f32[512]{0:T(512)} %param.31) | copy-start | bytes 6148
  47.4 7.8 %copy-start.122 = (f32[512]{0:T(512)S(1)}, f32[512]{0:T(512)}, u32[]{:S(2)}) copy-start(f32[512]{0:T(512)} %param.32) | copy-start | bytes 6148
  47.5 8.1 %copy-start.128 = (f32[1,256]{1,0:T(1,128)}, f32[1,256]{1,0:T(1,128)S(1)}, u32[]{:S(2)}) copy-start(f32[1,256]{1,0:T(1,128)S(1)} %broadcast.398) | copy-start | bytes 3076
  65.3 3.9 copy-start.99
  65.3 3.9 copy-start.130
  68.6 7.6 %slice-start = ((s8[4308992]{0:T(1024)(128)(4,1)}), s8[4194304]{0:T(1024)(128)(4,1)S(1)}, s32[]{:S(2)}) async-start(s8[4308992]{0:T(1024)(128)(4,1)} %bitcast.232), calls=%async_computation.1 | async-start | bytes 8388608
  68.9 7.2 %copy-start.4 = (f32[256,512]{1,0:T(8,128)}, f32[256,512]{1,0:T(8,128)S(1)}, u32[]{:S(2)}) copy-start(f32[256,512]{1,0:T(8,128)S(1)} %get-tuple-element.137) | copy-start | bytes 1572868
  68.9 4.0 copy-start.90
  69.2 4.5 %copy-start.45 = (bf16[1024,512]{1,0:T(8,128)(2,1)S(1)}, bf16[1024,512]{1,0:T(8,128)(2,1)}, u32[]{:S(2)}) copy-start(bf16[1024,512]{1,0:T(8,128)(2,1)} %param.29) | copy-start | bytes 3145732
  69.2 7.0 %slice-start.1 = ((s8[4308992]{0:T(1024)(128)(4,1)}), s8[114688]{0:T(1024)(128)(4,1)S(1)}, s32[]{:S(2)}) async-start(s8[4308992]{0:T(1024)(128)(4,1)} %bitcast.232), calls=%async_computation.2 | async-start | bytes 229376
  89.2 5.7 %copy-start.46 = (bf16[1024,512]{1,0:T(8,128)(2,1)S(1)}, bf16[1024,512]{1,0:T(8,128)(2,1)}, u32[]{:S(2)}) copy-start(bf16[1024,512]{1,0:T(8,128)(2,1)} %param.29) | copy-start | bytes 3145732
  89.2 5.7 %copy-start.136 = (f32[256,1024]{1,0:T(8,128)S(1)}, f32[256,1024]{1,0:T(8,128)}, u32[]{:S(2)}) copy-start(f32[256,1024]{1,0:T(8,128)} %get-tuple-element.135) | copy-start | bytes 3145732
  89.2 5.7 %copy-start.137 = (f32[256,1024]{1,0:T(8,128)S(1)}, f32[256,1024]{1,0:T(8,128)}, u32[]{:S(2)}) copy-start(f32[256,1024]{1,0:T(8,128)} %get-tuple-element.186) | copy-start | bytes 3145732
  94.9 5.2 %copy-start.1 = (f32[256,512]{1,0:T(8,128)}, f32[256,512]{1,0:T(8,128)S(1)}, u32[]{:S(2)}) copy-start(f32[256,512]{1,0:T(8,128)S(1)} %shard_map.338) | copy-start | bytes 1572868
  99.8 6.1 %copy-start.88 = (f32[2,2,128]{2,1,0:T(2,128)S(1)}, f32[2,2,128]{2,1,0:T(2,128)}, u32[]{:S(2)}) copy-start(f32[2,2,128]{2,1,0:T(2,128)} %log_add_fusion) | copy-start | bytes 6148
  112.2 4.9 %copy-start.18 = (f32[2,128,512]{2,1,0:T(8,128)S(1)}, f32[2,128,512]{2,1,0:T(8,128)}, u32[]{:S(2)}) copy-start(f32[2,128,512]{2,1,0:T(8,128)} %copy-done.17) | copy-start | bytes 1572868
  112.2 4.9 %copy-start.61 = (f32[1,512]{1,0:T(1,128)S(1)}, f32[1,512]{1,0:T(1,128)}, u32[]{:S(2)}) copy-start(f32[1,512]{1,0:T(1,128)} %copy-done.60) | copy-start | bytes 6148
  112.2 4.9 %copy-start.63 = (f32[1,512]{1,0:T(1,128)S(1)}, f32[1,512]{1,0:T(1,128)}, u32[]{:S(2)}) copy-start(f32[1,512]{1,0:T(1,128)} %copy-done.62) | copy-start | bytes 6148
  112.2 4.9 %copy-start.65 = (f32[1,512]{1,0:T(1,128)S(1)}, f32[1,512]{1,0:T(1,128)}, u32[]{:S(2)}) copy-start(f32[1,512]{1,0:T(1,128)} %copy-done.64) | copy-start | bytes 6148
  112.2 4.9 %copy-start.67 = (f32[1,512]{1,0:T(1,128)S(1)}, f32[1,512]{1,0:T(1,128)}, u32[]{:S(2)}) copy-start(f32[1,512]{1,0:T(1,128)} %copy-done.66) | copy-start | bytes 6148
  112.2 4.9 %copy-start.69 = (f32[1,512]{1,0:T(1,128)S(1)}, f32[1,512]{1,0:T(1,128)}, u32[]{:S(2)}) copy-start(f32[1,512]{1,0:T(1,128)} %copy-done.68) | copy-start | bytes 6148
  112.2 4.9 %copy-start.71 = (f32[1,512]{1,0:T(1,128)S(1)}, f32[1,512]{1,0:T(1,128)}, u32[]{:S(2)}) copy-start(f32[1,512]{1,0:T(1,128)} %copy-done.70) | copy-start | bytes 6148
  112.2 4.9 %copy-start.73 = (f32[1,512]{1,0:T(1,128)S(1)}, f32[1,512]{1,0:T(1,128)}, u32[]{:S(2)}) copy-start(f32[1,512]{1,0:T(1,128)} %copy-done.72) | copy-start | bytes 6148
  121.0 11.8 %copy-start.135 = (s32[2]{0:T(128)S(1)}, s32[2]{0:T(128)}, u32[]{:S(2)}) copy-start(s32[2]{0:T(128)} %param.39) | copy-start | bytes 28
  121.0 12.4 %copy-start.40 = (bf16[2,128,2,128]{3,2,1,0:T(2,128)(2,1)S(1)}, bf16[2,128,2,128]{3,2,1,0:T(2,128)(2,1)}, u32[]{:S(2)}) copy-start(bf16[2,128,2,128]{3,2,1,0:T(2,128)(2,1)} %copy.129) | copy-start | bytes 393220
  121.0 13.1 %copy-start.92 = (f32[256]{0:T(256)S(1)}, f32[256]{0:T(256)}, u32[]{:S(2)}) copy-start(f32[256]{0:T(256)} %copy-done.90) | copy-start | bytes 3076
  121.0 13.1 %copy-start.101 = (f32[512]{0:T(512)S(1)}, f32[512]{0:T(512)}, u32[]{:S(2)}) copy-start(f32[512]{0:T(512)} %param.33) | copy-start | bytes 6148
  121.0 13.1 %copy-start.104 = (f32[256]{0:T(256)S(1)}, f32[256]{0:T(256)}, u32[]{:S(2)}) copy-start(f32[256]{0:T(256)} %copy-done.102) | copy-start | bytes 3076
  121.0 13.1 %copy-start.131 = (f32[512]{0:T(512)S(1)}, f32[512]{0:T(512)}, u32[]{:S(2)}) copy-start(f32[512]{0:T(512)} %param.34) | copy-start | bytes 6148
  124.2 13.0 %copy-start.89 = (f32[2,2,128]{2,1,0:T(2,128)S(1)}, f32[2,2,128]{2,1,0:T(2,128)}, u32[]{:S(2)}) copy-start(f32[2,2,128]{2,1,0:T(2,128)} %log_add_fusion) | copy-start | bytes 6148
  124.2 266.2 %all-to-all-start = ((f32[256,16,32]{0,2,1:T(8,128)}), f32[256,16,32]{0,2,1:T(8,128)}, u32[]{:S(2)}, u32[]{:S(2)}) async-start(f32[256,16,32]{0,2,1:T(8,128)} %bitcast.245), calls=%async_computation | async-start | bytes 1048576 | tf_op jit(solution)/shard_map/all_to_all | solution.py:507
  137.2 4.0 copy-start.35
  156.1 4.5 %copy-start.49 = (bf16[256,256,1,1,1,1]{1,0,2,3,4,5:T(8,128)(2,1)S(1)}, bf16[256,256,1,1,1,1]{1,0,2,3,4,5:T(8,128)(2,1)}, u32[]{:S(2)}) copy-start(bf16[256,256,1,1,1,1]{1,0,2,3,4,5:T(8,128)(2,1)} %reshape.449) | copy-start | bytes 393220
  156.1 5.5 %copy-start.43 = (bf16[512,256]{1,0:T(8,128)(2,1)S(1)}, bf16[512,256]{1,0:T(8,128)(2,1)}, u32[]{:S(2)}) copy-start(bf16[512,256]{1,0:T(8,128)(2,1)} %copy.141) | copy-start | bytes 786436
  156.1 6.5 %copy-start.133 = (f32[2]{0:T(128)S(1)}, f32[2]{0:T(128)}, u32[]{:S(2)}) copy-start(f32[2]{0:T(128)} %get-tuple-element.176) | copy-start | bytes 28
  156.1 6.5 %copy-start.134 = (f32[2]{0:T(128)S(1)}, f32[2]{0:T(128)}, u32[]{:S(2)}) copy-start(f32[2]{0:T(128)} %broadcast_subtract_fusion) | copy-start | bytes 28
  156.2 6.6 %copy-start.123 = (f32[512]{0:T(512)S(1)}, f32[512]{0:T(512)}, u32[]{:S(2)}) copy-start(f32[512]{0:T(512)} %get-tuple-element.107) | copy-start | bytes 6148
  156.2 6.6 %copy-start.124 = (f32[512]{0:T(512)S(1)}, f32[512]{0:T(512)}, u32[]{:S(2)}) copy-start(f32[512]{0:T(512)} %get-tuple-element.119) | copy-start | bytes 6148
  156.2 6.6 %copy-start.125 = (f32[512]{0:T(512)S(1)}, f32[512]{0:T(512)}, u32[]{:S(2)}) copy-start(f32[512]{0:T(512)} %get-tuple-element.122) | copy-start | bytes 6148
  161.6 7.6 %copy-start.31 = (bf16[256,512]{1,0:T(8,128)(2,1)S(1)}, bf16[256,512]{1,0:T(8,128)(2,1)}, u32[]{:S(2)}) copy-start(bf16[256,512]{1,0:T(8,128)(2,1)} %copy-done.30) | copy-start | bytes 786436
  174.0 175.1 %copy-start.97 = (s32[256]{0:T(256)S(1)}, s32[256]{0:T(256)}, u32[]{:S(2)}) copy-start(s32[256]{0:T(256)} %param.41) | copy-start | bytes 3076
  422.2 3.8 copy-start.56
  422.2 4.5 %copy-start.55 = (f32[32,1024]{1,0:T(8,128)S(1)}, f32[32,1024]{1,0:T(8,128)}, u32[]{:S(2)}) copy-start(f32[32,1024]{1,0:T(8,128)} %get-tuple-element.30) | copy-start | bytes 393220
  422.2 5.1 %copy-start.48 = (f32[32,4224]{1,0:T(8,128)S(1)}, f32[32,4224]{1,0:T(8,128)}, u32[]{:S(2)}) copy-start(f32[32,4224]{1,0:T(8,128)} %get-tuple-element.31) | copy-start | bytes 1622020
  (77 other events, 157.3 us)

commit v2 on v1

v2 whole, which is shorter than its diff:
```python
from functools import partial
import math

import jax
import jax.numpy as jnp
from jax import lax
from jax.experimental import pallas as pl
from jax.experimental.pallas import tpu as pltpu
from jax.sharding import PartitionSpec as P

HD = 128
V = 8404
EPSILON = 1e-05
MESH = pl.DeviceIdType.MESH
VMEM = pl.BlockSpec(memory_space=pltpu.VMEM)
SMEM = pl.BlockSpec(memory_space=pltpu.SMEM)
ANY = pl.BlockSpec(memory_space=pl.ANY)
F32, BF16 = jnp.float32, jnp.bfloat16
NEG = -1e30


def other_core():
    return {"mp": 1 - lax.axis_index("mp")}


def dot_nn(a, b):
    return lax.dot_general(a, b, (((1,), (0,)), ((), ())), preferred_element_type=F32)


def dot_nt(a, b):
    return lax.dot_general(a, b, (((1,), (1,)), ((), ())), preferred_element_type=F32)


def dot_tn(a, b):
    return lax.dot_general(a, b, (((0,), (0,)), ((), ())), preferred_element_type=F32)


def normalise(rows):
    average = jnp.mean(rows, axis=-1, keepdims=True)
    centred = rows - average
    variance = jnp.mean(centred * centred, axis=-1, keepdims=True)
    scale = lax.rsqrt(variance + EPSILON)
    return centred * scale, scale


def normalise_back(grad_hat, hat, scale):
    first = jnp.mean(grad_hat, axis=-1, keepdims=True)
    second = jnp.mean(grad_hat * hat, axis=-1, keepdims=True)
    return scale * (grad_hat - first - hat * second)


def to_rows(columns):
    lane = lax.broadcasted_iota(jnp.int32, (columns[0].shape[0], 128), 1)
    tile = jnp.zeros(lane.shape, F32)
    for i, column in enumerate(columns):
        tile = jnp.where(lane == i, column, tile)
    return tile.T[:8]


def to_columns(rows):
    return jnp.concatenate([rows] * 16, axis=0).T


def decoder_kernel(
    vocab_here,
    half_cols,
    acoustic,
    taken,
    memory,
    w_query_hbm,
    w_key_hbm,
    w_value_hbm,
    w_out_hbm,
    w_in_hbm,
    w_back_hbm,
    w_vocab_hbm,
    w_tail_hbm,
    gain_one,
    bias_one,
    gain_two,
    bias_two,
    kernel_rows,
    rate_table,
    token_lengths,
    memory_lengths,
    rate_groups,
    glance,
    targets,
    loss_out,
    acoustic_out,
    memory_out,
    terms_out,
    small_out,
    vocab_out,
    in_out,
    back_out,
    query_out,
    out_out,
    kv_out,
    w_query,
    w_kv,
    w_out,
    w_in,
    w_back,
    w_vocab,
    mem_low,
    kv,
    padded,
    stream_in,
    stream_one,
    stream_two,
    stream_three,
    one_low,
    queries,
    probs,
    mixed,
    norm_low,
    hidden,
    gelu_slope,
    top,
    logits,
    grad_logits,
    part3,
    arrived3,
    grad_three,
    grad_two,
    branch_low,
    grad_pre,
    att_low,
    grad_queries,
    grad_kv,
    mem_part,
    mem_arrived,
    meta,
    stats,
    stats_arrived,
    sent,
    arrived,
    gathered,
    load_sem,
    swap_send,
    swap_recv,
):
    utterances, slots = targets.shape
    width = acoustic.shape[1]
    frames = memory.shape[0] // utterances
    heads = w_query_hbm.shape[1] // HD
    tokens = utterances * slots
    me, core = lax.axis_index("dp"), lax.axis_index("mp")
    side = lax.rem(me, 2)
    sibling = {"mp": 1 - core}
    pair = {"dp": me + 1 - 2 * side}
    cross = {"dp": me + 1 - 2 * side, "mp": 1 - core}
    score_scale = 1.0 / math.sqrt(HD)

    loads = []

    def load(source, target):
        copy = pltpu.make_async_copy(source, target, load_sem.at[len(loads)])
        copy.start()
        loads.append(copy)
        return copy

    load_memory = load(memory, mem_low)
    half = heads * HD
    load_kv = [
        load(w_key_hbm, w_kv.at[:, pl.ds(0, half)]),
        load(w_value_hbm, w_kv.at[:, pl.ds(half, half)]),
    ]
    load_query = load(w_query_hbm, w_query)
    load_out = load(w_out_hbm, w_out)
    load_in = load(w_in_hbm, w_in)
    load_back = load(w_back_hbm, w_back)
    main = w_vocab.shape[1] - w_tail_hbm.shape[1]
    load_vocab = [
        load(w_vocab_hbm.at[:, pl.ds(0, main)], w_vocab.at[:, pl.ds(0, main)]),
        load(w_tail_hbm, w_vocab.at[:, pl.ds(main, w_tail_hbm.shape[1])]),
    ]

    barrier = pltpu.get_barrier_semaphore()
    for device in (sibling, pair, cross):
        pl.semaphore_signal(barrier, inc=1, device_id=device, device_id_type=MESH)
    pl.semaphore_wait(barrier, 3)

    swaps = []

    def swap(source, target, device):
        k = len(swaps)
        copy = pltpu.make_async_remote_copy(
            src_ref=source,
            dst_ref=target,
            send_sem=swap_send.at[k],
            recv_sem=swap_recv.at[k],
            device_id=device,
            device_id_type=MESH,
        )
        copy.start()
        swaps.append(copy)
        return copy

    lane = lax.broadcasted_iota(jnp.int32, (1, slots), 1)
    row_of = lax.broadcasted_iota(jnp.int32, (8, slots), 0)
    for u in range(utterances):
        target_row = targets[pl.ds(u, 1), :].astype(F32)
        glance_row = glance[pl.ds(u, 1), :].astype(F32)
        valid_row = (lane < token_lengths[u]).astype(F32)
        meta[0, :, pl.ds(u * slots, slots)] = jnp.where(
            row_of == 0, target_row, jnp.where(row_of == 1, valid_row, glance_row)
        )
    meta_swap = swap(meta.at[0], meta.at[1], pair)
    own_columns = to_columns(meta[0])
    own_target = own_columns[:, 0:1]
    own_valid = own_columns[:, 1:2]
    own_glance = own_columns[:, 2:3]

    def rows(u):
        return pl.ds(u * slots, slots)

    gain_1, bias_1, gain_2, bias_2 = gain_one[...], bias_one[...], gain_two[...], bias_two[...]

    load_memory.wait()
    for copy in load_kv:
        copy.wait()
    step_rows = 256

    def kv_step(i, carry):
        at = pl.ds(pl.multiple_of(i * step_rows, step_rows), step_rows)
        group = jnp.zeros((1, width), jnp.int32) + rate_groups[i // (frames // step_rows)]
        rate_row = jnp.where(group == 1, rate_table[pl.ds(1, 1), :], rate_table[pl.ds(0, 1), :])
        low = (mem_low[at, :].astype(F32) + rate_row).astype(BF16)
        mem_low[at, :] = low
        kv[at, :] = dot_nn(low, w_kv[...]).astype(BF16)
        return carry

    lax.fori_loop(0, utterances * frames // step_rows, kv_step, 0)

    edge = jnp.zeros((8, width), F32)
    for u in range(utterances):
        padded[u, pl.ds(0, 8), :] = edge
        padded[u, pl.ds(8 + slots, 8), :] = edge

    load_query.wait()
    load_out.wait()

    def key_of(u, h):
        return kv[pl.ds(u * frames, frames), pl.ds(h * HD, HD)]

    def value_of(u, h):
        return kv[pl.ds(u * frames, frames), pl.ds(half + h * HD, HD)]

    frame_lane = lax.broadcasted_iota(jnp.int32, (1, frames), 1)

    def local_targets(target_column):
        local = target_column.astype(jnp.int32) - core * vocab_here
        return jnp.where((local >= 0) & (local < vocab_here), local, -1)

    def vocab_tile(tile, first, col, target, top_m, picked):
        ids = col + lax.broadcasted_iota(jnp.int32, (1, 128), 1)
        tile = jnp.where(ids < vocab_here, tile, NEG)
        logits[first] = tile
        return jnp.maximum(top_m, tile), picked + jnp.where(ids == target, tile, 0.0)

    def vocab_stats(top_rows, target, base, wide, narrow, first):
        start = (jnp.full((tokens, 128), NEG, F32), jnp.zeros((tokens, 128), F32))

        def step(j, carry):
            col = pl.multiple_of(base + j * 256, 128)
            product = dot_nn(top_rows(), w_vocab[:, pl.ds(col, 256)])
            carry = vocab_tile(product[:, :128], first + 2 * j, col, target, *carry)
            return vocab_tile(product[:, 128:], first + 2 * j + 1, col + 128, target, *carry)

        top_m, picked = lax.fori_loop(0, wide, step, start)
        if narrow:
            col = pl.multiple_of(base + wide * 256, 128)
            product = dot_nn(top_rows(), w_vocab[:, pl.ds(col, 128)])
            top_m, picked = vocab_tile(product, first + 2 * wide, col, target, top_m, picked)
        top_row = jnp.max(top_m, axis=1, keepdims=True)

        def add(j, total):
            return total + jnp.exp(logits[first + j] - top_row)

        total = lax.fori_loop(0, 2 * wide + narrow, add, jnp.zeros((tokens, 128), F32))
        return (
            top_row,
            jnp.sum(total, axis=1, keepdims=True),
            jnp.sum(picked, axis=1, keepdims=True),
        )

    def join(blocks):
        top_value = blocks[0][0:1]
        for b in blocks[1:]:
            top_value = jnp.maximum(top_value, b[0:1])
        total, picked = 0.0, 0.0
        for b in blocks:
            total = total + b[1:2] * jnp.exp(b[0:1] - top_value)
            picked = picked + b[2:3]
        return top_value + jnp.log(total), picked

    def forward(second):
        copies = []
        for u in range(utterances):
            at = rows(u)
            valid = own_valid[u * slots : (u + 1) * slots]
            hat, _ = normalise(stream_in[at, :])
            padded[u, pl.ds(8, slots), :] = (hat * gain_1 + bias_1) * valid
            for j in range(width // 128):
                cols = pl.ds(j * 128, 128)
                total = jnp.zeros((slots, 128), F32)
                for k in range(kernel_rows.shape[0]):
                    shift = 8 + k - kernel_rows.shape[0] // 2
                    total = total + kernel_rows[pl.ds(k, 1), cols] * padded[u, pl.ds(shift, slots), cols]
                stream_one[at, cols] = stream_in[at, cols] + total * valid
            low = stream_one[at, :].astype(BF16)
            one_low[at, :] = low
            queries[at, :] = dot_nn(low, w_query[...]).astype(BF16)
            frame_ok = frame_lane < memory_lengths[u]
            for h in range(heads):
                cols = pl.ds(h * HD, HD)
                scores = dot_nt(queries[at, cols], key_of(u, h)) * score_scale
                scores = jnp.where(frame_ok, scores, NEG)
                raised = jnp.exp(scores - jnp.max(scores, axis=-1, keepdims=True))
                prob = raised / jnp.sum(raised, axis=-1, keepdims=True)
                if second:
                    probs[u, h] = prob
                mixed[at, cols] = dot_nn(prob.astype(BF16), value_of(u, h)).astype(BF16)
            sent[u] = dot_nn(mixed[at, :], w_out[...])
            copies.append(swap(sent.at[u], arrived.at[u], sibling))
        if not second:
            load_in.wait()
            load_back.wait()
        ff_copies = []
        for u in range(utterances):
            at = rows(u)
            copies[u].wait()
            two = stream_one[at, :] + (sent[u] + arrived[u])
            stream_two[at, :] = two
            hat, _ = normalise(two)
            low = (hat * gain_2 + bias_2).astype(BF16)
            norm_low[at, :] = low
            pre = dot_nn(low, w_in[...])
            phi = 0.5 * (1.0 + lax.erf(pre * math.sqrt(0.5)))
            hidden[at, :] = (pre * phi).astype(BF16)
            if second:
                gelu_slope[at, :] = phi + pre * (
                    jnp.exp(-0.5 * pre * pre) * (1.0 / math.sqrt(2.0 * math.pi))
                )
            sent[utterances + u] = dot_nn(hidden[at, :], w_back[...])
            ff_copies.append(swap(sent.at[utterances + u], arrived.at[utterances + u], sibling))
        for u in range(utterances):
            at = rows(u)
            ff_copies[u].wait()
            three = stream_two[at, :] + (sent[utterances + u] + arrived[utterances + u])
            stream_three[u] = three
            top[0, at, :] = three.astype(BF16)

    stream_in[...] = acoustic[...].astype(F32)
    forward(False)
    for copy in load_vocab:
        copy.wait()
    first = vocab_stats(lambda: top[0], local_targets(own_target), 0, w_vocab.shape[1] // 256, 0, 0)
    stats[0, :, pl.ds(0, tokens)] = to_rows(first)
    first_swap = swap(stats.at[0, :, pl.ds(0, tokens)], stats_arrived.at[0, :, pl.ds(0, tokens)], sibling)
    wide_acoustic = acoustic[...].astype(F32)
    difference = taken[...].astype(F32) - wide_acoustic
    first_swap.wait()
    log_total, picked = join([stats[0, :, :tokens], stats_arrived[0, :, :tokens]])
    first_loss = (log_total - picked) * meta[0, 1:2, :]
    blend_row = meta[0, 2:3, :] * meta[0, 1:2, :] / (1.0 + jnp.exp(math.log(V) - first_loss))
    blend = to_columns(jnp.concatenate([blend_row] * 8, axis=0))[:, 0:1]
    stream_in[...] = wide_acoustic + blend * difference

    forward(True)
    token_swap = swap(stream_three.at[core], gathered.at[0], pair)
    base = side * half_cols
    wide, narrow = half_cols // 256, half_cols % 256 // 128
    per_group = 2 * wide + narrow
    meta_swap.wait()
    pair_columns = to_columns(meta[1])
    group_target = [local_targets(own_target), local_targets(pair_columns[:, 0:1])]
    group_valid = [own_valid, pair_columns[:, 1:2]]
    own_stats = vocab_stats(lambda: top[0], group_target[0], base, wide, narrow, 0)
    stats[1, :, pl.ds(0, tokens)] = to_rows(own_stats)
    token_swap.wait()
    share_swap = swap(gathered.at[0], gathered.at[1], sibling)
    at_core = pl.ds(pl.multiple_of(core * slots, slots), slots)
    at_other = pl.ds(pl.multiple_of((1 - core) * slots, slots), slots)
    top[1, at_core, :] = gathered[0].astype(BF16)
    share_swap.wait()
    top[1, at_other, :] = gathered[1].astype(BF16)
    pair_stats = vocab_stats(lambda: top[1], group_target[1], base, wide, narrow, per_group)
    stats[1, :, pl.ds(tokens, tokens)] = to_rows(pair_stats)
    stat_swaps = [
        swap(stats.at[1], stats_arrived.at[1], sibling),
        swap(stats.at[1], stats_arrived.at[2], pair),
        swap(stats.at[1], stats_arrived.at[3], cross),
    ]
    for copy in stat_swaps:
        copy.wait()

    def group_blocks(g):
        mine, theirs = pl.ds(g * tokens, tokens), pl.ds((1 - g) * tokens, tokens)
        return [
            stats[1, :, mine],
            stats_arrived[1, :, mine],
            stats_arrived[2, :, theirs],
            stats_arrived[3, :, theirs],
        ]

    log_totals = []
    for g in range(2):
        log_total, picked = join(group_blocks(g))
        log_totals.append(to_columns(jnp.concatenate([log_total] * 8, axis=0))[:, 0:1])
        if g == 0:
            loss = (log_total - picked) * meta[0, 1:2, :]
            for u in range(utterances):
                loss_out[pl.ds(u, 1), :] = loss[:, u * slots : (u + 1) * slots]

    for g in (1, 0):
        log_column, valid, target = log_totals[g], group_valid[g], group_target[g]

        def slope(j, carry):
            col = pl.multiple_of(j * 128, 128)
            ids = base + col + lax.broadcasted_iota(jnp.int32, (1, 128), 1)
            onehot = jnp.where(ids == target, 1.0, 0.0)
            grad = (jnp.exp(logits[g * per_group + j] - log_column) - onehot) * valid
            grad_logits[pl.ds(g * tokens, tokens), pl.ds(col, 128)] = grad.astype(BF16)
            return carry

        lax.fori_loop(0, per_group, slope, 0)
        part = dot_nt(
            grad_logits[pl.ds(g * tokens, tokens), :],
            w_vocab[:, pl.ds(pl.multiple_of(base, 128), half_cols)],
        )
        for u in range(utterances):
            part3[u, g] = part[u * slots : (u + 1) * slots]
    three_swap = swap(part3.at[1 - core], arrived3, sibling)
    top_all = jnp.concatenate([top[0], top[1]], axis=0)

    def vocab_grad(col, cols):
        vocab_out[:, pl.ds(col, cols)] = dot_tn(top_all, grad_logits[:, pl.ds(col, cols)])

    for j in range(wide):
        vocab_grad(j * 256, 256)
        if j == 0:
            three_swap.wait()
            sent[0] = part3[core, 1] + arrived3[1]
            pair_swap = swap(sent.at[0], arrived.at[0], pair)
    if narrow:
        vocab_grad(wide * 256, 128)
    pair_swap.wait()
    grad_three[core] = (part3[core, 0] + arrived3[0]) + arrived[0]
    share_three = swap(grad_three.at[core], arrived.at[1], sibling)
    share_three.wait()
    grad_three[1 - core] = arrived[1]

    copies = []
    for u in range(utterances):
        at = rows(u)
        low = grad_three[u].astype(BF16)
        branch_low[at, :] = low
        pre = (dot_nt(low, w_back[...]) * gelu_slope[at, :]).astype(BF16)
        grad_pre[at, :] = pre
        sent[utterances + u] = dot_nt(pre, w_in[...])
        copies.append(swap(sent.at[utterances + u], arrived.at[utterances + u], sibling))
    back_out[...] = dot_tn(branch_low[...], hidden[...])
    in_out[...] = dot_tn(norm_low[...], grad_pre[...])

    one_copies = []
    gain_2_total, bias_2_total = 0.0, 0.0
    for u in range(utterances):
        at = rows(u)
        copies[u].wait()
        grad_norm = sent[utterances + u] + arrived[utterances + u]
        hat, scale = normalise(stream_two[at, :])
        gain_2_total = gain_2_total + jnp.sum(grad_norm * hat, axis=0, keepdims=True)
        bias_2_total = bias_2_total + jnp.sum(grad_norm, axis=0, keepdims=True)
        two = grad_three[u] + normalise_back(grad_norm * gain_2, hat, scale)
        grad_two[at, :] = two
        low = two.astype(BF16)
        att_low[at, :] = low
        grad_mixed = dot_nt(low, w_out[...]).astype(BF16)
        for h in range(heads):
            cols = pl.ds(h * HD, HD)
            grad_head = grad_mixed[:, h * HD : (h + 1) * HD]
            prob = probs[u, h]
            grad_prob = dot_nt(grad_head, value_of(u, h))
            grad_kv[pl.ds(u * frames, frames), pl.ds(half + h * HD, HD)] = dot_tn(
                prob.astype(BF16), grad_head
            ).astype(BF16)
            inner = jnp.sum(prob * grad_prob, axis=-1, keepdims=True)
            grad_score = (prob * (grad_prob - inner)).astype(BF16)
            grad_queries[at, cols] = (dot_nn(grad_score, key_of(u, h)) * score_scale).astype(BF16)
            grad_kv[pl.ds(u * frames, frames), cols] = (
                dot_tn(grad_score, queries[at, cols]) * score_scale
            ).astype(BF16)
        sent[u] = dot_nt(grad_queries[at, :], w_query[...])
        one_copies.append(swap(sent.at[u], arrived.at[u], sibling))
    out_out[...] = dot_tn(att_low[...], mixed[...])
    query_out[...] = dot_tn(one_low[...], grad_queries[...])

    mem_copies = []
    for u in range(utterances):
        total = jnp.zeros((1, width), F32)
        for i in range(frames // step_rows):
            at = pl.ds(u * frames + i * step_rows, step_rows)
            part = dot_nt(grad_kv[at, :], w_kv[...])
            mem_part[0, at, :] = part[:, : width // 2]
            mem_part[1, at, :] = part[:, width // 2 :]
            total = total + jnp.sum(part, axis=0, keepdims=True)
        at = pl.ds(u * frames, frames)
        mem_copies.append(swap(mem_part.at[1 - core, at, :], mem_arrived.at[at, :], sibling))
        group = jnp.zeros((1, width), jnp.int32) + rate_groups[u]
        for r in range(2):
            share = jnp.where((group == 1) == (r == 1), total, 0.0)
            if u == 0:
                small_out[pl.ds(16 + r, 1), :] = share
            else:
                small_out[pl.ds(16 + r, 1), :] = small_out[pl.ds(16 + r, 1), :] + share
        product = dot_tn(mem_low[at, :], grad_kv[at, :])
        kv_out[...] = product if u == 0 else kv_out[...] + product

    gain_1_total, bias_1_total = 0.0, 0.0
    for u in range(utterances):
        at = rows(u)
        valid = own_valid[u * slots : (u + 1) * slots]
        one_copies[u].wait()
        one = grad_two[at, :] + (sent[u] + arrived[u])
        grad_two[at, :] = one
        masked = one * valid
        for k in range(kernel_rows.shape[0]):
            shift = 8 + k - kernel_rows.shape[0] // 2
            row = jnp.sum(masked * padded[u, pl.ds(shift, slots), :], axis=0, keepdims=True)
            if u == 0:
                small_out[pl.ds(k, 1), :] = row
            else:
                small_out[pl.ds(k, 1), :] = small_out[pl.ds(k, 1), :] + row
        padded[u, pl.ds(8, slots), :] = masked
        for j in range(width // 128):
            cols = pl.ds(j * 128, 128)
            total = jnp.zeros((slots, 128), F32)
            for k in range(kernel_rows.shape[0]):
                shift = 8 - k + kernel_rows.shape[0] // 2
                total = total + kernel_rows[pl.ds(k, 1), cols] * padded[u, pl.ds(shift, slots), cols]
            stream_one[at, cols] = total * valid
        grad_norm = stream_one[at, :]
        hat, scale = normalise(stream_in[at, :])
        gain_1_total = gain_1_total + jnp.sum(grad_norm * hat, axis=0, keepdims=True)
        bias_1_total = bias_1_total + jnp.sum(grad_norm, axis=0, keepdims=True)
        zero = grad_two[at, :] + normalise_back(grad_norm * gain_1, hat, scale)
        terms = blend[u * slots : (u + 1) * slots] * zero
        terms_out[at, :] = terms
        acoustic_out[at, :] = zero - terms
    small_out[pl.ds(11, 1), :] = jnp.zeros((1, width), F32)
    for i, row in enumerate((gain_1_total, bias_1_total, gain_2_total, bias_2_total)):
        small_out[pl.ds(12 + i, 1), :] = row
    small_out[pl.ds(18, 6), :] = jnp.zeros((6, width), F32)
    for u in range(utterances):
        at = pl.ds(u * frames, frames)
        mem_copies[u].wait()
        memory_out[at, :] = mem_part[core, at, :] + mem_arrived[at, :]


def decoder_call(
    acoustic, taken, memory, w_query, w_key, w_value, w_out, w_in, w_back, w_vocab, norms,
    fsmn_kernel, rate_table, token_lengths, memory_lengths, rate_groups, glance, targets,
):
    utterances = token_lengths.shape[0]
    tokens, width = acoustic.shape
    slots = tokens // utterances
    mem_rows = memory.shape[0]
    frames = mem_rows // utterances
    half = w_query.shape[1]
    heads = half // HD
    units = w_in.shape[1]
    vocab_here = w_vocab.shape[1]
    half_cols = (vocab_here + 255) // 256 * 128
    main = vocab_here // 128 * 128
    w_tail = jnp.pad(w_vocab[:, main:], ((0, 0), (0, 2 * half_cols - vocab_here)))
    f32 = lambda *shape: jax.ShapeDtypeStruct(shape, F32)
    out_shape = [
        f32(utterances, slots),
        f32(tokens, width),
        f32(mem_rows, width // 2),
        f32(tokens, width),
        f32(24, width),
        f32(width, half_cols),
        f32(width, units),
        f32(width, units),
        f32(width, half),
        f32(width, half),
        f32(width, 2 * half),
    ]
    v32 = lambda *shape: pltpu.VMEM(shape, F32)
    v16 = lambda *shape: pltpu.VMEM(shape, BF16)
    scratch = [
        v16(width, half),
        v16(width, 2 * half),
        v16(half, width),
        v16(width, units),
        v16(units, width),
        v16(width, 2 * half_cols),
        v16(mem_rows, width),
        v16(mem_rows, 2 * half),
        v32(utterances, slots + 16, width),
        v32(tokens, width),
        v32(tokens, width),
        v32(tokens, width),
        v32(utterances, slots, width),
        v16(tokens, width),
        v16(tokens, half),
        v32(utterances, heads, slots, frames),
        v16(tokens, half),
        v16(tokens, width),
        v16(tokens, units),
        v32(tokens, units),
        v16(2, tokens, width),
        v32(2 * half_cols // 128, tokens, 128),
        v16(2 * tokens, half_cols),
        v32(utterances, 2, slots, width),
        v32(2, slots, width),
        v32(utterances, slots, width),
        v32(tokens, width),
        v16(tokens, width),
        v16(tokens, units),
        v16(tokens, width),
        v16(tokens, half),
        v16(mem_rows, 2 * half),
        v32(2, mem_rows, width // 2),
        v32(mem_rows, width // 2),
        v32(2, 8, tokens),
        v32(2, 8, 2 * tokens),
        v32(4, 8, 2 * tokens),
        v32(2 * utterances, slots, width),
        v32(2 * utterances, slots, width),
        v32(2, slots, width),
        pltpu.SemaphoreType.DMA((16,)),
        pltpu.SemaphoreType.DMA((32,)),
        pltpu.SemaphoreType.DMA((32,)),
    ]
    return pl.pallas_call(
        partial(decoder_kernel, vocab_here, half_cols),
        out_shape=out_shape,
        in_specs=[VMEM] * 2 + [ANY] * 9 + [VMEM] * 6 + [SMEM] * 3 + [VMEM] * 2,
        out_specs=[VMEM] * len(out_shape),
        scratch_shapes=scratch,
        compiler_params=pltpu.CompilerParams(
            collective_id=1, has_side_effects=True, vmem_limit_bytes=62 << 20
        ),
    )(
        acoustic, taken, memory, w_query, w_key, w_value, w_out, w_in, w_back, w_vocab, w_tail,
        *[n[None] for n in norms], fsmn_kernel, rate_table,
        token_lengths, memory_lengths, rate_groups,
        glance.reshape(utterances, slots), targets.reshape(utterances, slots),
    )


def scatter_sum_kernel(bits, low_bits, chunks, shared_rows, n_in, *refs):
    ins, small = refs[:n_in], refs[n_in]
    outs, small_out = refs[n_in + 1 : 2 * n_in + 1], refs[2 * n_in + 1]
    scratch = list(refs[2 * n_in + 2 :])
    n_chunks = len(chunks)
    arrived = []
    for _, _, _, order in chunks:
        arrived.append([scratch.pop(0) for _ in order])
    small_arrived, small_sent, send_sem, recv_sem, small_send, small_recv = scratch
    me = lax.axis_index("dp")
    bit_of = {b: lax.rem(me // (1 << b), 2) for b in low_bits + bits}
    peer_of = {b: {"dp": me + (1 - 2 * bit_of[b]) * (1 << b)} for b in low_bits + bits}
    trade = not low_bits

    barrier = pltpu.get_barrier_semaphore()
    for b in low_bits + bits:
        pl.semaphore_signal(barrier, inc=1, device_id=peer_of[b], device_id_type=MESH)
    pl.semaphore_signal(barrier, inc=1, device_id=other_core(), device_id_type=MESH)
    pl.semaphore_wait(barrier, len(low_bits) + len(bits) + 1)

    def pick(c, step, half):
        source, start, width, order = chunks[c]
        rest = sorted([b for b in bits if b not in order[:step]], reverse=True)
        where = tuple(half if b == order[step] else slice(None) for b in rest)
        if step == 0:
            return ins[source], where + (slice(None), pl.ds(start, width))
        return arrived[c][step - 1], where + (slice(None), slice(None))

    def send(c, step):
        b = chunks[c][3][step]
        ref, where = pick(c, step, 1 - bit_of[b])
        copy = pltpu.make_async_remote_copy(
            src_ref=ref.at[where],
            dst_ref=arrived[c][step],
            send_sem=send_sem.at[c, step],
            recv_sem=recv_sem.at[c, step],
            device_id=peer_of[b],
            device_id_type=MESH,
        )
        copy.start()
        return copy

    def take(c, step, copy):
        source, start, width, order = chunks[c]
        ref, where = pick(c, step, bit_of[order[step]])
        copy.wait_recv()
        got = arrived[c][step]
        cols = pl.ds(start, width)
        if source == 0 and trade and step == len(order) - 1:
            outs[0][bit_of[0], :, cols] = ref[where]
            outs[0][1 - bit_of[0], :, cols] = got[...]
        elif step == len(order) - 1:
            outs[source][:, cols] = got[...] + ref[where]
        else:
            got[...] = got[...] + ref[where]

    small_peers = [peer_of[b] for b in low_bits + bits] + [other_core()]
    small_sent[0] = small[...]

    def small_send_step(step):
        copy = pltpu.make_async_remote_copy(
            src_ref=small_sent.at[step],
            dst_ref=small_arrived.at[step],
            send_sem=small_send.at[step],
            recv_sem=small_recv.at[step],
            device_id=small_peers[step],
            device_id_type=MESH,
        )
        copy.start()
        return copy

    def small_take(step, copy):
        copy.wait_recv()
        if step + 1 < len(small_peers):
            small_sent[step + 1] = small_sent[step] + small_arrived[step]
        else:
            small_out[...] = small_sent[step]
            rows = small_out.shape[0] - shared_rows
            small_out[pl.ds(shared_rows, rows)] = (
                small_sent[step, pl.ds(shared_rows, rows)]
                + small_arrived[step, pl.ds(shared_rows, rows)]
            )

    started = []
    small_copy = small_send_step(0)
    small_step = 0
    started.append(small_copy)
    flying = {}
    for c in range(n_chunks):
        flying[c] = send(c, 0)
        started.append(flying[c])
    longest = max(len(order) for _, _, _, order in chunks)
    for wave in range(n_chunks + 2 * (longest - 1)):
        for step in reversed(range(longest)):
            c = wave - 2 * step
            if not 0 <= c < n_chunks or step >= len(chunks[c][3]):
                continue
            take(c, step, flying[c])
            if step + 1 < len(chunks[c][3]):
                flying[c] = send(c, step + 1)
                started.append(flying[c])
        if small_step < len(small_peers):
            small_take(small_step, small_copy)
            small_step += 1
            if small_step < len(small_peers):
                small_copy = small_send_step(small_step)
                started.append(small_copy)
    for copy in started:
        copy.wait_send()


def scatter_sum(parts, small, shared_rows, n_dp):
    nbits = n_dp.bit_length() - 1
    rows = parts[0].shape[0]
    steps = nbits
    while rows >> steps < 8:
        steps -= 1
    low_bits, bits = list(range(nbits - steps)), list(range(nbits - steps, nbits))
    block = rows >> steps
    shaped = [p.reshape((2,) * steps + (block, p.shape[1])) for p in parts]
    swapped = [bits[1], bits[0]] + bits[2:]
    chunks = []
    for i, p in enumerate(parts):
        width = p.shape[1]
        pieces = max(1, width // 512)
        edges = [width // 128 * k // pieces * 128 for k in range(pieces)] + [width]
        for k in range(pieces):
            order = [bits, swapped][len(chunks) % 2]
            if i == 0:
                order = [b for b in bits if b != 0]
                if k % 2:
                    order = order[1:] + order[:1]
                if not low_bits:
                    order = order + [0]
            chunks.append((i, edges[k], edges[k + 1] - edges[k], order))
    scratch = []
    for _, _, width, order in chunks:
        for step in range(len(order)):
            scratch.append(pltpu.VMEM((2,) * (len(bits) - 1 - step) + (block, width), F32))
    n_small = nbits + 1
    scratch += [
        pltpu.VMEM((n_small,) + small.shape, F32),
        pltpu.VMEM((n_small,) + small.shape, F32),
        pltpu.SemaphoreType.DMA((len(chunks), steps)),
        pltpu.SemaphoreType.DMA((len(chunks), steps)),
        pltpu.SemaphoreType.DMA((n_small,)),
        pltpu.SemaphoreType.DMA((n_small,)),
    ]
    out_shape = [jax.ShapeDtypeStruct((block, p.shape[1]), F32) for p in parts]
    if not low_bits:
        out_shape[0] = jax.ShapeDtypeStruct((2,) + out_shape[0].shape, F32)
    out = pl.pallas_call(
        partial(scatter_sum_kernel, bits, low_bits, chunks, shared_rows, len(parts)),
        out_shape=out_shape + [jax.ShapeDtypeStruct(small.shape, F32)],
        in_specs=[VMEM] * (len(parts) + 1),
        out_specs=[VMEM] * (len(parts) + 1),
        scratch_shapes=scratch,
        compiler_params=pltpu.CompilerParams(
            collective_id=4, has_side_effects=True, vmem_limit_bytes=56 << 20
        ),
    )(*shaped, small)
    summed, small_sum = list(out[:-1]), out[-1]
    if low_bits:
        size = 1 << len(low_bits)
        groups = [list(range(g * size, (g + 1) * size)) for g in range(n_dp // size)]
        first = lax.all_to_all(
            summed[0].reshape(2, block // 2, -1), "dp", 0, 0,
            axis_index_groups=[[2 * g, 2 * g + 1] for g in range(n_dp // 2)], tiled=True,
        )
        summed = [first] + [
            lax.psum_scatter(s, "dp", scatter_dimension=0, axis_index_groups=groups, tiled=True)
            for s in summed[1:]
        ]
    vocab = jnp.concatenate([summed[0][0], summed[0][1]], axis=1)
    return [vocab] + summed[1:], small_sum


def per_device(
    acoustic,
    memory,
    embedding,
    w_query,
    w_key,
    w_value,
    w_out,
    w_in,
    w_back,
    w_vocab,
    gain_one,
    bias_one,
    gain_two,
    bias_two,
    fsmn_kernel,
    rate_table,
    token_lengths,
    memory_lengths,
    rate_groups,
    glance_mask,
    targets,
):
    tok_rows, model_width = acoustic.shape
    half = w_query.shape[1]
    (
        token_loss, grad_acoustic, grad_memory, table_terms, small,
        grad_vocab, grad_in, grad_back, grad_query, grad_out, grad_kv,
    ) = decoder_call(
        acoustic, embedding[targets], memory, w_query, w_key, w_value, w_out, w_in, w_back, w_vocab,
        (gain_one, bias_one, gain_two, bias_two), fsmn_kernel, rate_table,
        token_lengths, memory_lengths, rate_groups, glance_mask, targets,
    )
    group_size = lax.axis_size("dp")
    id_columns = jnp.broadcast_to(targets.astype(F32)[:, None], (tok_rows, group_size))
    arrived_rows, arrived_ids = (
        lax.all_to_all(table_terms, "dp", split_axis=1, concat_axis=0, tiled=True),
        lax.all_to_all(id_columns, "dp", split_axis=1, concat_axis=0, tiled=True),
    )
    grad_embedding = jax.ops.segment_sum(
        arrived_rows, arrived_ids[:, 0].astype(jnp.int32), num_segments=embedding.shape[0]
    )
    (grad_vocab, grad_in, grad_back, grad_query, grad_out, grad_kv), small = scatter_sum(
        [grad_vocab, grad_in, grad_back, grad_query, grad_out, grad_kv], small, 16, group_size
    )
    own = model_width // group_size
    grad_rate = small[16:18]
    small = lax.dynamic_slice_in_dim(small, lax.axis_index("dp") * own, own, axis=1)
    return (
        token_loss.reshape(tok_rows),
        grad_acoustic,
        grad_memory,
        grad_embedding,
        grad_query,
        grad_kv[:, :half],
        grad_kv[:, half:],
        grad_out.T,
        grad_in,
        grad_back.T,
        grad_vocab[:, : w_vocab.shape[1]],
        small[12],
        small[13],
        small[14],
        small[15],
        small[: fsmn_kernel.shape[0]],
        grad_rate,
    )


def solution(mesh):
    return jax.shard_map(
        per_device,
        mesh=mesh,
        in_specs=(
            P("dp", None),
            P("dp", None),
            P(),
            P(None, "mp"),
            P(None, "mp"),
            P(None, "mp"),
            P("mp", None),
            P(None, "mp"),
            P("mp", None),
            P(None, "mp"),
            P(),
            P(),
            P(),
            P(),
            P(),
            P(),
            P("dp"),
            P("dp"),
            P("dp"),
            P("dp"),
            P("dp"),
        ),
        out_specs=(
            P("dp"),
            P("dp", None),
            P("dp", "mp"),
            P(None, "dp"),
            P("dp", "mp"),
            P("dp", "mp"),
            P("dp", "mp"),
            P("mp", "dp"),
            P("dp", "mp"),
            P("mp", "dp"),
            P("dp", "mp"),
            P("dp"),
            P("dp"),
            P("dp"),
            P("dp"),
            P(None, "dp"),
            P(),
        ),
        check_vma=False,
    )
```

time: 436 us -> 279 us (0.64); the launches traced: 428 us -> 279 us
  matrix products: 60.9 us -> 0 us
  blocking collectives: 38.5 us -> 0 us
  local copies, waits for them, and re-layouts: 65 us -> 32.6 us
  other arithmetic: 57.8 us -> 26.2 us
  waiting for transfers between devices: 0.01 us -> 7.19 us
  Pallas kernels: 195 us -> 200 us
    dot_general x32 -> x0, matrix products: 57.8 us -> none  [the longest x11 18.4 us: product(): return jnp.dot(left_side, right_side, preferred_element_type=jnp.float32)]
    pallas_call x10 -> x1, Pallas kernels: 20.8 us -> 75.9 us  [decoder_call(): pl.pallas_call(partial(decoder_kernel, vocab_here, half_cols), out_shape=...]
    pallas_call x1, Pallas kernels: 174 us -> 124 us  [scatter_sum(): pl.pallas_call(partial(scatter_sum_kernel, bits, low_bits, chunks, shared...]
    all_gather x1 -> x0, blocking collectives: 38.5 us -> none  [per_device(): all_targets = lax.all_gather(targets, 'dp', tiled=True)]
    reduce_sum x19 -> x0, other arithmetic: 14.5 us -> none  [the longest x2 2.87 us: memory_block(): kernel[position] * padded[:, position:position + token_slots]]
    reshape x12 -> x0, local copies, waits for them, and re-layouts: 10.6 us -> none  [the longest x2 3.26 us: per_device(): grad_mixed = product_right(grad_attended, w_out).astype(jnp.bfloat16).res...]
    unnamed x291 -> x25, local copies, waits for them, and re-layouts: 24.1 us -> 15.7 us
    all_to_all x0 -> x1, starting transfers between devices: none -> 8.31 us  [per_device(): lax.all_to_all(id_columns, 'dp', split_axis=1, concat_axis=0, tiled=True)]
  transfers between devices with their start and end apart: 1 -> 2, of which waited for: 0 -> 1; matrix products, arithmetic and copies ran while one was open for 9% -> 8% of each run, Pallas kernels for 42% -> 72%
where the time goes in v2:
time: 279 us
  Pallas kernels  200 us (72%)
  local copies, waits for them, and re-layouts  32.6 us (12%)
  other arithmetic  26.2 us (9%)
  starting transfers between devices  12.2 us (4%)
  waiting for transfers between devices  7.19 us (3%)
    pallas_call x1, Pallas kernels, scatter_sum(): pl.pallas_call(partial(scatter_sum_kernel, bits, low_bits, chunks, shared...  124 us
    pallas_call x1, Pallas kernels, decoder_call(): pl.pallas_call(partial(decoder_kernel, vocab_here, half_cols), out_shape=...  75.9 us
    scatter-add x1, other arithmetic, per_device(): jax.ops.segment_sum(arrived_rows, arrived_ids[:, 0].astype(jnp.int32), nu...  24.6 us
    unnamed x25, local copies, waits for them, and re-layouts  15.7 us
    all_to_all x1, starting transfers between devices, per_device(): lax.all_to_all(id_columns, 'dp', split_axis=1, concat_axis=0, tiled=True)  8.31 us
    all_to_all x1, waiting for transfers between devices, per_device(): lax.all_to_all(table_terms, 'dp', split_axis=1, concat_axis=0, tiled=True)  7.18 us
    gather x1, local copies, waits for them, and re-layouts, per_device(): embedding[targets]  6.46 us
  transfers between devices with their start and end apart: 2, of which 1 were waited for; matrix products, arithmetic and copies ran while one was open for 8% of the time, Pallas kernels for 72%

profile of v2, /device:TPU:0, one launch (start us, length us, event | category | flops | bytes accessed | tf_op | source)
XLA Modules:
  0.0 278.7 jit_solution(12459854662992724597)
XLA Ops:
  0.7 0.8 fusion.3
  1.4 0.6 broadcast_in_dim.31
  2.0 8.3 %all-to-all-start = ((f32[256,16,1]{0,2,1:T(1,128)}), f32[256,16,1]{0,2,1:T(1,128)S(1)}, u32[]{:S(2)}, u32[]{:S(2)}) async-start(f32[256,16,1]{0,2,1:T(1,128)} %broadcast_in_dim.31), calls=%async_computation | async-start | bytes 32768 | tf_op jit(solution)/shard_map/all_to_all | solution.py:871
  10.3 6.6 %copy.52.w_vocab_hbm = bf16[512,4202]{1,0:T(8,128)(2,1)} copy(bf16[512,4202]{0,1:T(8,128)(2,1)} %param.30) | data formatting | bytes 8605696 | tf_op args[9]
  16.9 0.9 slice.50
  17.9 0.7 pad.4.w_tail_hbm
  18.6 6.5 %gather_fusion = bf16[256,512]{1,0:T(8,128)(2,1)} fusion(bf16[8404,512]{1,0:T(8,128)(2,1)} %param.23, s32[1024]{0:T(1024)S(1)} %pad_clamp_fusion), kind=kCustom, calls=%fused_computation | custom fusion | bytes 525312 | tf_op jit(solution)/shard_map/gather | solution.py:863
  25.1 75.9 %shard_map.332 = (f32[2,128]{1,0:T(2,128)}, f32[256,512]{1,0:T(8,128)}, f32[2048,256]{1,0:T(8,128)}, f32[256,512]{1,0:T(8,128)}, f32[24,512]{1,0:T(8,128)}, /*in...) custom-call(bf16[256,512]{1,0:T(8,128)(2,1)} %acoustic.1, ...), custom_call_target="tpu_custom_call" | custom-call | tf_op jit(solution)/shard_map/pallas_call | solution.py:640
  100.9 0.0 copy-start.2
  101.0 123.9 %shard_map.333 = (f32[2,32,2176]{2,1,0:T(8,128)}, f32[32,1024]{1,0:T(8,128)}, f32[32,1024]{1,0:T(8,128)}, f32[32,256]{1,0:T(8,128)}, f32[32,256]{1,0:T(8,128)}, /*index=5*/f32[32,512]{1,0:T(8,128)}, f32[24,512]{1,0:T(8,128)}) custom-call(f32[2,2,2,2,32,2176]{5,4,3,2,1,0:T(8,128)} %bitcast.33, f32[2,2,2,2,32,1024]{5,4,3,2,1,0:T(8,128)} %bitcast.36, ...), custom_call_target="tpu_custom_call" | custom-call | tf_op jit(solution)/shard_map/pallas_call | solution.py:808
  224.9 1.1 slice_bitcast_fusion.1
  225.9 1.3 slice.47
  227.3 0.0 copy-done.2
  227.3 1.0 copy.53
  228.2 0.0 all-to-all-done
  228.3 3.9 %all-to-all-start.1 = ((f32[256,16,32]{0,2,1:T(8,128)}), f32[256,16,32]{0,2,1:T(8,128)S(1)}, u32[]{:S(2)}, u32[]{:S(2)}) async-start(f32[256,16,32]{0,2,1:T(8,128)} %bitcast.9), calls=%async_computation.1 | async-start | bytes 1048576 | tf_op jit(solution)/shard_map/all_to_all | solution.py:870
  232.2 1.4 dynamic-slice_bitcast_fusion
  233.6 1.4 constant_dynamic-slice_fusion
  235.0 1.4 fusion.2
  236.4 0.8 pad_maximum_fusion
  237.2 7.2 %all-to-all-done.1 = f32[256,16,32]{0,2,1:T(8,128)S(1)} async-done(((f32[256,16,32]{0,2,1:T(8,128)}), f32[256,16,32]{0,2,1:T(8,128)S(1)}, u32[]{:S(2)}, u32[]{:S(2)}) %all-to-all-start.1) | async-done | bytes 524320 | tf_op jit(solution)/shard_map/all_to_all | solution.py:870
  244.4 0.6 copy.57
  245.0 0.0 copy-start.7
  245.0 0.0 copy-start.1
  245.0 24.6 %scatter_custom_fusion = f32[8404,32]{1,0:T(8,128)} fusion(s32[4096]{0:T(1024)S(1)} %bitcast.43, f32[4096,32]{1,0:T(8,128)S(1)} %bitcast.34, f32[]{:T(128)} %constant.6.clone.1), kind=kCustom, calls=%fused_computation.2 | custom fusion | flops 131072 | bytes 1075716 | tf_op jit(solution)/shard_map/scatter-add | solution.py:873
  269.6 0.0 copy-start
  269.6 0.0 copy-start.6
  269.6 0.0 copy-start.5
  269.6 0.0 copy-start.4
  269.6 0.0 copy-start.3
  269.6 3.8 %copy.56 = f32[8404,32]{0,1:T(8,128)} copy(f32[8404,32]{1,0:T(8,128)} %scatter_custom_fusion) | data formatting | bytes 2151424
  273.4 0.0 copy-done.7
  273.4 0.6 copy.66
  274.0 0.0 copy-done.1
  274.0 0.8 copy.67
  274.8 0.0 copy-done
  274.8 1.3 copy.68
  276.1 0.0 copy-done.6
  276.1 0.6 copy.69
  276.7 0.0 copy-done.5
  276.7 0.6 copy.70
  277.3 0.0 copy-done.4
  277.3 0.7 copy.71
  278.0 0.0 copy-done.3
  278.0 0.7 copy.72
  (2 shorter events, 0.0 us)
Async XLA Ops:
  2.0 226.2 %all-to-all-start = ((f32[256,16,1]{0,2,1:T(1,128)}), f32[256,16,1]{0,2,1:T(1,128)S(1)}, u32[]{:S(2)}, u32[]{:S(2)}) async-start(f32[256,16,1]{0,2,1:T(1,128)} %broadcast_in_dim.31), calls=%async_computation | async-start | bytes 32768 | tf_op jit(solution)/shard_map/all_to_all | solution.py:871
  100.9 126.3 %copy-start.2 = (f32[256,512]{1,0:T(8,128)S(1)}, f32[256,512]{1,0:T(8,128)}, u32[]{:S(2)}) copy-start(f32[256,512]{1,0:T(8,128)} %get-tuple-element.38) | copy-start | bytes 1572868
  228.3 16.1 %all-to-all-start.1 = ((f32[256,16,32]{0,2,1:T(8,128)}), f32[256,16,32]{0,2,1:T(8,128)S(1)}, u32[]{:S(2)}, u32[]{:S(2)}) async-start(f32[256,16,32]{0,2,1:T(8,128)} %bitcast.9), calls=%async_computation.1 | async-start | bytes 1048576 | tf_op jit(solution)/shard_map/all_to_all | solution.py:870
  245.0 28.4 %copy-start.7 = (f32[2,128]{1,0:T(2,128)S(1)}, f32[2,128]{1,0:T(2,128)}, u32[]{:S(2)}) copy-start(f32[2,128]{1,0:T(2,128)} %get-tuple-element.35) | copy-start | bytes 3076
  245.0 29.0 %copy-start.1 = (f32[256,512]{1,0:T(8,128)S(1)}, f32[256,512]{1,0:T(8,128)}, u32[]{:S(2)}) copy-start(f32[256,512]{1,0:T(8,128)} %get-tuple-element.132) | copy-start | bytes 1572868
  269.6 5.2 %copy-start = (f32[2048,256]{1,0:T(8,128)S(1)}, f32[2048,256]{1,0:T(8,128)}, u32[]{:S(2)}) copy-start(f32[2048,256]{1,0:T(8,128)} %get-tuple-element.133) | copy-start | bytes 6291460
  269.6 6.5 %copy-start.6 = (f32[32,256]{1,0:T(8,128)S(1)}, f32[32,256]{1,0:T(8,128)}, u32[]{:S(2)}) copy-start(f32[32,256]{1,0:T(8,128)} %get-tuple-element.135) | copy-start | bytes 98308
  269.6 7.1 %copy-start.5 = (f32[32,256]{1,0:T(8,128)S(1)}, f32[32,256]{1,0:T(8,128)}, u32[]{:S(2)}) copy-start(f32[32,256]{1,0:T(8,128)} %get-tuple-element.48) | copy-start | bytes 98308
  269.6 7.8 %copy-start.4 = (f32[32,1024]{1,0:T(8,128)S(1)}, f32[32,1024]{1,0:T(8,128)}, u32[]{:S(2)}) copy-start(f32[32,1024]{1,0:T(8,128)} %get-tuple-element.139) | copy-start | bytes 393220
  269.6 8.4 %copy-start.3 = (f32[32,1024]{1,0:T(8,128)S(1)}, f32[32,1024]{1,0:T(8,128)}, u32[]{:S(2)}) copy-start(f32[32,1024]{1,0:T(8,128)} %get-tuple-element.50) | copy-start | bytes 393220

commit v3 on v2

v3 whole, which is shorter than its diff:
```python
import math
from types import SimpleNamespace

import jax
import jax.numpy as jnp
from jax import lax
from jax.experimental import pallas as pl
from jax.experimental.pallas import tpu as pltpu
from jax.sharding import PartitionSpec as P

HD = 128
V = 8404
EPSILON = 1e-05
MESH = pl.DeviceIdType.MESH
VMEM = pl.BlockSpec(memory_space=pltpu.VMEM)
SMEM = pl.BlockSpec(memory_space=pltpu.SMEM)
ANY = pl.BlockSpec(memory_space=pl.ANY)
F32, BF16 = jnp.float32, jnp.bfloat16
NEG = -1e30


def other_core():
    return {"mp": 1 - lax.axis_index("mp")}


def dot_nn(a, b):
    return lax.dot_general(a, b, (((1,), (0,)), ((), ())), preferred_element_type=F32)


def dot_nt(a, b):
    return lax.dot_general(a, b, (((1,), (1,)), ((), ())), preferred_element_type=F32)


def dot_tn(a, b):
    return lax.dot_general(a, b, (((0,), (0,)), ((), ())), preferred_element_type=F32)


def normalise(rows):
    average = jnp.mean(rows, axis=-1, keepdims=True)
    centred = rows - average
    variance = jnp.mean(centred * centred, axis=-1, keepdims=True)
    scale = lax.rsqrt(variance + EPSILON)
    return centred * scale, scale


def normalise_back(grad_hat, hat, scale):
    first = jnp.mean(grad_hat, axis=-1, keepdims=True)
    second = jnp.mean(grad_hat * hat, axis=-1, keepdims=True)
    return scale * (grad_hat - first - hat * second)


def to_rows(columns):
    lane = lax.broadcasted_iota(jnp.int32, (columns[0].shape[0], 128), 1)
    tile = jnp.zeros(lane.shape, F32)
    for i, column in enumerate(columns):
        tile = jnp.where(lane == i, column, tile)
    return tile.T[:8]


def to_columns(rows):
    return jnp.concatenate([rows] * 16, axis=0).T


class Planner:
    RATE = 0.0425e6
    HOP = 1.5
    BACKLOG = 12.0

    def __init__(self):
        self.now = 0.0
        self.free = {}
        self.flying = []
        self.waiting = []
        self.started = []
        self.count = 0

    def launch(self, item, step):
        link, size = item.steps[step]
        begin = max(self.now, self.free.get(link, 0.0))
        self.free[link] = begin + size / self.RATE
        copy = item.send(step)
        self.started.append(copy)
        self.count += 1
        self.flying.append((self.free[link] + self.HOP, self.count, item, step, copy))

    def release(self):
        kept = []
        for item in self.waiting:
            link = item.steps[0][0]
            if self.free.get(link, 0.0) - self.now < self.BACKLOG:
                self.launch(item, 0)
            else:
                kept.append(item)
        self.waiting = kept

    def post(self, *items):
        self.waiting += items
        self.release()

    def run_until(self, time):
        while self.flying or self.waiting:
            if not self.flying:
                self.now = max(self.now, min(self.free[i.steps[0][0]] for i in self.waiting))
                self.release()
                continue
            first = min(self.flying, key=lambda f: f[:2])
            if first[0] > time:
                break
            self.flying.remove(first)
            self.now = max(self.now, first[0])
            _, _, item, step, copy = first
            item.take(step, copy)
            if step + 1 < len(item.steps):
                self.launch(item, step + 1)
            self.release()
        if time != math.inf:
            self.now = max(self.now, time)
        self.release()

    def finish(self):
        self.run_until(math.inf)
        for copy in self.started:
            copy.wait_send()


class Chunk:
    def __init__(self, steps, send, take):
        self.steps, self.send, self.take = steps, send, take


def decoder_kernel(
    names,
    vocab_here,
    half_cols,
    table_rows,
    n_dp,
    bits,
    low_bits,
    *refs,
):
    r = SimpleNamespace(**dict(zip(names, refs)))
    acoustic, memory, table, tails = r.acoustic, r.memory, r.table, r.tails
    targets, glance = r.targets, r.glance
    gain_1, bias_1 = r.gain_one[...], r.bias_one[...]
    gain_2, bias_2 = r.gain_two[...], r.bias_two[...]
    kernel_rows, rate_table = r.kernel_rows, r.rate_table
    token_lengths, memory_lengths, rate_groups = r.token_lengths, r.memory_lengths, r.rate_groups
    w_query, w_kv, w_out, w_in, w_back, w_vocab = r.w_query, r.w_kv, r.w_out, r.w_in, r.w_back, r.w_vocab
    mem_low, kv, padded, spare = r.mem_low, r.kv, r.padded, r.spare
    stream_in, stream_one, stream_two, stream_three = r.stream_in, r.stream_one, r.stream_two, r.stream_three
    one_low, queries, probs, mixed = r.one_low, r.queries, r.probs, r.mixed
    norm_low, hidden, gelu_slope, top = r.norm_low, r.hidden, r.gelu_slope, r.top
    logits, grad_logits, part3, arrived3 = r.logits, r.grad_logits, r.part3, r.arrived3
    grad_three, grad_two, branch_low = r.grad_three, r.grad_two, r.branch_low
    grad_pre, att_low, grad_queries = r.grad_pre, r.att_low, r.grad_queries
    mem_arrived, meta, stats, stats_arrived = r.mem_arrived, r.meta, r.stats, r.stats_arrived
    sent, arrived, gathered = r.sent, r.arrived, r.gathered
    small_sent, small_arrived = r.small_sent, r.small_arrived
    terms, term_blocks, term_arrived = grad_three, r.term_blocks, r.term_arrived
    onehot_lo, table_theirs, table_out = r.onehot_lo, r.table_theirs, r.table_out
    swap_send, swap_recv, load_sem = r.swap_send, r.swap_recv, r.load_sem

    utterances, slots = targets.shape
    width = acoustic.shape[1]
    frames = memory.shape[0] // utterances
    half = w_query.shape[1]
    heads = half // HD
    tokens = utterances * slots
    me, core = lax.axis_index("dp"), lax.axis_index("mp")
    side = lax.rem(me, 2)
    sibling = {"mp": 1 - core}
    pair = {"dp": me + 1 - 2 * side}
    cross = {"dp": me + 1 - 2 * side, "mp": 1 - core}
    bit_of = {b: lax.rem(me // (1 << b), 2) for b in low_bits + bits}
    peer_of = {b: {"dp": me + (1 - 2 * bit_of[b]) * (1 << b)} for b in low_bits + bits}
    score_scale = 1.0 / math.sqrt(HD)

    loads = []

    def load(source, target):
        copy = pltpu.make_async_copy(source, target, load_sem.at[len(loads)])
        copy.start()
        loads.append(copy)
        return copy

    load_memory = load(memory, mem_low)
    load_kv = [
        load(r.w_key_hbm, w_kv.at[:, pl.ds(0, half)]),
        load(r.w_value_hbm, w_kv.at[:, pl.ds(half, half)]),
    ]
    load_query = load(r.w_query_hbm, w_query)
    load_out = load(r.w_out_hbm, w_out)

    barrier = pltpu.get_barrier_semaphore()

    def greet(k, carry):
        pl.semaphore_signal(
            barrier, inc=1, device_id={"dp": lax.rem(me + k, n_dp)}, device_id_type=MESH
        )
        return carry

    lax.fori_loop(1, n_dp, greet, 0)
    for device in (sibling, cross):
        pl.semaphore_signal(barrier, inc=1, device_id=device, device_id_type=MESH)

    load_in = load(r.w_in_hbm, w_in)
    load_back = load(r.w_back_hbm, w_back)
    block = 1024
    per_core = table_rows // (2 * block)
    mains = 2 * per_core * block

    def load_table(k):
        at = pl.ds(pl.multiple_of((core * per_core + k) * block, block), block)
        return load(table.at[at, :], spare.at[pl.ds(k % 2 * block, block), :])

    table_loads = [load_table(0), load_table(1)]
    tail_rows = tails.shape[0] - 256
    main = w_vocab.shape[0] - tail_rows
    load_vocab = [
        load(r.w_vocab_hbm.at[pl.ds(0, main), :], w_vocab.at[pl.ds(0, main), :]),
        load(tails.at[pl.ds(0, tail_rows), :], w_vocab.at[pl.ds(main, tail_rows), :]),
    ]

    swaps = []

    def swap(source, target, device):
        k = len(swaps)
        copy = pltpu.make_async_remote_copy(
            src_ref=source,
            dst_ref=target,
            send_sem=swap_send.at[k],
            recv_sem=swap_recv.at[k],
            device_id=device,
            device_id_type=MESH,
        )
        copy.start()
        swaps.append(copy)
        return copy

    lane = lax.broadcasted_iota(jnp.int32, (1, slots), 1)
    row_of = lax.broadcasted_iota(jnp.int32, (8, slots), 0)
    for u in range(utterances):
        target_row = targets[pl.ds(u, 1), :].astype(F32)
        glance_row = glance[pl.ds(u, 1), :].astype(F32)
        valid_row = (lane < token_lengths[u]).astype(F32)
        meta[0, :, pl.ds(u * slots, slots)] = jnp.where(
            row_of == 0, target_row, jnp.where(row_of == 1, valid_row, glance_row)
        )
    own_columns = to_columns(meta[0])
    own_target = own_columns[:, 0:1]
    own_valid = own_columns[:, 1:2]

    def rows(u):
        return pl.ds(u * slots, slots)

    load_memory.wait()
    for copy in load_kv:
        copy.wait()
    step_rows = 256
    row_chunks = frames // step_rows

    def kv_step(i, carry):
        at = pl.ds(pl.multiple_of(i * step_rows, step_rows), step_rows)
        group = jnp.zeros((1, width), jnp.int32) + rate_groups[i // row_chunks]
        rate_row = jnp.where(group == 1, rate_table[pl.ds(1, 1), :], rate_table[pl.ds(0, 1), :])
        low = (mem_low[at, :].astype(F32) + rate_row).astype(BF16)
        mem_low[at, :] = low
        kv[at, :] = dot_nn(low, w_kv[...]).astype(BF16)
        return carry

    lax.fori_loop(0, utterances * row_chunks, kv_step, 0)

    edge = jnp.zeros((8, width), F32)
    for u in range(utterances):
        padded[u, pl.ds(0, 8), :] = edge
        padded[u, pl.ds(8 + slots, 8), :] = edge

    pl.semaphore_wait(barrier, n_dp + 1)
    meta_swap = swap(meta.at[0], meta.at[1], pair)
    load_query.wait()
    load_out.wait()

    def key_of(u, h):
        return kv[pl.ds(u * frames, frames), pl.ds(h * HD, HD)]

    def value_of(u, h):
        return kv[pl.ds(u * frames, frames), pl.ds(half + h * HD, HD)]

    frame_lane = lax.broadcasted_iota(jnp.int32, (1, frames), 1)

    def look_up(first_row, count, allowed, source):
        ids = first_row + lax.broadcasted_iota(jnp.int32, (1, count), 1)
        local = jnp.where(allowed, own_target.astype(jnp.int32), -1)
        onehot = jnp.where(ids == local, 1.0, 0.0).astype(BF16)
        return dot_nn(onehot, source)

    def look_up_block(k):
        table_loads[k].wait()
        part = look_up(
            (core * per_core + k) * block, block, True, spare[pl.ds(k % 2 * block, block), :]
        )
        for u in range(utterances):
            piece = part[u * slots : (u + 1) * slots]
            part3[0, u] = piece if k == 0 else part3[0, u] + piece
        if k + 2 < per_core:
            table_loads.append(load_table(k + 2))

    def look_up_rest():
        part = look_up(mains, 256, core == 0, tails[pl.ds(tail_rows, 256), :])
        for u in range(utterances):
            part3[0, u] = part3[0, u] + part[u * slots : (u + 1) * slots]

    def local_targets(target_column):
        local = target_column.astype(jnp.int32) - core * vocab_here
        return jnp.where((local >= 0) & (local < vocab_here), local, -1)

    def vocab_tile(tile, first, col, target, top_m, picked):
        ids = col + lax.broadcasted_iota(jnp.int32, (1, 128), 1)
        tile = jnp.where(ids < vocab_here, tile, NEG)
        logits[first] = tile
        return jnp.maximum(top_m, tile), picked + jnp.where(ids == target, tile, 0.0)

    def vocab_stats(g, target, base, wide, narrow, first):
        start = (jnp.full((tokens, 128), NEG, F32), jnp.zeros((tokens, 128), F32))

        def step(j, carry):
            col = pl.multiple_of(base + j * 256, 128)
            product = dot_nt(top[g], w_vocab[pl.ds(col, 256), :])
            carry = vocab_tile(product[:, :128], first + 2 * j, col, target, *carry)
            return vocab_tile(product[:, 128:], first + 2 * j + 1, col + 128, target, *carry)

        top_m, picked = lax.fori_loop(0, wide, step, start)
        if narrow:
            col = pl.multiple_of(base + wide * 256, 128)
            product = dot_nt(top[g], w_vocab[pl.ds(col, 128), :])
            top_m, picked = vocab_tile(product, first + 2 * wide, col, target, top_m, picked)
        top_row = jnp.max(top_m, axis=1, keepdims=True)

        def add(j, total):
            return total + jnp.exp(logits[first + j] - top_row)

        total = lax.fori_loop(0, 2 * wide + narrow, add, jnp.zeros((tokens, 128), F32))
        return (
            top_row,
            jnp.sum(total, axis=1, keepdims=True),
            jnp.sum(picked, axis=1, keepdims=True),
        )

    def join(blocks):
        top_value = blocks[0][0:1]
        for b in blocks[1:]:
            top_value = jnp.maximum(top_value, b[0:1])
        total, picked = 0.0, 0.0
        for b in blocks:
            total = total + b[1:2] * jnp.exp(b[0:1] - top_value)
            picked = picked + b[2:3]
        return top_value + jnp.log(total), picked

    def forward(second, beside_one=None, beside_two=None):
        copies = []
        for u in range(utterances):
            at = rows(u)
            valid = own_valid[u * slots : (u + 1) * slots]
            hat, _ = normalise(stream_in[at, :])
            padded[u, pl.ds(8, slots), :] = (hat * gain_1 + bias_1) * valid
            for j in range(width // 128):
                cols = pl.ds(j * 128, 128)
                total = jnp.zeros((slots, 128), F32)
                for k in range(kernel_rows.shape[0]):
                    shift = 8 + k - kernel_rows.shape[0] // 2
                    total = total + kernel_rows[pl.ds(k, 1), cols] * padded[u, pl.ds(shift, slots), cols]
                stream_one[at, cols] = stream_in[at, cols] + total * valid
            low = stream_one[at, :].astype(BF16)
            one_low[at, :] = low
            queries[at, :] = dot_nn(low, w_query[...]).astype(BF16)
            frame_ok = frame_lane < memory_lengths[u]
            for h in range(heads):
                cols = pl.ds(h * HD, HD)
                scores = dot_nt(queries[at, cols], key_of(u, h)) * score_scale
                scores = jnp.where(frame_ok, scores, NEG)
                raised = jnp.exp(scores - jnp.max(scores, axis=-1, keepdims=True))
                prob = raised / jnp.sum(raised, axis=-1, keepdims=True)
                if second:
                    probs[u, h] = prob
                mixed[at, cols] = dot_nn(prob.astype(BF16), value_of(u, h)).astype(BF16)
            sent[u] = dot_nn(mixed[at, :], w_out[...])
            copies.append(swap(sent.at[u], arrived.at[u], sibling))
        if not second:
            beside_one()
            load_in.wait()
            load_back.wait()
        ff_copies = []
        for u in range(utterances):
            at = rows(u)
            copies[u].wait()
            two = stream_one[at, :] + (sent[u] + arrived[u])
            stream_two[at, :] = two
            hat, _ = normalise(two)
            low = (hat * gain_2 + bias_2).astype(BF16)
            norm_low[at, :] = low
            pre = dot_nn(low, w_in[...])
            phi = 0.5 * (1.0 + lax.erf(pre * math.sqrt(0.5)))
            hidden[at, :] = (pre * phi).astype(BF16)
            if second:
                gelu_slope[at, :] = phi + pre * (
                    jnp.exp(-0.5 * pre * pre) * (1.0 / math.sqrt(2.0 * math.pi))
                )
            sent[utterances + u] = dot_nn(hidden[at, :], w_back[...])
            ff_copies.append(swap(sent.at[utterances + u], arrived.at[utterances + u], sibling))
        if not second:
            beside_two()
        for u in range(utterances):
            at = rows(u)
            ff_copies[u].wait()
            three = stream_two[at, :] + (sent[utterances + u] + arrived[utterances + u])
            stream_three[u] = three
            top[0, at, :] = three.astype(BF16)

    stream_in[...] = acoustic[...].astype(F32)

    def beside_one():
        look_up_block(0)
        look_up_block(1)

    def beside_two():
        for k in range(2, per_core):
            look_up_block(k)
        look_up_rest()

    forward(False, beside_one, beside_two)
    table_swap = swap(part3.at[0], arrived3, sibling)
    for copy in load_vocab:
        copy.wait()
    first = vocab_stats(0, local_targets(own_target), 0, w_vocab.shape[0] // 256, 0, 0)
    stats[0, :, pl.ds(0, tokens)] = to_rows(first)
    first_swap = swap(stats.at[0, :, pl.ds(0, tokens)], stats_arrived.at[0, :, pl.ds(0, tokens)], sibling)
    table_swap.wait()
    first_swap.wait()
    log_total, picked = join([stats[0, :, :tokens], stats_arrived[0, :, :tokens]])
    first_loss = (log_total - picked) * meta[0, 1:2, :]
    blend_row = meta[0, 2:3, :] * meta[0, 1:2, :] / (1.0 + jnp.exp(math.log(V) - first_loss))
    blend = to_columns(jnp.concatenate([blend_row] * 8, axis=0))[:, 0:1]
    for u in range(utterances):
        at = rows(u)
        wide_acoustic = acoustic[at, :].astype(F32)
        taken = part3[0, u] + arrived3[u]
        stream_in[at, :] = wide_acoustic + blend[u * slots : (u + 1) * slots] * (taken - wide_acoustic)

    forward(True)
    token_swap = swap(stream_three.at[core], gathered.at[0], pair)
    base = side * half_cols
    wide, narrow = half_cols // 256, half_cols % 256 // 128
    per_group = 2 * wide + narrow
    meta_swap.wait()
    pair_columns = to_columns(meta[1])
    group_target = [local_targets(own_target), local_targets(pair_columns[:, 0:1])]
    group_valid = [own_valid, pair_columns[:, 1:2]]
    own_stats = vocab_stats(0, group_target[0], base, wide, narrow, 0)
    stats[1, :, pl.ds(0, tokens)] = to_rows(own_stats)
    token_swap.wait()
    share_swap = swap(gathered.at[0], gathered.at[1], sibling)
    at_core = pl.ds(pl.multiple_of(core * slots, slots), slots)
    at_other = pl.ds(pl.multiple_of((1 - core) * slots, slots), slots)
    top[1, at_core, :] = gathered[0].astype(BF16)
    share_swap.wait()
    top[1, at_other, :] = gathered[1].astype(BF16)
    pair_stats = vocab_stats(1, group_target[1], base, wide, narrow, per_group)
    stats[1, :, pl.ds(tokens, tokens)] = to_rows(pair_stats)
    stat_swaps = [
        swap(stats.at[1], stats_arrived.at[1], sibling),
        swap(stats.at[1], stats_arrived.at[2], pair),
        swap(stats.at[1], stats_arrived.at[3], cross),
    ]
    for copy in stat_swaps:
        copy.wait()

    def group_blocks(g):
        mine, theirs = pl.ds(g * tokens, tokens), pl.ds((1 - g) * tokens, tokens)
        return [
            stats[1, :, mine],
            stats_arrived[1, :, mine],
            stats_arrived[2, :, theirs],
            stats_arrived[3, :, theirs],
        ]

    log_totals = []
    for g in range(2):
        log_total, picked = join(group_blocks(g))
        log_totals.append(to_columns(jnp.concatenate([log_total] * 8, axis=0))[:, 0:1])
        if g == 0:
            loss = (log_total - picked) * meta[0, 1:2, :]
            for u in range(utterances):
                r.loss_out[pl.ds(u, 1), :] = loss[:, u * slots : (u + 1) * slots]

    plan = Planner()
    steps_all = len(bits)
    trade = not low_bits
    scatter_send, scatter_recv = r.scatter_send, r.scatter_recv

    def make_chunk(index):
        name, start, cols, order = chunk_list(half_cols, width, bits, low_bits, r)[index]
        source, landing = getattr(r, "src_" + name), r.landing[index]
        out = getattr(r, name + "_out")
        rows_here = source.shape[-2]

        def pick(step, which):
            rest = sorted([b for b in bits if b not in order[:step]], reverse=True)
            where = tuple(which if b == order[step] else slice(None) for b in rest)
            if step == 0:
                return source, where + (slice(None), pl.ds(start, cols))
            return landing[step - 1], where + (slice(None), slice(None))

        def send(step):
            b = order[step]
            ref, where = pick(step, 1 - bit_of[b])
            copy = pltpu.make_async_remote_copy(
                src_ref=ref.at[where],
                dst_ref=landing[step],
                send_sem=scatter_send.at[index, step],
                recv_sem=scatter_recv.at[index, step],
                device_id=peer_of[b],
                device_id_type=MESH,
            )
            copy.start()
            return copy

        def take(step, copy):
            copy.wait_recv()
            ref, where = pick(step, bit_of[order[step]])
            got = landing[step]
            at = pl.ds(start, cols)
            last = step == len(order) - 1
            if last and name == "vocab" and trade:
                out[bit_of[0], :, at] = ref[where]
                out[1 - bit_of[0], :, at] = got[...]
            elif last:
                out[:, at] = got[...] + ref[where]
            else:
                got[...] = got[...] + ref[where]

        steps = [
            (link_of(b, bits), rows_here * cols * 4 * 2 ** (steps_all - 1 - s))
            for s, b in enumerate(order)
        ]
        return Chunk(steps, send, take)

    chunks = {}
    for index, (name, start, _, _) in enumerate(chunk_list(half_cols, width, bits, low_bits, r)):
        chunks[name, start] = make_chunk(index)

    def put(name, at, product):
        source = getattr(r, "src_" + name)
        source[..., at] = product.reshape(source.shape[:-1] + (product.shape[1],))

    for g in (1, 0):
        log_column, valid, target = log_totals[g], group_valid[g], group_target[g]

        def slope(j, carry):
            col = pl.multiple_of(j * 128, 128)
            ids = base + col + lax.broadcasted_iota(jnp.int32, (1, 128), 1)
            onehot = jnp.where(ids == target, 1.0, 0.0)
            grad = (jnp.exp(logits[g * per_group + j] - log_column) - onehot) * valid
            grad_logits[pl.ds(g * tokens, tokens), pl.ds(col, 128)] = grad.astype(BF16)
            return carry

        lax.fori_loop(0, per_group, slope, 0)
        part = dot_nn(
            grad_logits[pl.ds(g * tokens, tokens), :],
            w_vocab[pl.ds(pl.multiple_of(base, 128), half_cols), :],
        )
        for u in range(utterances):
            part3[u, g] = part[u * slots : (u + 1) * slots]
    three_swap = swap(part3.at[1 - core], arrived3, sibling)
    top_all = jnp.concatenate([top[0], top[1]], axis=0)
    vocab_starts = sorted(start for name, start in chunks if name == "vocab")
    pair_swap = None
    for i, start in enumerate(vocab_starts):
        stop = (vocab_starts + [half_cols])[i + 1]
        for col in range(start, stop, 256):
            at = pl.ds(col, min(256, stop - col))
            put("vocab", at, dot_tn(top_all, grad_logits[:, at]))
        plan.run_until(1.0 * i)
        plan.post(chunks["vocab", start])
        if pair_swap is None:
            three_swap.wait()
            sent[0] = part3[core, 1] + arrived3[1]
            pair_swap = swap(sent.at[0], arrived.at[0], pair)
            plan.free[link_of(0, bits)] = plan.now + 6.0
    pair_swap.wait()
    grad_three[core] = (part3[core, 0] + arrived3[0]) + arrived[0]
    share_three = swap(grad_three.at[core], arrived.at[1], sibling)
    plan.run_until(9.0)
    share_three.wait()
    grad_three[1 - core] = arrived[1]

    copies = []
    for u in range(utterances):
        at = rows(u)
        low = grad_three[u].astype(BF16)
        branch_low[at, :] = low
        pre = (dot_nt(low, w_back[...]) * gelu_slope[at, :]).astype(BF16)
        grad_pre[at, :] = pre
        sent[utterances + u] = dot_nt(pre, w_in[...])
        copies.append(swap(sent.at[utterances + u], arrived.at[utterances + u], sibling))
    plan.run_until(13.0)
    for name, left, right in (("back", branch_low, hidden), ("in", norm_low, grad_pre)):
        for start in sorted(s for n, s in chunks if n == name):
            at = pl.ds(start, 512)
            put(name, at, dot_tn(left[...], right[:, at]))
            plan.post(chunks[name, start])
    plan.run_until(15.0)

    one_copies = []
    gain_2_total, bias_2_total = 0.0, 0.0
    for u in range(utterances):
        at = rows(u)
        copies[u].wait()
        grad_norm = sent[utterances + u] + arrived[utterances + u]
        hat, scale = normalise(stream_two[at, :])
        gain_2_total = gain_2_total + jnp.sum(grad_norm * hat, axis=0, keepdims=True)
        bias_2_total = bias_2_total + jnp.sum(grad_norm, axis=0, keepdims=True)
        two = grad_three[u] + normalise_back(grad_norm * gain_2, hat, scale)
        grad_two[at, :] = two
        low = two.astype(BF16)
        att_low[at, :] = low
        grad_mixed = dot_nt(low, w_out[...]).astype(BF16)
        for h in range(heads):
            cols = pl.ds(h * HD, HD)
            grad_head = grad_mixed[:, h * HD : (h + 1) * HD]
            prob = probs[u, h]
            grad_prob = dot_nt(grad_head, value_of(u, h))
            spare[pl.ds(u * frames, frames), pl.ds(half + h * HD, HD)] = dot_tn(
                prob.astype(BF16), grad_head
            ).astype(BF16)
            inner = jnp.sum(prob * grad_prob, axis=-1, keepdims=True)
            grad_score = (prob * (grad_prob - inner)).astype(BF16)
            grad_queries[at, cols] = (dot_nn(grad_score, key_of(u, h)) * score_scale).astype(BF16)
            spare[pl.ds(u * frames, frames), cols] = (
                dot_tn(grad_score, queries[at, cols]) * score_scale
            ).astype(BF16)
            plan.run_until(17.0 + 2.0 * (heads * u + h))
        sent[u] = dot_nt(grad_queries[at, :], w_query[...])
        one_copies.append(swap(sent.at[u], arrived.at[u], sibling))
    every = slice(None)
    put("out", every, dot_tn(att_low[...], mixed[...]))
    plan.post(chunks["out", 0])
    put("query", every, dot_tn(one_low[...], grad_queries[...]))
    plan.post(chunks["query", 0])
    plan.run_until(25.0)

    mem_copies = []
    rate_sums = [0.0, 0.0]
    for u in range(utterances):
        total = jnp.zeros((1, width), F32)
        for i in range(row_chunks):
            at = pl.ds(u * frames + i * step_rows, step_rows)
            part = dot_nt(spare[at, :], w_kv[...])
            for j in range(width // 128):
                side_of, tile = j // (width // 256), j % (width // 256)
                index = ((side_of * utterances + u) * row_chunks + i) * (width // 256) + tile
                logits[index] = part[:, j * 128 : (j + 1) * 128]
            total = total + jnp.sum(part, axis=0, keepdims=True)
        tiles = row_chunks * (width // 256)
        mem_copies.append(
            swap(
                logits.at[pl.ds(((1 - core) * utterances + u) * tiles, tiles)],
                mem_arrived.at[pl.ds(u * tiles, tiles)],
                sibling,
            )
        )
        group = jnp.zeros((1, width), jnp.int32) + rate_groups[u]
        for k in range(2):
            rate_sums[k] = rate_sums[k] + jnp.where((group == 1) == (k == 1), total, 0.0)
        plan.run_until(26.5 + 1.5 * u)
    for start in sorted(s for n, s in chunks if n == "kv"):
        at = pl.ds(start, 256)
        put("kv", at, dot_tn(mem_low[...], spare[:, at]))
        plan.post(chunks["kv", start])
        plan.run_until(29.0 + start / 256)

    gain_1_total, bias_1_total = 0.0, 0.0
    for u in range(utterances):
        at = rows(u)
        valid = own_valid[u * slots : (u + 1) * slots]
        one_copies[u].wait()
        one = grad_two[at, :] + (sent[u] + arrived[u])
        grad_two[at, :] = one
        masked = one * valid
        for k in range(kernel_rows.shape[0]):
            shift = 8 + k - kernel_rows.shape[0] // 2
            row = jnp.sum(masked * padded[u, pl.ds(shift, slots), :], axis=0, keepdims=True)
            if u == 0:
                small_sent[0, pl.ds(k, 1), :] = row
            else:
                small_sent[0, pl.ds(k, 1), :] = small_sent[0, pl.ds(k, 1), :] + row
        padded[u, pl.ds(8, slots), :] = masked
        for j in range(width // 128):
            cols = pl.ds(j * 128, 128)
            total = jnp.zeros((slots, 128), F32)
            for k in range(kernel_rows.shape[0]):
                shift = 8 - k + kernel_rows.shape[0] // 2
                total = total + kernel_rows[pl.ds(k, 1), cols] * padded[u, pl.ds(shift, slots), cols]
            stream_one[at, cols] = total * valid
        grad_norm = stream_one[at, :]
        hat, scale = normalise(stream_in[at, :])
        gain_1_total = gain_1_total + jnp.sum(grad_norm * hat, axis=0, keepdims=True)
        bias_1_total = bias_1_total + jnp.sum(grad_norm, axis=0, keepdims=True)
        zero = grad_two[at, :] + normalise_back(grad_norm * gain_1, hat, scale)
        terms[u] = blend[u * slots : (u + 1) * slots] * zero
        r.acoustic_out[at, :] = zero - terms[u]
        plan.run_until(32.0 + 2.0 * u)

    last_taps = kernel_rows.shape[0]
    small_sent[0, pl.ds(last_taps, 12 - last_taps), :] = jnp.zeros((12 - last_taps, width), F32)
    for i, row in enumerate((gain_1_total, bias_1_total, gain_2_total, bias_2_total)):
        small_sent[0, pl.ds(12 + i, 1), :] = row
    for k in range(2):
        small_sent[0, pl.ds(16 + k, 1), :] = rate_sums[k]
    small_sent[0, pl.ds(18, 6), :] = jnp.zeros((6, width), F32)
    small_peers = [peer_of[b] for b in low_bits + bits] + [sibling]

    def small_send(step):
        copy = pltpu.make_async_remote_copy(
            src_ref=small_sent.at[step],
            dst_ref=small_arrived.at[step],
            send_sem=r.small_send.at[step],
            recv_sem=r.small_recv.at[step],
            device_id=small_peers[step],
            device_id_type=MESH,
        )
        copy.start()
        return copy

    def small_take(step, copy):
        copy.wait_recv()
        if step + 1 < len(small_peers):
            small_sent[step + 1] = small_sent[step] + small_arrived[step]
        else:
            r.small_out[pl.ds(0, 16), :] = small_sent[step, pl.ds(0, 16), :]
            r.small_out[pl.ds(16, 8), :] = (
                small_sent[step, pl.ds(16, 8), :] + small_arrived[step, pl.ds(16, 8), :]
            )

    small_links = [link_of(b, bits) for b in low_bits + bits] + ["core"]
    plan.post(Chunk([(l, 24 * width * 4) for l in small_links], small_send, small_take))

    features = width // n_dp
    feature_rows = max(features, 8)
    block_rows = term_blocks.shape[1]
    turned = terms[core].T
    id_row = targets[pl.ds(core, 1), :].astype(F32)
    rest = block_rows - features - 1
    for p in range(n_dp):
        term_blocks[p, pl.ds(0, features), :] = turned[p * features : (p + 1) * features]
        term_blocks[p, pl.ds(features, 1), :] = id_row
        term_blocks[p, pl.ds(features + 1, rest), :] = jnp.zeros((rest, slots), F32)

    def term_copy(k):
        there = lax.rem(me + k, n_dp)
        return pltpu.make_async_remote_copy(
            src_ref=term_blocks.at[there],
            dst_ref=term_arrived.at[me],
            send_sem=r.term_send.at[k],
            recv_sem=r.term_recv.at[k],
            device_id={"dp": there},
            device_id_type=MESH,
        )

    def term_start(k, carry):
        term_copy(k).start()
        return carry

    def term_wait(k, carry):
        term_copy(k).wait()
        return carry

    term_arrived[me] = term_blocks[me]
    lax.fori_loop(1, n_dp, term_start, 0)
    for u in range(utterances):
        mem_copies[u].wait()
        for i in range(row_chunks):
            for j in range(width // 256):
                index = (u * row_chunks + i) * (width // 256) + j
                first_tile = (core * utterances) * row_chunks * (width // 256)
                r.memory_out[pl.ds(u * frames + i * step_rows, step_rows), pl.ds(j * 128, 128)] = (
                    logits[first_tile + index] + mem_arrived[index]
                )
    plan.run_until(45.0)
    lax.fori_loop(1, n_dp, term_wait, 0)
    per_piece = 512 // slots
    blocks_hi = table_out.shape[1] // 256
    batch = 4

    def table_piece(p, fresh):
        found = [term_arrived[p * per_piece + i] for i in range(per_piece)]
        values = jnp.concatenate([f[:feature_rows] for f in found], axis=1)
        ids = jnp.concatenate([f[features : features + 1] for f in found], axis=1).astype(jnp.int32)
        low_ids, high_ids = ids & 255, ids >> 8
        onehot_lo[...] = jnp.where(
            lax.broadcasted_iota(jnp.int32, (256, 512), 0) == low_ids, 1.0, 0.0
        ).astype(BF16)
        coarse = values.astype(BF16).astype(F32)
        both = jnp.concatenate([coarse, values - coarse], axis=0)
        for first_hi in range(0, blocks_hi, batch):
            here = range(first_hi, min(first_hi + batch, blocks_hi))
            masked = jnp.concatenate([jnp.where(high_ids == hi, both, 0.0) for hi in here], axis=0)
            product = dot_nt(masked.astype(BF16), onehot_lo[...])
            for i, hi in enumerate(here):
                top_part = product[2 * i * feature_rows : (2 * i + 1) * feature_rows]
                low_part = product[(2 * i + 1) * feature_rows : (2 * i + 2) * feature_rows]
                at = pl.ds(hi * 256, 256)
                if fresh:
                    table_out[:, at] = top_part + low_part
                else:
                    table_out[:, at] = table_out[:, at] + (top_part + low_part)

    pieces = n_dp // per_piece
    table_piece(0, True)
    if pieces <= 4:
        for p in range(1, pieces):
            plan.run_until(45.0 + 1.5 * p)
            table_piece(p, False)
    else:
        lax.fori_loop(1, pieces, lambda p, c: (table_piece(p, False), c)[1], 0)
    table_swap = swap(table_out, table_theirs, sibling)
    plan.run_until(56.0)
    table_swap.wait()
    table_out[...] = table_out[...] + table_theirs[...]
    plan.finish()


def link_of(bit, bits):
    if bit == bits[-1]:
        return bits[-2]
    return bit


def chunk_list(half_cols, width, bits, low_bits, sizes):
    own = [b for b in bits if b != 0]
    turned = own[1:] + own[:1]
    last = [] if low_bits else [0]
    listing = []
    edges = [half_cols // 128 * k // 4 * 128 for k in range(4)] + [half_cols]
    for k in range(4):
        order = turned if k == 1 else own
        listing.append(("vocab", edges[k], edges[k + 1] - edges[k], order + last))
    units = sizes.units
    for name in ("back", "in"):
        for start in range(0, units, 512):
            listing.append((name, start, 512, bits))
    half = sizes.half
    listing.append(("out", 0, half, bits))
    listing.append(("query", 0, half, bits))
    for start in range(0, 2 * half, 256):
        listing.append(("kv", start, 256, bits))
    return listing


def decoder_call(
    acoustic, memory, embedding, w_query, w_key, w_value, w_out, w_in, w_back, w_vocab, norms,
    fsmn_kernel, rate_table, token_lengths, memory_lengths, rate_groups, glance, targets, n_dp,
):
    utterances = token_lengths.shape[0]
    tokens, width = acoustic.shape
    slots = tokens // utterances
    mem_rows = memory.shape[0]
    half = w_query.shape[1]
    heads = half // HD
    frames = mem_rows // utterances
    units = w_in.shape[1]
    vocab_here = w_vocab.shape[1]
    table_rows = embedding.shape[0]
    half_cols = (vocab_here + 255) // 256 * 128
    w_turned = w_vocab.T
    main = vocab_here // 256 * 256
    mains = table_rows // 2048 * 2048
    tails = jnp.concatenate(
        [
            jnp.pad(w_turned[main:], ((0, 2 * half_cols - vocab_here), (0, 0))),
            jnp.pad(embedding[mains:], ((0, 256 - table_rows + mains), (0, 0))),
        ]
    )
    nbits = n_dp.bit_length() - 1
    steps = nbits
    while width >> steps < 8:
        steps -= 1
    low_bits, bits = list(range(nbits - steps)), list(range(nbits - steps, nbits))
    rows = width >> steps
    features = width // n_dp
    feature_rows = max(features, 8)
    block_rows = feature_rows + 8 if features >= 8 else 8
    blocks_hi = (table_rows + 255) // 256
    sizes = SimpleNamespace(units=units, half=half)
    listing = chunk_list(half_cols, width, bits, low_bits, sizes)
    most = max(len(c[3]) for c in listing)

    f32 = lambda *shape: jax.ShapeDtypeStruct(shape, F32)
    v32 = lambda *shape: pltpu.VMEM(shape, F32)
    v16 = lambda *shape: pltpu.VMEM(shape, BF16)
    dma = lambda *shape: pltpu.SemaphoreType.DMA(shape)
    inputs = dict(
        acoustic=(VMEM, acoustic),
        tails=(VMEM, tails),
        memory=(ANY, memory),
        table=(ANY, embedding),
        w_query_hbm=(ANY, w_query),
        w_key_hbm=(ANY, w_key),
        w_value_hbm=(ANY, w_value),
        w_out_hbm=(ANY, w_out),
        w_in_hbm=(ANY, w_in),
        w_back_hbm=(ANY, w_back),
        w_vocab_hbm=(ANY, w_turned),
        gain_one=(VMEM, norms[0][None]),
        bias_one=(VMEM, norms[1][None]),
        gain_two=(VMEM, norms[2][None]),
        bias_two=(VMEM, norms[3][None]),
        kernel_rows=(VMEM, fsmn_kernel),
        rate_table=(VMEM, rate_table),
        token_lengths=(SMEM, token_lengths),
        memory_lengths=(SMEM, memory_lengths),
        rate_groups=(SMEM, rate_groups),
        glance=(VMEM, glance.reshape(utterances, slots)),
        targets=(VMEM, targets.reshape(utterances, slots)),
    )
    outputs = dict(
        loss_out=f32(utterances, slots),
        acoustic_out=f32(tokens, width),
        memory_out=f32(mem_rows, width // 2),
        table_out=f32(feature_rows, blocks_hi * 256),
        small_out=f32(24, width),
        vocab_out=f32(*(() if low_bits else (2,)), rows, half_cols),
        in_out=f32(rows, units),
        back_out=f32(rows, units),
        query_out=f32(rows, half),
        out_out=f32(rows, half),
        kv_out=f32(rows, 2 * half),
    )
    shape = (2,) * steps + (rows,)
    scratch = dict(
        w_query=v16(width, half),
        w_kv=v16(width, 2 * half),
        w_out=v16(half, width),
        w_in=v16(width, units),
        w_back=v16(units, width),
        w_vocab=v16(2 * half_cols, width),
        mem_low=v16(mem_rows, width),
        kv=v16(mem_rows, 2 * half),
        spare=v16(mem_rows, 2 * half),
        padded=v32(utterances, slots + 16, width),
        stream_in=v32(tokens, width),
        stream_one=v32(tokens, width),
        stream_two=v32(tokens, width),
        stream_three=v32(utterances, slots, width),
        one_low=v16(tokens, width),
        queries=v16(tokens, half),
        probs=v32(utterances, heads, slots, frames),
        mixed=v16(tokens, half),
        norm_low=v16(tokens, width),
        hidden=v16(tokens, units),
        gelu_slope=v32(tokens, units),
        top=v16(2, tokens, width),
        logits=v32(2 * half_cols // 128, tokens, 128),
        grad_logits=v16(2 * tokens, half_cols),
        part3=v32(utterances, 2, slots, width),
        arrived3=v32(2, slots, width),
        grad_three=v32(utterances, slots, width),
        grad_two=v32(tokens, width),
        branch_low=v16(tokens, width),
        grad_pre=v16(tokens, units),
        att_low=v16(tokens, width),
        grad_queries=v16(tokens, half),
        mem_arrived=v32(mem_rows // 256 * (width // 256), 256, 128),
        meta=v32(2, 8, tokens),
        stats=v32(2, 8, 2 * tokens),
        stats_arrived=v32(4, 8, 2 * tokens),
        sent=v32(2 * utterances, slots, width),
        arrived=v32(2 * utterances, slots, width),
        gathered=v32(2, slots, width),
        small_sent=v32(nbits + 1, 24, width),
        small_arrived=v32(nbits + 1, 24, width),
        term_blocks=v32(n_dp, block_rows, slots),
        term_arrived=v32(n_dp, block_rows, slots),
        onehot_lo=v16(256, 512),
        table_theirs=v32(feature_rows, blocks_hi * 256),
        src_vocab=v32(*shape, half_cols),
        src_back=v32(*shape, units),
        src_in=v32(*shape, units),
        src_out=v32(*shape, half),
        src_query=v32(*shape, half),
        src_kv=v32(*shape, 2 * half),
        load_sem=dma(24),
        swap_send=dma(40),
        swap_recv=dma(40),
        scatter_send=dma(len(listing), most),
        scatter_recv=dma(len(listing), most),
        small_send=dma(nbits + 1),
        small_recv=dma(nbits + 1),
        term_send=dma(n_dp),
        term_recv=dma(n_dp),
    )
    landing = [
        [v32(*(2,) * (steps - 1 - s), rows, cols) for s in range(len(order))]
        for _, _, cols, order in listing
    ]
    names = list(inputs) + list(outputs) + list(scratch)
    flat = [ref for chunk in landing for ref in chunk]

    def kernel(*refs):
        named, rest = refs[: len(names)], list(refs[len(names) :])
        lands = [[rest.pop(0) for _ in chunk] for chunk in landing]
        decoder_kernel(
            names + ["landing", "units", "half"], vocab_here, half_cols, table_rows, n_dp, bits,
            low_bits, *named, lands, units, half,
        )

    out = pl.pallas_call(
        kernel,
        out_shape=list(outputs.values()),
        in_specs=[spec for spec, _ in inputs.values()],
        out_specs=[VMEM] * len(outputs),
        scratch_shapes=list(scratch.values()) + flat,
        compiler_params=pltpu.CompilerParams(
            collective_id=1, has_side_effects=True, vmem_limit_bytes=64 << 20
        ),
    )(*[value for _, value in inputs.values()])
    return SimpleNamespace(**dict(zip(outputs, out))), low_bits


def per_device(
    acoustic,
    memory,
    embedding,
    w_query,
    w_key,
    w_value,
    w_out,
    w_in,
    w_back,
    w_vocab,
    gain_one,
    bias_one,
    gain_two,
    bias_two,
    fsmn_kernel,
    rate_table,
    token_lengths,
    memory_lengths,
    rate_groups,
    glance_mask,
    targets,
):
    tok_rows, model_width = acoustic.shape
    half = w_query.shape[1]
    n_dp = lax.axis_size("dp")
    result, low_bits = decoder_call(
        acoustic, memory, embedding, w_query, w_key, w_value, w_out, w_in, w_back, w_vocab,
        (gain_one, bias_one, gain_two, bias_two), fsmn_kernel, rate_table,
        token_lengths, memory_lengths, rate_groups, glance_mask, targets, n_dp,
    )
    vocab = result.vocab_out
    summed = [result.query_out, result.kv_out, result.out_out, result.in_out, result.back_out]
    if low_bits:
        size = 1 << len(low_bits)
        groups = [list(range(g * size, (g + 1) * size)) for g in range(n_dp // size)]
        pairs = [[2 * g, 2 * g + 1] for g in range(n_dp // 2)]
        vocab = lax.all_to_all(
            vocab.reshape(2, vocab.shape[0] // 2, -1), "dp", 0, 0, axis_index_groups=pairs, tiled=True
        )
        summed = [
            lax.psum_scatter(s, "dp", scatter_dimension=0, axis_index_groups=groups, tiled=True)
            for s in summed
        ]
    grad_query, grad_kv, grad_out, grad_in, grad_back = summed
    grad_vocab = jnp.concatenate([vocab[0], vocab[1]], axis=1)[:, : w_vocab.shape[1]]
    own = model_width // n_dp
    small = result.small_out
    grad_rate = small[16:18]
    small = lax.dynamic_slice_in_dim(small, lax.axis_index("dp") * own, own, axis=1)
    return (
        result.loss_out.reshape(tok_rows),
        result.acoustic_out,
        result.memory_out,
        result.table_out[:own, : embedding.shape[0]].T,
        grad_query,
        grad_kv[:, :half],
        grad_kv[:, half:],
        grad_out.T,
        grad_in,
        grad_back.T,
        grad_vocab,
        small[12],
        small[13],
        small[14],
        small[15],
        small[: fsmn_kernel.shape[0]],
        grad_rate,
    )


def solution(mesh):
    return jax.shard_map(
        per_device,
        mesh=mesh,
        in_specs=(
            P("dp", None),
            P("dp", None),
            P(),
            P(None, "mp"),
            P(None, "mp"),
            P(None, "mp"),
            P("mp", None),
            P(None, "mp"),
            P("mp", None),
            P(None, "mp"),
            P(),
            P(),
            P(),
            P(),
            P(),
            P(),
            P("dp"),
            P("dp"),
            P("dp"),
            P("dp"),
            P("dp"),
        ),
        out_specs=(
            P("dp"),
            P("dp", None),
            P("dp", "mp"),
            P(None, "dp"),
            P("dp", "mp"),
            P("dp", "mp"),
            P("dp", "mp"),
            P("mp", "dp"),
            P("dp", "mp"),
            P("mp", "dp"),
            P("dp", "mp"),
            P("dp"),
            P("dp"),
            P("dp"),
            P("dp"),
            P(None, "dp"),
            P(),
        ),
        check_vma=False,
    )
```

time: 279 us -> 187 us (0.67)
  Pallas kernels: 200 us -> 170 us
  other arithmetic: 26.2 us -> 1.66 us
  local copies, waits for them, and re-layouts: 32.6 us -> 14.8 us
  starting transfers between devices: 12.2 us -> 0 us
  waiting for transfers between devices: 7.19 us -> 0 us
    pallas_call x2 -> x1, Pallas kernels: 200 us -> 170 us  [decoder_call(): pl.pallas_call(kernel, out_shape=list(outputs.values()), in_specs=[spec f...]
    scatter-add x1 -> x0, other arithmetic: 24.6 us -> none  [per_device(): jax.ops.segment_sum(arrived_rows, arrived_ids[:, 0].astype(jnp.int32), nu...]
    all_to_all x2 -> x0, starting transfers between devices: 12.2 us -> none  [the longest x1 8.31 us: per_device(): lax.all_to_all(id_columns, 'dp', split_axis=1, concat_axis=0, tiled=True)]
    unnamed x25 -> x23, local copies, waits for them, and re-layouts: 15.7 us -> 5.25 us
    all_to_all x2 -> x0, waiting for transfers between devices: 7.19 us -> none  [the longest x1 7.18 us: per_device(): lax.all_to_all(table_terms, 'dp', split_axis=1, concat_axis=0, tiled=True)]
    gather x1 -> x0, local copies, waits for them, and re-layouts: 6.46 us -> none  [per_device(): embedding[targets]]
  transfers between devices with their start and end apart: 2 -> 0, of which waited for: 1 -> 0; matrix products, arithmetic and copies ran while one was open for 8% -> 0% of each run, Pallas kernels for 72% -> 0%
where the time goes in v3:
time: 187 us
  Pallas kernels  170 us (91%)
  local copies, waits for them, and re-layouts  14.8 us (8%)
    pallas_call x1, Pallas kernels, decoder_call(): pl.pallas_call(kernel, out_shape=list(outputs.values()), in_specs=[spec f...  170 us
    unnamed x23, local copies, waits for them, and re-layouts  5.25 us

profile of v3, /device:TPU:0, one launch (start us, length us, event | category | flops | bytes accessed | tf_op | source)
XLA Modules:
  0.0 186.9 jit_solution(17253038162334369323)
XLA Ops:
  0.7 0.9 slice.56
  1.6 0.9 slice.43
  2.5 0.8 fusion.2.refs_1_
  3.4 169.7 %shard_map.332 = (f32[2,128]{1,0:T(2,128)}, f32[256,512]{1,0:T(8,128)}, f32[2048,256]{1,0:T(8,128)}, f32[32,8448]{1,0:T(8,128)}, f32[24,512]{1,0:T(8,128)}, /*in...) custom-call(bf16[256,512]{1,0:T(8,128)(2,1)} %refs_0_.1, ...), custom_call_target="tpu_custom_call" | custom-call | tf_op jit(solution)/shard_map/pallas_call | solution.py:1016
  173.1 0.0 copy-start.1
  173.1 1.4 dynamic-slice_bitcast_fusion
  174.5 1.3 slice.55
  175.8 1.4 constant_dynamic-slice_fusion
  177.2 1.4 fusion.3
  178.6 0.0 copy-start.7
  178.6 0.0 copy-start.2
  178.6 1.1 slice_bitcast_fusion.2
  179.7 0.0 copy-start
  179.8 0.8 pad_maximum_fusion
  180.6 0.0 copy-done.1
  180.6 1.1 slice_bitcast_fusion
  181.6 0.0 copy-done.7
  181.6 0.6 copy.45
  182.2 0.0 copy-done.2
  182.2 0.8 copy.46
  183.0 0.0 copy-done
  183.0 0.0 copy-start.6
  183.0 0.0 copy-start.5
  183.0 0.0 copy-start.4
  183.0 0.0 copy-start.3
  183.0 1.3 copy.47
  184.3 0.0 copy-done.6
  184.4 0.6 copy.48
  185.0 0.0 copy-done.5
  185.0 0.6 copy.49
  185.6 0.0 copy-done.4
  185.6 0.7 copy.50
  186.2 0.0 copy-done.3
  186.2 0.7 copy.51
Async XLA Ops:
  173.1 7.5 %copy-start.1 = (f32[32,8448]{1,0:T(8,128)S(1)}, f32[32,8448]{1,0:T(8,128)}, u32[]{:S(2)}) copy-start(f32[32,8448]{1,0:T(8,128)} %get-tuple-element.31) | copy-start | bytes 3244036
  178.6 3.0 %copy-start.7 = (f32[2,128]{1,0:T(2,128)S(1)}, f32[2,128]{1,0:T(2,128)}, u32[]{:S(2)}) copy-start(f32[2,128]{1,0:T(2,128)} %get-tuple-element.28) | copy-start | bytes 3076
  178.6 3.6 %copy-start.2 = (f32[256,512]{1,0:T(8,128)S(1)}, f32[256,512]{1,0:T(8,128)}, u32[]{:S(2)}) copy-start(f32[256,512]{1,0:T(8,128)} %get-tuple-element.65) | copy-start | bytes 1572868
  179.7 3.3 %copy-start = (f32[2048,256]{1,0:T(8,128)S(1)}, f32[2048,256]{1,0:T(8,128)}, u32[]{:S(2)}) copy-start(f32[2048,256]{1,0:T(8,128)} %get-tuple-element.66) | copy-start | bytes 6291460
  183.0 1.3 copy-start.6
  183.0 2.0 %copy-start.5 = (f32[32,256]{1,0:T(8,128)S(1)}, f32[32,256]{1,0:T(8,128)}, u32[]{:S(2)}) copy-start(f32[32,256]{1,0:T(8,128)} %get-tuple-element.34) | copy-start | bytes 98308
  183.0 2.6 %copy-start.4 = (f32[32,1024]{1,0:T(8,128)S(1)}, f32[32,1024]{1,0:T(8,128)}, u32[]{:S(2)}) copy-start(f32[32,1024]{1,0:T(8,128)} %get-tuple-element.72) | copy-start | bytes 393220
  183.0 3.2 %copy-start.3 = (f32[32,1024]{1,0:T(8,128)S(1)}, f32[32,1024]{1,0:T(8,128)}, u32[]{:S(2)}) copy-start(f32[32,1024]{1,0:T(8,128)} %get-tuple-element.36) | copy-start | bytes 393220

commit v4 on v3

--- a/solution.py
+++ b/solution.py
@@ -1,3 +1,4 @@
+from functools import partial
 import math
 from types import SimpleNamespace
 
@@ -64,7 +65,7 @@
 class Planner:
     RATE = 0.0425e6
     HOP = 1.5
-    BACKLOG = 12.0
+    BACKLOG = math.inf
 
     def __init__(self):
         self.now = 0.0
@@ -139,7 +140,7 @@
     *refs,
 ):
     r = SimpleNamespace(**dict(zip(names, refs)))
-    acoustic, memory, table, tails = r.acoustic, r.memory, r.table, r.tails
+    acoustic, memory, table = r.acoustic, r.memory, r.table
     targets, glance = r.targets, r.glance
     gain_1, bias_1 = r.gain_one[...], r.bias_one[...]
     gain_2, bias_2 = r.gain_two[...], r.bias_two[...]
@@ -214,12 +215,12 @@
         return load(table.at[at, :], spare.at[pl.ds(k % 2 * block, block), :])
 
     table_loads = [load_table(0), load_table(1)]
-    tail_rows = tails.shape[0] - 256
-    main = w_vocab.shape[0] - tail_rows
-    load_vocab = [
-        load(r.w_vocab_hbm.at[pl.ds(0, main), :], w_vocab.at[pl.ds(0, main), :]),
-        load(tails.at[pl.ds(0, tail_rows), :], w_vocab.at[pl.ds(main, tail_rows), :]),
-    ]
+    main = vocab_here // 256 * 256
+    load_vocab = load(r.w_vocab_hbm.at[pl.ds(0, main), :], w_vocab.at[pl.ds(0, main), :])
+    w_vocab[pl.ds(main, w_vocab.shape[0] - main), :] = jnp.zeros((w_vocab.shape[0] - main, width), BF16)
+    w_vocab[pl.ds(main, vocab_here - main), :] = r.w_tail[...]
+    r.table_rest[...] = jnp.zeros(r.table_rest.shape, BF16)
+    r.table_rest[pl.ds(0, table_rows - mains), :] = r.table_tail[...]
 
     swaps = []
 
@@ -306,7 +307,7 @@
             table_loads.append(load_table(k + 2))
 
     def look_up_rest():
-        part = look_up(mains, 256, core == 0, tails[pl.ds(tail_rows, 256), :])
+        part = look_up(mains, r.table_rest.shape[0], core == 0, r.table_rest[...])
         for u in range(utterances):
             part3[0, u] = part3[0, u] + part[u * slots : (u + 1) * slots]
 
@@ -429,8 +430,7 @@
 
     forward(False, beside_one, beside_two)
     table_swap = swap(part3.at[0], arrived3, sibling)
-    for copy in load_vocab:
-        copy.wait()
+    load_vocab.wait()
     first = vocab_stats(0, local_targets(own_target), 0, w_vocab.shape[0] // 256, 0, 0)
     stats[0, :, pl.ds(0, tokens)] = to_rows(first)
     first_swap = swap(stats.at[0, :, pl.ds(0, tokens)], stats_arrived.at[0, :, pl.ds(0, tokens)], sibling)
@@ -837,13 +837,11 @@
 
 def chunk_list(half_cols, width, bits, low_bits, sizes):
     own = [b for b in bits if b != 0]
-    turned = own[1:] + own[:1]
     last = [] if low_bits else [0]
     listing = []
     edges = [half_cols // 128 * k // 4 * 128 for k in range(4)] + [half_cols]
     for k in range(4):
-        order = turned if k == 1 else own
-        listing.append(("vocab", edges[k], edges[k + 1] - edges[k], order + last))
+        listing.append(("vocab", edges[k], edges[k + 1] - edges[k], own + last))
     units = sizes.units
     for name in ("back", "in"):
         for start in range(0, units, 512):
@@ -874,12 +872,6 @@
     w_turned = w_vocab.T
     main = vocab_here // 256 * 256
     mains = table_rows // 2048 * 2048
-    tails = jnp.concatenate(
-        [
-            jnp.pad(w_turned[main:], ((0, 2 * half_cols - vocab_here), (0, 0))),
-            jnp.pad(embedding[mains:], ((0, 256 - table_rows + mains), (0, 0))),
-        ]
-    )
     nbits = n_dp.bit_length() - 1
     steps = nbits
     while width >> steps < 8:
@@ -900,7 +892,8 @@
     dma = lambda *shape: pltpu.SemaphoreType.DMA(shape)
     inputs = dict(
         acoustic=(VMEM, acoustic),
-        tails=(VMEM, tails),
+        w_tail=(VMEM, w_turned[main:]),
+        table_tail=(VMEM, embedding[mains:]),
         memory=(ANY, memory),
         table=(ANY, embedding),
         w_query_hbm=(ANY, w_query),
@@ -981,6 +974,7 @@
         term_blocks=v32(n_dp, block_rows, slots),
         term_arrived=v32(n_dp, block_rows, slots),
         onehot_lo=v16(256, 512),
+        table_rest=v16((table_rows - mains + 127) // 128 * 128, width),
         table_theirs=v32(feature_rows, blocks_hi * 256),
         src_vocab=v32(*shape, half_cols),
         src_back=v32(*shape, units),
@@ -1024,6 +1018,44 @@
         ),
     )(*[value for _, value in inputs.values()])
     return SimpleNamespace(**dict(zip(outputs, out))), low_bits
+
+
+def deliver_kernel(n_dp, *refs):
+    loss, small, table, vocab, kv, query, out, in_, back, acoustic, memory = refs[:11]
+    (
+        loss_to, gain_one_to, bias_one_to, gain_two_to, bias_two_to, taps_to, rate_to,
+        table_to, vocab_to, key_to, value_to, query_to, out_to, in_to, back_to, acoustic_to, memory_to,
+    ) = refs[11:28]
+    sem = refs[28]
+    copies = []
+    for source, target in (
+        (memory, memory_to), (acoustic, acoustic_to), (in_, in_to), (back, back_to),
+        (query, query_to), (out, out_to),
+    ):
+        copies.append(pltpu.make_async_copy(source, target, sem.at[len(copies)]))
+        copies[-1].start()
+    slots = loss.shape[1]
+    for u in range(loss.shape[0]):
+        loss_to[:, pl.ds(u * slots, slots)] = loss[pl.ds(u, 1), :]
+    me = lax.axis_index("dp")
+    own = small.shape[1] // n_dp
+    mine = jnp.zeros((16, own), F32)
+    for p in range(n_dp):
+        mine = jnp.where(me == p, small[pl.ds(0, 16), p * own : (p + 1) * own], mine)
+    taps_to[...] = mine[: taps_to.shape[0]]
+    for i, target in enumerate((gain_one_to, bias_one_to, gain_two_to, bias_two_to)):
+        target[...] = mine[12 + i : 13 + i]
+    rate_to[...] = small[pl.ds(16, 2), :]
+    table_to[...] = table[pl.ds(0, table_to.shape[0]), :][:, : table_to.shape[1]]
+    half_cols = vocab.shape[2]
+    vocab_to[:, pl.ds(0, half_cols)] = vocab[0]
+    rest = vocab_to.shape[1] - half_cols
+    vocab_to[:, pl.ds(half_cols, rest)] = vocab[1][:, :rest]
+    half = key_to.shape[1]
+    key_to[...] = kv[:, pl.ds(0, half)]
+    value_to[...] = kv[:, pl.ds(half, half)]
+    for copy in copies:
+        copy.wait()
 
 
 def per_device(
@@ -1071,28 +1103,51 @@
             for s in summed
         ]
     grad_query, grad_kv, grad_out, grad_in, grad_back = summed
-    grad_vocab = jnp.concatenate([vocab[0], vocab[1]], axis=1)[:, : w_vocab.shape[1]]
     own = model_width // n_dp
-    small = result.small_out
-    grad_rate = small[16:18]
-    small = lax.dynamic_slice_in_dim(small, lax.axis_index("dp") * own, own, axis=1)
+    f32 = lambda *shape: jax.ShapeDtypeStruct(shape, F32)
+    like = lambda x: jax.ShapeDtypeStruct(x.shape, F32)
+    (
+        token_loss, gain_1, bias_1, gain_2, bias_2, grad_taps, grad_rate, grad_table, grad_vocab,
+        grad_key, grad_value, grad_query, grad_out, grad_in, grad_back, grad_acoustic, grad_memory,
+    ) = pl.pallas_call(
+        partial(deliver_kernel, n_dp),
+        out_shape=[
+            f32(1, tok_rows),
+            *[f32(1, own)] * 4,
+            f32(fsmn_kernel.shape[0], own),
+            f32(2, model_width),
+            f32(own, embedding.shape[0]),
+            f32(own, w_vocab.shape[1]),
+            *[f32(own, half)] * 2,
+            *[like(x) for x in (grad_query, grad_out, grad_in, grad_back)],
+            like(result.acoustic_out),
+            like(result.memory_out),
+        ],
+        in_specs=[VMEM] * 5 + [ANY] * 6,
+        out_specs=[VMEM] * 11 + [ANY] * 6,
+        scratch_shapes=[pltpu.SemaphoreType.DMA((6,))],
+        compiler_params=pltpu.CompilerParams(vmem_limit_bytes=32 << 20),
+    )(
+        result.loss_out, result.small_out, result.table_out, vocab, grad_kv, grad_query, grad_out,
+        grad_in, grad_back, result.acoustic_out, result.memory_out,
+    )
     return (
-        result.loss_out.reshape(tok_rows),
-        result.acoustic_out,
-        result.memory_out,
-        result.table_out[:own, : embedding.shape[0]].T,
+        token_loss.reshape(tok_rows),
+        grad_acoustic,
+        grad_memory,
+        grad_table.T,
         grad_query,
-        grad_kv[:, :half],
-        grad_kv[:, half:],
+        grad_key,
+        grad_value,
         grad_out.T,
         grad_in,
         grad_back.T,
         grad_vocab,
-        small[12],
-        small[13],
-        small[14],
-        small[15],
-        small[: fsmn_kernel.shape[0]],
+        gain_1.reshape(own),
+        bias_1.reshape(own),
+        gain_2.reshape(own),
+        bias_2.reshape(own),
+        grad_taps,
         grad_rate,
     )
 

time: 187 us -> 221 us (1.18)
  Pallas kernels: 170 us -> 206 us
    pallas_call x1, Pallas kernels: 170 us -> 203 us  [decoder_call(): pl.pallas_call(kernel, out_shape=list(outputs.values()), in_specs=[spec f...]
    unnamed x23 -> x22, local copies, waits for them, and re-layouts: 5.25 us -> 10.5 us
    slice x3 -> x0, local copies, waits for them, and re-layouts: 4.08 us -> none  [the longest x1 1.4 us: per_device(): grad_kv[:, half:]]
    pallas_call x0 -> x1, Pallas kernels: none -> 2.83 us  [per_device(): pl.pallas_call(partial(deliver_kernel, n_dp), out_shape=[f32(1, tok_rows)...]
    squeeze x2 -> x0, local copies, waits for them, and re-layouts: 2.57 us -> none  [the longest x1 1.44 us: per_device(): small[15]]
where the time goes in v4:
time: 221 us; the launch traced here: 220 us
  Pallas kernels  206 us (93%)
  local copies, waits for them, and re-layouts  13.7 us (6%)
    pallas_call x1, Pallas kernels, decoder_call(): pl.pallas_call(kernel, out_shape=list(outputs.values()), in_specs=[spec f...  203 us
    unnamed x22, local copies, waits for them, and re-layouts  10.5 us

profile of v4, /device:TPU:0, one launch (start us, length us, event | category | flops | bytes accessed | tf_op | source)
XLA Modules:
  0.0 220.4 jit_solution(15817683634980429632)
XLA Ops:
  0.7 1.6 slice.8.refs_1_
  2.2 1.6 slice.7.refs_2_
  3.8 203.0 %shard_map.332 = (f32[2,128]{1,0:T(2,128)}, f32[256,512]{1,0:T(8,128)}, f32[2048,256]{1,0:T(8,128)}, f32[32,8448]{1,0:T(8,128)}, f32[24,512]{1,0:T(8,128)}, /*in...) custom-call(bf16[256,512]{1,0:T(8,128)(2,1)} %refs_0_.1, ...), custom_call_target="tpu_custom_call" | custom-call | tf_op jit(solution)/shard_map/pallas_call | solution.py:1010
  206.8 0.0 copy-start
  206.8 1.6 copy-done
  208.4 0.0 copy-start.1
  208.4 1.2 copy-done.1
  209.7 0.0 copy-start.2
  209.7 1.1 copy-done.2
  210.7 0.0 copy-start.3
  210.7 1.0 copy-done.3
  211.8 0.0 copy-start.4
  211.8 0.9 copy-done.4
  212.7 0.0 copy-start.5
  212.7 0.9 copy-done.5
  213.6 0.0 copy-start.6
  213.6 0.8 copy-done.6
  214.4 0.0 copy-start.7
  214.4 0.8 copy-done.7
  215.2 0.0 copy-start.8
  215.2 0.8 copy-done.8
  216.0 0.0 copy-start.9
  216.0 0.8 copy-done.9
  216.7 0.0 copy-start.10
  216.7 0.7 copy-done.10
  217.4 2.8 %shard_map.333 = (f32[1,256]{1,0:T(1,128)}, f32[1,32]{1,0:T(1,128)}, f32[1,32]{1,0:T(1,128)}, f32[1,32]{1,0:T(1,128)}, f32[1,32]{1,0:T(1,128)}, /*index=5*/f32[1...) custom-call(f32[2,128]{1,0:T(2,128)S(1)} %copy-done.10, ...), custom_call_target="tpu_custom_call" | custom-call | tf_op jit(solution)/shard_map/pallas_call | solution.py:1112
Async XLA Ops:
  206.8 1.6 copy-start
  208.4 1.2 copy-start.1
  209.7 1.1 copy-start.2
  210.7 1.0 copy-start.3
  211.8 0.9 copy-start.4
  212.7 0.9 copy-start.5
  213.6 0.8 copy-start.6
  214.4 0.8 copy-start.7
  215.2 0.8 copy-start.8
  216.0 0.8 copy-start.9
  216.7 0.7 copy-start.10

commit v5 on v4

--- a/solution.py
+++ b/solution.py
@@ -63,9 +63,9 @@
 
 
 class Planner:
-    RATE = 0.0425e6
+    RATE = 0.045e6
     HOP = 1.5
-    BACKLOG = math.inf
+    BACKLOG = 6.0
 
     def __init__(self):
         self.now = 0.0
@@ -113,6 +113,8 @@
             item.take(step, copy)
             if step + 1 < len(item.steps):
                 self.launch(item, step + 1)
+            elif item.follow is not None:
+                self.launch(item.follow, 0)
             self.release()
         if time != math.inf:
             self.now = max(self.now, time)
@@ -126,13 +128,26 @@
 
 class Chunk:
     def __init__(self, steps, send, take):
-        self.steps, self.send, self.take = steps, send, take
+        self.steps, self.send, self.take, self.follow = steps, send, take, None
+
+
+class Several:
+    def __init__(self, copies):
+        self.copies = copies
+
+    def wait_recv(self):
+        for copy in self.copies:
+            copy.wait_recv()
+
+    def wait_send(self):
+        for copy in self.copies:
+            copy.wait_send()
 
 
 def decoder_kernel(
     names,
     vocab_here,
-    half_cols,
+    part_cols,
     table_rows,
     n_dp,
     bits,
@@ -151,14 +166,15 @@
     stream_in, stream_one, stream_two, stream_three = r.stream_in, r.stream_one, r.stream_two, r.stream_three
     one_low, queries, probs, mixed = r.one_low, r.queries, r.probs, r.mixed
     norm_low, hidden, gelu_slope, top = r.norm_low, r.hidden, r.gelu_slope, r.top
-    logits, grad_logits, part3, arrived3 = r.logits, r.grad_logits, r.part3, r.arrived3
+    logits, grad_logits, grad_others = r.logits, r.grad_logits, r.grad_others
+    taken_mine, taken_theirs = r.taken_mine, r.taken_theirs
     grad_three, grad_two, branch_low = r.grad_three, r.grad_two, r.branch_low
     grad_pre, att_low, grad_queries = r.grad_pre, r.att_low, r.grad_queries
     mem_arrived, meta, stats, stats_arrived = r.mem_arrived, r.meta, r.stats, r.stats_arrived
     sent, arrived, gathered = r.sent, r.arrived, r.gathered
     small_sent, small_arrived = r.small_sent, r.small_arrived
     terms, term_blocks, term_arrived = grad_three, r.term_blocks, r.term_arrived
-    onehot_lo, table_theirs, table_out = r.onehot_lo, r.table_theirs, r.table_out
+    onehot_lo, table_theirs, table_out = r.onehot_lo, r.table_theirs, r.table_mine
     swap_send, swap_recv, load_sem = r.swap_send, r.swap_recv, r.load_sem
 
     utterances, slots = targets.shape
@@ -168,10 +184,10 @@
     heads = half // HD
     tokens = utterances * slots
     me, core = lax.axis_index("dp"), lax.axis_index("mp")
-    side = lax.rem(me, 2)
     sibling = {"mp": 1 - core}
-    pair = {"dp": me + 1 - 2 * side}
-    cross = {"dp": me + 1 - 2 * side, "mp": 1 - core}
+    quarter = lax.rem(me, 4)
+    flips = [1 - 2 * lax.rem(me, 2), 2 - 4 * lax.rem(me // 2, 2)]
+    mate = [me + flips[0] * (j % 2) + flips[1] * (j // 2) for j in range(4)]
     bit_of = {b: lax.rem(me // (1 << b), 2) for b in low_bits + bits}
     peer_of = {b: {"dp": me + (1 - 2 * bit_of[b]) * (1 << b)} for b in low_bits + bits}
     score_scale = 1.0 / math.sqrt(HD)
@@ -201,8 +217,7 @@
         return carry
 
     lax.fori_loop(1, n_dp, greet, 0)
-    for device in (sibling, cross):
-        pl.semaphore_signal(barrier, inc=1, device_id=device, device_id_type=MESH)
+    pl.semaphore_signal(barrier, inc=1, device_id=sibling, device_id_type=MESH)
 
     load_in = load(r.w_in_hbm, w_in)
     load_back = load(r.w_back_hbm, w_back)
@@ -276,8 +291,7 @@
         padded[u, pl.ds(0, 8), :] = edge
         padded[u, pl.ds(8 + slots, 8), :] = edge
 
-    pl.semaphore_wait(barrier, n_dp + 1)
-    meta_swap = swap(meta.at[0], meta.at[1], pair)
+    pl.semaphore_wait(barrier, n_dp)
     load_query.wait()
     load_out.wait()
 
@@ -302,14 +316,14 @@
         )
         for u in range(utterances):
             piece = part[u * slots : (u + 1) * slots]
-            part3[0, u] = piece if k == 0 else part3[0, u] + piece
+            taken_mine[u] = piece if k == 0 else taken_mine[u] + piece
         if k + 2 < per_core:
             table_loads.append(load_table(k + 2))
 
     def look_up_rest():
         part = look_up(mains, r.table_rest.shape[0], core == 0, r.table_rest[...])
         for u in range(utterances):
-            part3[0, u] = part3[0, u] + part[u * slots : (u + 1) * slots]
+            taken_mine[u] = taken_mine[u] + part[u * slots : (u + 1) * slots]
 
     def local_targets(target_column):
         local = target_column.astype(jnp.int32) - core * vocab_here
@@ -321,26 +335,22 @@
         logits[first] = tile
         return jnp.maximum(top_m, tile), picked + jnp.where(ids == target, tile, 0.0)
 
-    def vocab_stats(g, target, base, wide, narrow, first):
+    def vocab_stats(target):
         start = (jnp.full((tokens, 128), NEG, F32), jnp.zeros((tokens, 128), F32))
 
         def step(j, carry):
-            col = pl.multiple_of(base + j * 256, 128)
-            product = dot_nt(top[g], w_vocab[pl.ds(col, 256), :])
-            carry = vocab_tile(product[:, :128], first + 2 * j, col, target, *carry)
-            return vocab_tile(product[:, 128:], first + 2 * j + 1, col + 128, target, *carry)
-
-        top_m, picked = lax.fori_loop(0, wide, step, start)
-        if narrow:
-            col = pl.multiple_of(base + wide * 256, 128)
-            product = dot_nt(top[g], w_vocab[pl.ds(col, 128), :])
-            top_m, picked = vocab_tile(product, first + 2 * wide, col, target, top_m, picked)
+            col = pl.multiple_of(j * 256, 256)
+            product = dot_nt(top[0], w_vocab[pl.ds(col, 256), :])
+            carry = vocab_tile(product[:, :128], 2 * j, col, target, *carry)
+            return vocab_tile(product[:, 128:], 2 * j + 1, col + 128, target, *carry)
+
+        top_m, picked = lax.fori_loop(0, w_vocab.shape[0] // 256, step, start)
         top_row = jnp.max(top_m, axis=1, keepdims=True)
 
         def add(j, total):
-            return total + jnp.exp(logits[first + j] - top_row)
-
-        total = lax.fori_loop(0, 2 * wide + narrow, add, jnp.zeros((tokens, 128), F32))
+            return total + jnp.exp(logits[j] - top_row)
+
+        total = lax.fori_loop(0, w_vocab.shape[0] // 128, add, jnp.zeros((tokens, 128), F32))
         return (
             top_row,
             jnp.sum(total, axis=1, keepdims=True),
@@ -380,7 +390,7 @@
                 scores = dot_nt(queries[at, cols], key_of(u, h)) * score_scale
                 scores = jnp.where(frame_ok, scores, NEG)
                 raised = jnp.exp(scores - jnp.max(scores, axis=-1, keepdims=True))
-                prob = raised / jnp.sum(raised, axis=-1, keepdims=True)
+                prob = raised * (1.0 / jnp.sum(raised, axis=-1, keepdims=True))
                 if second:
                     probs[u, h] = prob
                 mixed[at, cols] = dot_nn(prob.astype(BF16), value_of(u, h)).astype(BF16)
@@ -429,78 +439,63 @@
         look_up_rest()
 
     forward(False, beside_one, beside_two)
-    table_swap = swap(part3.at[0], arrived3, sibling)
+    table_swap = swap(taken_mine, taken_theirs, sibling)
     load_vocab.wait()
-    first = vocab_stats(0, local_targets(own_target), 0, w_vocab.shape[0] // 256, 0, 0)
-    stats[0, :, pl.ds(0, tokens)] = to_rows(first)
-    first_swap = swap(stats.at[0, :, pl.ds(0, tokens)], stats_arrived.at[0, :, pl.ds(0, tokens)], sibling)
+    own_local = local_targets(own_target)
+    stats[0] = to_rows(vocab_stats(own_local))
+    first_swap = swap(stats.at[0], stats_arrived.at[0], sibling)
     table_swap.wait()
     first_swap.wait()
-    log_total, picked = join([stats[0, :, :tokens], stats_arrived[0, :, :tokens]])
+    log_total, picked = join([stats[0], stats_arrived[0]])
     first_loss = (log_total - picked) * meta[0, 1:2, :]
     blend_row = meta[0, 2:3, :] * meta[0, 1:2, :] / (1.0 + jnp.exp(math.log(V) - first_loss))
     blend = to_columns(jnp.concatenate([blend_row] * 8, axis=0))[:, 0:1]
     for u in range(utterances):
         at = rows(u)
         wide_acoustic = acoustic[at, :].astype(F32)
-        taken = part3[0, u] + arrived3[u]
+        taken = taken_mine[u] + taken_theirs[u]
         stream_in[at, :] = wide_acoustic + blend[u * slots : (u + 1) * slots] * (taken - wide_acoustic)
 
     forward(True)
-    token_swap = swap(stream_three.at[core], gathered.at[0], pair)
-    base = side * half_cols
-    wide, narrow = half_cols // 256, half_cols % 256 // 128
-    per_group = 2 * wide + narrow
-    meta_swap.wait()
-    pair_columns = to_columns(meta[1])
-    group_target = [local_targets(own_target), local_targets(pair_columns[:, 0:1])]
-    group_valid = [own_valid, pair_columns[:, 1:2]]
-    own_stats = vocab_stats(0, group_target[0], base, wide, narrow, 0)
-    stats[1, :, pl.ds(0, tokens)] = to_rows(own_stats)
-    token_swap.wait()
-    share_swap = swap(gathered.at[0], gathered.at[1], sibling)
-    at_core = pl.ds(pl.multiple_of(core * slots, slots), slots)
-    at_other = pl.ds(pl.multiple_of((1 - core) * slots, slots), slots)
-    top[1, at_core, :] = gathered[0].astype(BF16)
-    share_swap.wait()
-    top[1, at_other, :] = gathered[1].astype(BF16)
-    pair_stats = vocab_stats(1, group_target[1], base, wide, narrow, per_group)
-    stats[1, :, pl.ds(tokens, tokens)] = to_rows(pair_stats)
-    stat_swaps = [
-        swap(stats.at[1], stats_arrived.at[1], sibling),
-        swap(stats.at[1], stats_arrived.at[2], pair),
-        swap(stats.at[1], stats_arrived.at[3], cross),
+    token_swaps = [
+        swap(stream_three.at[core], gathered.at[j - 1, 0], {"dp": mate[j]}) for j in range(1, 4)
     ]
-    for copy in stat_swaps:
-        copy.wait()
-
-    def group_blocks(g):
-        mine, theirs = pl.ds(g * tokens, tokens), pl.ds((1 - g) * tokens, tokens)
-        return [
-            stats[1, :, mine],
-            stats_arrived[1, :, mine],
-            stats_arrived[2, :, theirs],
-            stats_arrived[3, :, theirs],
-        ]
-
-    log_totals = []
-    for g in range(2):
-        log_total, picked = join(group_blocks(g))
-        log_totals.append(to_columns(jnp.concatenate([log_total] * 8, axis=0))[:, 0:1])
-        if g == 0:
-            loss = (log_total - picked) * meta[0, 1:2, :]
-            for u in range(utterances):
-                r.loss_out[pl.ds(u, 1), :] = loss[:, u * slots : (u + 1) * slots]
+    stats[1] = to_rows(vocab_stats(own_local))
+    stat_swap = swap(stats.at[1], stats_arrived.at[1], sibling)
+    stat_swap.wait()
+    log_total, picked = join([stats[1], stats_arrived[1]])
+    loss = (log_total - picked) * meta[0, 1:2, :]
+    for u in range(utterances):
+        r.loss_out[pl.ds(u, 1), :] = loss[:, u * slots : (u + 1) * slots]
+    meta[0] = jnp.where(
+        lax.broadcasted_iota(jnp.int32, (8, tokens), 0) == 3, log_total, meta[0]
+    )
+    meta_swaps = [swap(meta.at[0], meta.at[j], {"dp": mate[j]}) for j in range(1, 4)]
+
+    log_column = to_columns(meta[0])[:, 3:4]
+
+    def slope(j, carry):
+        col = pl.multiple_of(j * 128, 128)
+        ids = col + lax.broadcasted_iota(jnp.int32, (1, 128), 1)
+        onehot = jnp.where(ids == own_local, 1.0, 0.0)
+        grad = (jnp.exp(logits[j] - log_column) - onehot) * own_valid
+        grad_logits[:, pl.ds(col, 128)] = grad.astype(BF16)
+        return carry
+
+    lax.fori_loop(0, w_vocab.shape[0] // 128, slope, 0)
+    three_copies = []
+    for u in range(utterances):
+        sent[u] = dot_nn(grad_logits[rows(u), :], w_vocab[...])
+        three_copies.append(swap(sent.at[u], arrived.at[u], sibling))
 
     plan = Planner()
     steps_all = len(bits)
-    trade = not low_bits
     scatter_send, scatter_recv = r.scatter_send, r.scatter_recv
 
     def make_chunk(index):
-        name, start, cols, order = chunk_list(half_cols, width, bits, low_bits, r)[index]
+        name, start, cols, order = chunk_list(part_cols, width, bits, low_bits, r)[index]
         source, landing = getattr(r, "src_" + name), r.landing[index]
-        out = getattr(r, name + "_out")
+        out = r.vocab_sum if name == "vocab" and not low_bits else getattr(r, name + "_out")
         rows_here = source.shape[-2]
 
         def pick(step, which):
@@ -529,14 +524,12 @@
             ref, where = pick(step, bit_of[order[step]])
             got = landing[step]
             at = pl.ds(start, cols)
-            last = step == len(order) - 1
-            if last and name == "vocab" and trade:
-                out[bit_of[0], :, at] = ref[where]
-                out[1 - bit_of[0], :, at] = got[...]
-            elif last:
+            if step < len(order) - 1:
+                got[...] = got[...] + ref[where]
+            elif name == "vocab":
+                out[..., at] = got[...] + ref[where]
+            else:
                 out[:, at] = got[...] + ref[where]
-            else:
-                got[...] = got[...] + ref[where]
 
         steps = [
             (link_of(b, bits), rows_here * cols * 4 * 2 ** (steps_all - 1 - s))
@@ -544,71 +537,106 @@
         ]
         return Chunk(steps, send, take)
 
+    def make_trade(start, cols):
+        summed, traded = r.vocab_sum, r.vocab_traded
+        at = pl.ds(start, cols)
+
+        def send(step):
+            copies = []
+            for j in range(1, 4):
+                to = lax.rem(mate[j], 4)
+                copies.append(
+                    pltpu.make_async_remote_copy(
+                        src_ref=summed.at[to // 2, lax.rem(to, 2), :, at],
+                        dst_ref=traded.at[j - 1, :, at],
+                        send_sem=r.trade_send.at[start // 128, j - 1],
+                        recv_sem=r.trade_recv.at[start // 128, j - 1],
+                        device_id={"dp": mate[j]},
+                        device_id_type=MESH,
+                    )
+                )
+                copies[-1].start()
+            return Several(copies)
+
+        def take(step, copies):
+            copies.wait_recv()
+            for j in range(1, 4):
+                r.vocab_out[lax.rem(mate[j], 4), :, at] = traded[j - 1, :, at]
+            r.vocab_out[quarter, :, at] = summed[quarter // 2, lax.rem(quarter, 2), :, at]
+
+        return Chunk([(0, 2 * r.src_vocab.shape[-2] * cols * 4)], send, take)
+
     chunks = {}
-    for index, (name, start, _, _) in enumerate(chunk_list(half_cols, width, bits, low_bits, r)):
+    for index, (name, start, cols, _) in enumerate(chunk_list(part_cols, width, bits, low_bits, r)):
         chunks[name, start] = make_chunk(index)
+        if name == "vocab" and not low_bits:
+            chunks[name, start].follow = make_trade(start, cols)
 
     def put(name, at, product):
         source = getattr(r, "src_" + name)
         source[..., at] = product.reshape(source.shape[:-1] + (product.shape[1],))
 
-    for g in (1, 0):
-        log_column, valid, target = log_totals[g], group_valid[g], group_target[g]
-
-        def slope(j, carry):
-            col = pl.multiple_of(j * 128, 128)
-            ids = base + col + lax.broadcasted_iota(jnp.int32, (1, 128), 1)
-            onehot = jnp.where(ids == target, 1.0, 0.0)
-            grad = (jnp.exp(logits[g * per_group + j] - log_column) - onehot) * valid
-            grad_logits[pl.ds(g * tokens, tokens), pl.ds(col, 128)] = grad.astype(BF16)
-            return carry
-
-        lax.fori_loop(0, per_group, slope, 0)
-        part = dot_nn(
-            grad_logits[pl.ds(g * tokens, tokens), :],
-            w_vocab[pl.ds(pl.multiple_of(base, 128), half_cols), :],
-        )
-        for u in range(utterances):
-            part3[u, g] = part[u * slots : (u + 1) * slots]
-    three_swap = swap(part3.at[1 - core], arrived3, sibling)
-    top_all = jnp.concatenate([top[0], top[1]], axis=0)
-    vocab_starts = sorted(start for name, start in chunks if name == "vocab")
-    pair_swap = None
-    for i, start in enumerate(vocab_starts):
-        stop = (vocab_starts + [half_cols])[i + 1]
-        for col in range(start, stop, 256):
-            at = pl.ds(col, min(256, stop - col))
-            put("vocab", at, dot_tn(top_all, grad_logits[:, at]))
-        plan.run_until(1.0 * i)
-        plan.post(chunks["vocab", start])
-        if pair_swap is None:
-            three_swap.wait()
-            sent[0] = part3[core, 1] + arrived3[1]
-            pair_swap = swap(sent.at[0], arrived.at[0], pair)
-            plan.free[link_of(0, bits)] = plan.now + 6.0
-    pair_swap.wait()
-    grad_three[core] = (part3[core, 0] + arrived3[0]) + arrived[0]
-    share_three = swap(grad_three.at[core], arrived.at[1], sibling)
-    plan.run_until(9.0)
-    share_three.wait()
-    grad_three[1 - core] = arrived[1]
-
     copies = []
     for u in range(utterances):
         at = rows(u)
-        low = grad_three[u].astype(BF16)
+        three_copies[u].wait()
+        three = sent[u] + arrived[u]
+        grad_three[u] = three
+        low = three.astype(BF16)
         branch_low[at, :] = low
         pre = (dot_nt(low, w_back[...]) * gelu_slope[at, :]).astype(BF16)
         grad_pre[at, :] = pre
         sent[utterances + u] = dot_nt(pre, w_in[...])
         copies.append(swap(sent.at[utterances + u], arrived.at[utterances + u], sibling))
-    plan.run_until(13.0)
+    plan.run_until(4.0)
     for name, left, right in (("back", branch_low, hidden), ("in", norm_low, grad_pre)):
+        left_turned = left[...].T
         for start in sorted(s for n, s in chunks if n == name):
             at = pl.ds(start, 512)
-            put(name, at, dot_tn(left[...], right[:, at]))
+            put(name, at, dot_nn(left_turned, right[:, at]))
+            plan.run_until(plan.now + 0.5)
             plan.post(chunks[name, start])
-    plan.run_until(15.0)
+
+    at_core = pl.ds(pl.multiple_of(core * slots, slots), slots)
+    at_other = pl.ds(pl.multiple_of((1 - core) * slots, slots), slots)
+    share_swaps = []
+    for j in range(1, 4):
+        token_swaps[j - 1].wait()
+        share_swaps.append(swap(gathered.at[j - 1, 0], gathered.at[j - 1, 1], sibling))
+        top[j, at_core, :] = gathered[j - 1, 0].astype(BF16)
+    base = pl.multiple_of(
+        quarter * part_cols - quarter // 3 * (4 * part_cols - w_vocab.shape[0]), 128
+    )
+    pieces = [(c, 256) for c in range(0, part_cols // 256 * 256, 256)]
+    if part_cols % 256:
+        pieces.append((part_cols // 256 * 256, part_cols % 256))
+    for j in range(1, 4):
+        meta_swaps[j - 1].wait()
+        columns = to_columns(meta[j])
+        target, valid, log_total = local_targets(columns[:, 0:1]), columns[:, 1:2], columns[:, 3:4]
+        share_swaps[j - 1].wait()
+        top[j, at_other, :] = gathered[j - 1, 1].astype(BF16)
+        for col, cols in pieces:
+            ids = base + col + lax.broadcasted_iota(jnp.int32, (1, cols), 1)
+            tile = dot_nt(top[j], w_vocab[pl.ds(base + col, cols), :])
+            tile = jnp.where(ids < vocab_here, tile, NEG)
+            grad = (jnp.exp(tile - log_total) - jnp.where(ids == target, 1.0, 0.0)) * valid
+            grad_others[pl.ds((j - 1) * tokens, tokens), pl.ds(col, cols)] = grad.astype(BF16)
+        plan.run_until(plan.now + 0.8)
+    top_turned = r.top_turned
+    for j in range(4):
+        top_turned[:, pl.ds(j * tokens, tokens)] = top[j].T
+    starts = sorted(start for name, start in chunks if name == "vocab")
+    for start, stop in zip(starts, starts[1:] + [part_cols]):
+        for col in range(start, stop, 256):
+            cols = min(256, stop - col)
+            product = dot_nn(top_turned[:, pl.ds(0, tokens)], grad_logits[:, pl.ds(base + col, cols)])
+            product = product + dot_nn(
+                top_turned[:, pl.ds(tokens, 3 * tokens)], grad_others[:, pl.ds(col, cols)]
+            )
+            put("vocab", pl.ds(col, cols), product)
+        plan.run_until(plan.now + 0.7)
+        plan.post(chunks["vocab", start])
 
     one_copies = []
     gain_2_total, bias_2_total = 0.0, 0.0
@@ -638,7 +666,7 @@
             spare[pl.ds(u * frames, frames), cols] = (
                 dot_tn(grad_score, queries[at, cols]) * score_scale
             ).astype(BF16)
-            plan.run_until(17.0 + 2.0 * (heads * u + h))
+            plan.run_until(plan.now + 1.5)
         sent[u] = dot_nt(grad_queries[at, :], w_query[...])
         one_copies.append(swap(sent.at[u], arrived.at[u], sibling))
     every = slice(None)
@@ -646,7 +674,7 @@
     plan.post(chunks["out", 0])
     put("query", every, dot_tn(one_low[...], grad_queries[...]))
     plan.post(chunks["query", 0])
-    plan.run_until(25.0)
+    plan.run_until(plan.now + 1.0)
 
     mem_copies = []
     rate_sums = [0.0, 0.0]
@@ -671,12 +699,15 @@
         group = jnp.zeros((1, width), jnp.int32) + rate_groups[u]
         for k in range(2):
             rate_sums[k] = rate_sums[k] + jnp.where((group == 1) == (k == 1), total, 0.0)
-        plan.run_until(26.5 + 1.5 * u)
-    for start in sorted(s for n, s in chunks if n == "kv"):
-        at = pl.ds(start, 256)
-        put("kv", at, dot_tn(mem_low[...], spare[:, at]))
-        plan.post(chunks["kv", start])
-        plan.run_until(29.0 + start / 256)
+        plan.run_until(plan.now + 1.2)
+    span = frames // 2
+    for k in range(2 * utterances):
+        at = pl.ds(k * span, span)
+        product = dot_tn(mem_low[at, :], spare[at, :])
+        product = product.reshape(r.src_kv.shape)
+        r.src_kv[...] = product if k == 0 else r.src_kv[...] + product
+    plan.run_until(plan.now + 2.0)
+    plan.post(*[chunks["kv", start] for start in sorted(s for n, s in chunks if n == "kv")])
 
     gain_1_total, bias_1_total = 0.0, 0.0
     for u in range(utterances):
@@ -707,8 +738,8 @@
         bias_1_total = bias_1_total + jnp.sum(grad_norm, axis=0, keepdims=True)
         zero = grad_two[at, :] + normalise_back(grad_norm * gain_1, hat, scale)
         terms[u] = blend[u * slots : (u + 1) * slots] * zero
-        r.acoustic_out[at, :] = zero - terms[u]
-        plan.run_until(32.0 + 2.0 * u)
+        stream_one[at, :] = zero - terms[u]
+        plan.run_until(plan.now + 1.5)
 
     last_taps = kernel_rows.shape[0]
     small_sent[0, pl.ds(last_taps, 12 - last_taps), :] = jnp.zeros((12 - last_taps, width), F32)
@@ -776,16 +807,24 @@
 
     term_arrived[me] = term_blocks[me]
     lax.fori_loop(1, n_dp, term_start, 0)
+    stores = []
+
+    def store(source, target):
+        copy = pltpu.make_async_copy(source, target, r.store_sem.at[len(stores)])
+        copy.start()
+        stores.append(copy)
+
+    store(stream_one, r.acoustic_out)
     for u in range(utterances):
         mem_copies[u].wait()
         for i in range(row_chunks):
             for j in range(width // 256):
                 index = (u * row_chunks + i) * (width // 256) + j
                 first_tile = (core * utterances) * row_chunks * (width // 256)
-                r.memory_out[pl.ds(u * frames + i * step_rows, step_rows), pl.ds(j * 128, 128)] = (
-                    logits[first_tile + index] + mem_arrived[index]
-                )
-    plan.run_until(45.0)
+                mem_arrived[index] = logits[first_tile + index] + mem_arrived[index]
+                at = pl.ds(u * frames + i * step_rows, step_rows)
+                store(mem_arrived.at[index], r.memory_out.at[at, pl.ds(j * 128, 128)])
+    plan.run_until(plan.now + 8.0)
     lax.fori_loop(1, n_dp, term_wait, 0)
     per_piece = 512 // slots
     blocks_hi = table_out.shape[1] // 256
@@ -818,15 +857,18 @@
     table_piece(0, True)
     if pieces <= 4:
         for p in range(1, pieces):
-            plan.run_until(45.0 + 1.5 * p)
+            plan.run_until(plan.now + 1.5)
             table_piece(p, False)
     else:
         lax.fori_loop(1, pieces, lambda p, c: (table_piece(p, False), c)[1], 0)
     table_swap = swap(table_out, table_theirs, sibling)
-    plan.run_until(56.0)
+    plan.run_until(plan.now + 3.0)
     table_swap.wait()
     table_out[...] = table_out[...] + table_theirs[...]
+    store(table_out, r.table_out)
     plan.finish()
+    for copy in stores:
+        copy.wait()
 
 
 def link_of(bit, bits):
@@ -835,22 +877,21 @@
     return bit
 
 
-def chunk_list(half_cols, width, bits, low_bits, sizes):
-    own = [b for b in bits if b != 0]
-    last = [] if low_bits else [0]
+def chunk_list(part_cols, width, bits, low_bits, sizes):
+    turned = [bits[1], bits[0]] + bits[2:]
     listing = []
-    edges = [half_cols // 128 * k // 4 * 128 for k in range(4)] + [half_cols]
-    for k in range(4):
-        listing.append(("vocab", edges[k], edges[k + 1] - edges[k], own + last))
-    units = sizes.units
-    for name in ("back", "in"):
-        for start in range(0, units, 512):
-            listing.append((name, start, 512, bits))
-    half = sizes.half
-    listing.append(("out", 0, half, bits))
-    listing.append(("query", 0, half, bits))
-    for start in range(0, 2 * half, 256):
-        listing.append(("kv", start, 256, bits))
+    tiles = part_cols // 128
+    edges = [tiles * k // 3 * 128 for k in range(4)]
+    for k in range(3):
+        order = [b for b in bits if b > 1]
+        listing.append(("vocab", edges[k], edges[k + 1] - edges[k], order))
+    for name, order in (("back", turned), ("in", bits)):
+        for start in range(0, sizes.units, 512):
+            listing.append((name, start, 512, order))
+    listing.append(("out", 0, sizes.half, turned))
+    listing.append(("query", 0, sizes.half, bits))
+    for k, start in enumerate(range(0, 2 * sizes.half, 256)):
+        listing.append(("kv", start, 256, [bits, turned][k % 2]))
     return listing
 
 
@@ -868,7 +909,8 @@
     units = w_in.shape[1]
     vocab_here = w_vocab.shape[1]
     table_rows = embedding.shape[0]
-    half_cols = (vocab_here + 255) // 256 * 128
+    part_cols = ((vocab_here + 127) // 128 + 3) // 4 * 128
+    all_cols = (vocab_here + 255) // 256 * 256
     w_turned = w_vocab.T
     main = vocab_here // 256 * 256
     mains = table_rows // 2048 * 2048
@@ -883,7 +925,8 @@
     block_rows = feature_rows + 8 if features >= 8 else 8
     blocks_hi = (table_rows + 255) // 256
     sizes = SimpleNamespace(units=units, half=half)
-    listing = chunk_list(half_cols, width, bits, low_bits, sizes)
+    plane = [b for b in bits if b < 2]
+    listing = chunk_list(part_cols, width, bits, low_bits, sizes)
     most = max(len(c[3]) for c in listing)
 
     f32 = lambda *shape: jax.ShapeDtypeStruct(shape, F32)
@@ -917,16 +960,16 @@
     )
     outputs = dict(
         loss_out=f32(utterances, slots),
-        acoustic_out=f32(tokens, width),
-        memory_out=f32(mem_rows, width // 2),
-        table_out=f32(feature_rows, blocks_hi * 256),
         small_out=f32(24, width),
-        vocab_out=f32(*(() if low_bits else (2,)), rows, half_cols),
+        vocab_out=f32(*((2,) * len(plane) if low_bits else (4,)), rows, part_cols),
         in_out=f32(rows, units),
         back_out=f32(rows, units),
         query_out=f32(rows, half),
         out_out=f32(rows, half),
         kv_out=f32(rows, 2 * half),
+        acoustic_out=f32(tokens, width),
+        memory_out=f32(mem_rows, width // 2),
+        table_out=f32(feature_rows, blocks_hi * 256),
     )
     shape = (2,) * steps + (rows,)
     scratch = dict(
@@ -935,7 +978,7 @@
         w_out=v16(half, width),
         w_in=v16(width, units),
         w_back=v16(units, width),
-        w_vocab=v16(2 * half_cols, width),
+        w_vocab=v16(all_cols, width),
         mem_low=v16(mem_rows, width),
         kv=v16(mem_rows, 2 * half),
         spare=v16(mem_rows, 2 * half),
@@ -951,11 +994,13 @@
         norm_low=v16(tokens, width),
         hidden=v16(tokens, units),
         gelu_slope=v32(tokens, units),
-        top=v16(2, tokens, width),
-        logits=v32(2 * half_cols // 128, tokens, 128),
-        grad_logits=v16(2 * tokens, half_cols),
-        part3=v32(utterances, 2, slots, width),
-        arrived3=v32(2, slots, width),
+        top=v16(4, tokens, width),
+        logits=v32(all_cols // 128, tokens, 128),
+        grad_logits=v16(tokens, all_cols),
+        grad_others=v16(3 * tokens, part_cols),
+        top_turned=v16(width, 4 * tokens),
+        taken_mine=v32(utterances, slots, width),
+        taken_theirs=v32(utterances, slots, width),
         grad_three=v32(utterances, slots, width),
         grad_two=v32(tokens, width),
         branch_low=v16(tokens, width),
@@ -963,12 +1008,12 @@
         att_low=v16(tokens, width),
         grad_queries=v16(tokens, half),
         mem_arrived=v32(mem_rows // 256 * (width // 256), 256, 128),
-        meta=v32(2, 8, tokens),
-        stats=v32(2, 8, 2 * tokens),
-        stats_arrived=v32(4, 8, 2 * tokens),
+        meta=v32(4, 8, tokens),
+        stats=v32(2, 8, tokens),
+        stats_arrived=v32(2, 8, tokens),
         sent=v32(2 * utterances, slots, width),
         arrived=v32(2 * utterances, slots, width),
-        gathered=v32(2, slots, width),
+        gathered=v32(3, 2, slots, width),
         small_sent=v32(nbits + 1, 24, width),
         small_arrived=v32(nbits + 1, 24, width),
         term_blocks=v32(n_dp, block_rows, slots),
@@ -976,13 +1021,19 @@
         onehot_lo=v16(256, 512),
         table_rest=v16((table_rows - mains + 127) // 128 * 128, width),
         table_theirs=v32(feature_rows, blocks_hi * 256),
-        src_vocab=v32(*shape, half_cols),
+        table_mine=v32(feature_rows, blocks_hi * 256),
+        src_vocab=v32(*shape, part_cols),
         src_back=v32(*shape, units),
+        vocab_sum=v32(*(2,) * len(plane), rows, part_cols),
+        vocab_traded=v32(3, rows, part_cols),
         src_in=v32(*shape, units),
         src_out=v32(*shape, half),
         src_query=v32(*shape, half),
         src_kv=v32(*shape, 2 * half),
         load_sem=dma(24),
+        store_sem=dma(24),
+        trade_send=dma(part_cols // 128, 3),
+        trade_recv=dma(part_cols // 128, 3),
         swap_send=dma(40),
         swap_recv=dma(40),
         scatter_send=dma(len(listing), most),
@@ -1003,7 +1054,7 @@
         named, rest = refs[: len(names)], list(refs[len(names) :])
         lands = [[rest.pop(0) for _ in chunk] for chunk in landing]
         decoder_kernel(
-            names + ["landing", "units", "half"], vocab_here, half_cols, table_rows, n_dp, bits,
+            names + ["landing", "units", "half"], vocab_here, part_cols, table_rows, n_dp, bits,
             low_bits, *named, lands, units, half,
         )
 
@@ -1011,7 +1062,7 @@
         kernel,
         out_shape=list(outputs.values()),
         in_specs=[spec for spec, _ in inputs.values()],
-        out_specs=[VMEM] * len(outputs),
+        out_specs=[VMEM] * (len(outputs) - 3) + [ANY] * 3,
         scratch_shapes=list(scratch.values()) + flat,
         compiler_params=pltpu.CompilerParams(
             collective_id=1, has_side_effects=True, vmem_limit_bytes=64 << 20
@@ -1021,19 +1072,23 @@
 
 
 def deliver_kernel(n_dp, *refs):
-    loss, small, table, vocab, kv, query, out, in_, back, acoustic, memory = refs[:11]
+    loss_from, small_from, table_from, vocab_from, kv_from = refs[:5]
+    query, out, in_, back, acoustic, memory = refs[5:11]
     (
         loss_to, gain_one_to, bias_one_to, gain_two_to, bias_two_to, taps_to, rate_to,
         table_to, vocab_to, key_to, value_to, query_to, out_to, in_to, back_to, acoustic_to, memory_to,
     ) = refs[11:28]
-    sem = refs[28]
+    loss, small, table, vocab, kv, sem = refs[28:]
     copies = []
     for source, target in (
+        (loss_from, loss), (small_from, small), (table_from, table), (vocab_from, vocab), (kv_from, kv),
         (memory, memory_to), (acoustic, acoustic_to), (in_, in_to), (back, back_to),
         (query, query_to), (out, out_to),
     ):
         copies.append(pltpu.make_async_copy(source, target, sem.at[len(copies)]))
         copies[-1].start()
+    for copy in copies[:5]:
+        copy.wait()
     slots = loss.shape[1]
     for u in range(loss.shape[0]):
         loss_to[:, pl.ds(u * slots, slots)] = loss[pl.ds(u, 1), :]
@@ -1047,14 +1102,18 @@
         target[...] = mine[12 + i : 13 + i]
     rate_to[...] = small[pl.ds(16, 2), :]
     table_to[...] = table[pl.ds(0, table_to.shape[0]), :][:, : table_to.shape[1]]
-    half_cols = vocab.shape[2]
-    vocab_to[:, pl.ds(0, half_cols)] = vocab[0]
-    rest = vocab_to.shape[1] - half_cols
-    vocab_to[:, pl.ds(half_cols, rest)] = vocab[1][:, :rest]
+    part_cols = vocab.shape[2]
+    vocab_here = vocab_to.shape[1]
+    last = (vocab_here + 255) // 256 * 256 - part_cols
+    for k in range(3):
+        vocab_to[:, pl.ds(k * part_cols, part_cols)] = vocab[k]
+    rest = vocab_here - 3 * part_cols
+    skip = 3 * part_cols - last
+    vocab_to[:, pl.ds(3 * part_cols, rest)] = vocab[3][:, skip : skip + rest]
     half = key_to.shape[1]
     key_to[...] = kv[:, pl.ds(0, half)]
     value_to[...] = kv[:, pl.ds(half, half)]
-    for copy in copies:
+    for copy in copies[5:]:
         copy.wait()
 
 
@@ -1094,9 +1153,10 @@
     if low_bits:
         size = 1 << len(low_bits)
         groups = [list(range(g * size, (g + 1) * size)) for g in range(n_dp // size)]
-        pairs = [[2 * g, 2 * g + 1] for g in range(n_dp // 2)]
+        planes = [list(range(4 * g, 4 * g + 4)) for g in range(n_dp // 4)]
+        own_rows = model_width // n_dp
         vocab = lax.all_to_all(
-            vocab.reshape(2, vocab.shape[0] // 2, -1), "dp", 0, 0, axis_index_groups=pairs, tiled=True
+            vocab.reshape(4, own_rows, -1), "dp", 0, 0, axis_index_groups=planes, tiled=True
         )
         summed = [
             lax.psum_scatter(s, "dp", scatter_dimension=0, axis_index_groups=groups, tiled=True)
@@ -1123,10 +1183,14 @@
             like(result.acoustic_out),
             like(result.memory_out),
         ],
-        in_specs=[VMEM] * 5 + [ANY] * 6,
+        in_specs=[ANY] * 11,
         out_specs=[VMEM] * 11 + [ANY] * 6,
-        scratch_shapes=[pltpu.SemaphoreType.DMA((6,))],
-        compiler_params=pltpu.CompilerParams(vmem_limit_bytes=32 << 20),
+        scratch_shapes=[
+            pltpu.VMEM(x.shape, F32)
+            for x in (result.loss_out, result.small_out, result.table_out, vocab, grad_kv)
+        ]
+        + [pltpu.SemaphoreType.DMA((11,))],
+        compiler_params=pltpu.CompilerParams(vmem_limit_bytes=60 << 20),
     )(
         result.loss_out, result.small_out, result.table_out, vocab, grad_kv, grad_query, grad_out,
         grad_in, grad_back, result.acoustic_out, result.memory_out,

time: 221 us -> 227 us (1.027)
  Pallas kernels: 206 us -> 223 us
  local copies, waits for them, and re-layouts: 13.7 us -> 3.19 us
    pallas_call x1, Pallas kernels: 2.83 us -> 91.8 us  [per_device(): pl.pallas_call(partial(deliver_kernel, n_dp), out_shape=[f32(1, tok_rows)...]
    pallas_call x1, Pallas kernels: 203 us -> 131 us  [decoder_call(): pl.pallas_call(kernel, out_shape=list(outputs.values()), in_specs=[spec f...]
    unnamed x22 -> x0, local copies, waits for them, and re-layouts: 10.5 us -> none
where the time goes in v5:
time: 227 us
  Pallas kernels  223 us (98%)
  local copies, waits for them, and re-layouts  3.19 us (1%)
    pallas_call x1, Pallas kernels, decoder_call(): pl.pallas_call(kernel, out_shape=list(outputs.values()), in_specs=[spec f...  131 us
    pallas_call x1, Pallas kernels, per_device(): pl.pallas_call(partial(deliver_kernel, n_dp), out_shape=[f32(1, tok_rows)...  91.8 us

profile of v5, /device:TPU:0, one launch (start us, length us, event | category | flops | bytes accessed | tf_op | source)
XLA Modules:
  0.0 226.7 jit_solution(9073513580047742730)
XLA Ops:
  0.7 1.6 slice.8.refs_1_
  2.2 1.6 slice.7.refs_2_
  3.8 130.9 %shard_map.332 = (f32[2,128]{1,0:T(2,128)}, f32[24,512]{1,0:T(8,128)}, f32[4,32,1152]{2,1,0:T(8,128)}, f32[32,1024]{1,0:T(8,128)}, f32[32,1024]{1,0:T(8,128)}, /...) custom-call(bf16[256,512]{1,0:T(8,128)(2,1)} %refs_0_.1, ...), custom_call_target="tpu_custom_call" | custom-call | tf_op jit(solution)/shard_map/pallas_call | solution.py:1061
  134.8 91.8 %shard_map.333 = (f32[1,256]{1,0:T(1,128)}, f32[1,32]{1,0:T(1,128)}, f32[1,32]{1,0:T(1,128)}, f32[1,32]{1,0:T(1,128)}, f32[1,32]{1,0:T(1,128)}, /*index=5*/f32[1...) custom-call(f32[2,128]{1,0:T(2,128)} %get-tuple-element.45.refs_0_, ...), custom_call_target="tpu_custom_call" | custom-call | tf_op jit(solution)/shard_map/pallas_call | solution.py:1172

commit v6 on v5

--- a/solution.py
+++ b/solution.py
@@ -1072,23 +1072,22 @@
 
 
 def deliver_kernel(n_dp, *refs):
-    loss_from, small_from, table_from, vocab_from, kv_from = refs[:5]
-    query, out, in_, back, acoustic, memory = refs[5:11]
+    sources, targets, held, sem_in, sem_out = refs[:11], refs[11:28], refs[28:39], refs[39], refs[40]
+    loss, small, table, vocab, kv = held[:5]
     (
         loss_to, gain_one_to, bias_one_to, gain_two_to, bias_two_to, taps_to, rate_to,
-        table_to, vocab_to, key_to, value_to, query_to, out_to, in_to, back_to, acoustic_to, memory_to,
-    ) = refs[11:28]
-    loss, small, table, vocab, kv, sem = refs[28:]
-    copies = []
-    for source, target in (
-        (loss_from, loss), (small_from, small), (table_from, table), (vocab_from, vocab), (kv_from, kv),
-        (memory, memory_to), (acoustic, acoustic_to), (in_, in_to), (back, back_to),
-        (query, query_to), (out, out_to),
-    ):
-        copies.append(pltpu.make_async_copy(source, target, sem.at[len(copies)]))
-        copies[-1].start()
-    for copy in copies[:5]:
-        copy.wait()
+        table_to, vocab_to, key_to, value_to,
+    ) = targets[:11]
+    reads, writes = [], []
+    for i, (source, buffer) in enumerate(zip(sources, held)):
+        reads.append(pltpu.make_async_copy(source, buffer, sem_in.at[i]))
+        reads[-1].start()
+    for i in range(5, 11):
+        reads[i].wait()
+        writes.append(pltpu.make_async_copy(held[i], targets[6 + i], sem_out.at[i]))
+        writes[-1].start()
+    for i in range(5):
+        reads[i].wait()
     slots = loss.shape[1]
     for u in range(loss.shape[0]):
         loss_to[:, pl.ds(u * slots, slots)] = loss[pl.ds(u, 1), :]
@@ -1113,7 +1112,7 @@
     half = key_to.shape[1]
     key_to[...] = kv[:, pl.ds(0, half)]
     value_to[...] = kv[:, pl.ds(half, half)]
-    for copy in copies[5:]:
+    for copy in writes:
         copy.wait()
 
 
@@ -1166,6 +1165,10 @@
     own = model_width // n_dp
     f32 = lambda *shape: jax.ShapeDtypeStruct(shape, F32)
     like = lambda x: jax.ShapeDtypeStruct(x.shape, F32)
+    handed = (
+        result.loss_out, result.small_out, result.table_out, vocab, grad_kv, grad_query, grad_out,
+        grad_in, grad_back, result.acoustic_out, result.memory_out,
+    )
     (
         token_loss, gain_1, bias_1, gain_2, bias_2, grad_taps, grad_rate, grad_table, grad_vocab,
         grad_key, grad_value, grad_query, grad_out, grad_in, grad_back, grad_acoustic, grad_memory,
@@ -1185,16 +1188,10 @@
         ],
         in_specs=[ANY] * 11,
         out_specs=[VMEM] * 11 + [ANY] * 6,
-        scratch_shapes=[
-            pltpu.VMEM(x.shape, F32)
-            for x in (result.loss_out, result.small_out, result.table_out, vocab, grad_kv)
-        ]
-        + [pltpu.SemaphoreType.DMA((11,))],
+        scratch_shapes=[pltpu.VMEM(x.shape, F32) for x in handed]
+        + [pltpu.SemaphoreType.DMA((11,)), pltpu.SemaphoreType.DMA((11,))],
         compiler_params=pltpu.CompilerParams(vmem_limit_bytes=60 << 20),
-    )(
-        result.loss_out, result.small_out, result.table_out, vocab, grad_kv, grad_query, grad_out,
-        grad_in, grad_back, result.acoustic_out, result.memory_out,
-    )
+    )(*handed)
     return (
         token_loss.reshape(tok_rows),
         grad_acoustic,

time: 227 us -> 140 us (0.62)
  Pallas kernels: 223 us -> 136 us
    pallas_call x1, Pallas kernels: 91.8 us -> 5.17 us  [per_device(): pl.pallas_call(partial(deliver_kernel, n_dp), out_shape=[f32(1, tok_rows)...]
where the time goes in v6:
time: 140 us
  Pallas kernels  136 us (97%)
  local copies, waits for them, and re-layouts  3.19 us (2%)
    pallas_call x1, Pallas kernels, decoder_call(): pl.pallas_call(kernel, out_shape=list(outputs.values()), in_specs=[spec f...  131 us
    pallas_call x1, Pallas kernels, per_device(): pl.pallas_call(partial(deliver_kernel, n_dp), out_shape=[f32(1, tok_rows)...  5.17 us

profile of v6, /device:TPU:0, one launch (start us, length us, event | category | flops | bytes accessed | tf_op | source)
XLA Modules:
  0.0 140.1 jit_solution(17463784011220112229)
XLA Ops:
  0.7 1.6 %slice.8.refs_1_ = bf16[106,512]{1,0:T(8,128)(2,1)} slice(bf16[4202,512]{1,0:T(8,128)(2,1)} %bitcast.15), slice={[4096:4202], [0:512]} | slice | bytes 217088 | tf_op jit(solution)/shard_map/slice | solution.py:938
  2.2 1.6 %slice.7.refs_2_ = bf16[212,512]{1,0:T(8,128)(2,1)} slice(bf16[8404,512]{1,0:T(8,128)(2,1)} %refs_4_.1), slice={[8192:8404], [0:512]} | slice | bytes 434176 | tf_op jit(solution)/shard_map/slice | solution.py:939
  3.8 130.9 %shard_map.332 = (f32[2,128]{1,0:T(2,128)}, f32[24,512]{1,0:T(8,128)}, f32[4,32,1152]{2,1,0:T(8,128)}, f32[32,1024]{1,0:T(8,128)}, f32[32,1024]{1,0:T(8,128)}, /...) custom-call(bf16[256,512]{1,0:T(8,128)(2,1)} %refs_0_.1, ...), custom_call_target="tpu_custom_call" | custom-call | tf_op jit(solution)/shard_map/pallas_call | solution.py:1061
  134.8 5.2 %shard_map.333 = (f32[1,256]{1,0:T(1,128)}, f32[1,32]{1,0:T(1,128)}, f32[1,32]{1,0:T(1,128)}, f32[1,32]{1,0:T(1,128)}, f32[1,32]{1,0:T(1,128)}, /*index=5*/f32[1...) custom-call(f32[2,128]{1,0:T(2,128)} %get-tuple-element.45.refs_0_, ...), custom_call_target="tpu_custom_call" | custom-call | tf_op jit(solution)/shard_map/pallas_call | solution.py:1175

commit v7 on v6

--- a/solution.py
+++ b/solution.py
@@ -65,7 +65,7 @@
 class Planner:
     RATE = 0.045e6
     HOP = 1.5
-    BACKLOG = 6.0
+    BACKLOG = 3.0
 
     def __init__(self):
         self.now = 0.0
@@ -230,10 +230,10 @@
         return load(table.at[at, :], spare.at[pl.ds(k % 2 * block, block), :])
 
     table_loads = [load_table(0), load_table(1)]
-    main = vocab_here // 256 * 256
-    load_vocab = load(r.w_vocab_hbm.at[pl.ds(0, main), :], w_vocab.at[pl.ds(0, main), :])
-    w_vocab[pl.ds(main, w_vocab.shape[0] - main), :] = jnp.zeros((w_vocab.shape[0] - main, width), BF16)
-    w_vocab[pl.ds(main, vocab_here - main), :] = r.w_tail[...]
+    main = 4 * part_cols
+    load_vocab = load(r.w_vocab_hbm, w_vocab)
+    w_rest = r.w_rest
+    w_rest[...] = jnp.zeros(w_rest.shape, BF16)
     r.table_rest[...] = jnp.zeros(r.table_rest.shape, BF16)
     r.table_rest[pl.ds(0, table_rows - mains), :] = r.table_tail[...]
 
@@ -269,31 +269,13 @@
     def rows(u):
         return pl.ds(u * slots, slots)
 
-    load_memory.wait()
-    for copy in load_kv:
-        copy.wait()
-    step_rows = 256
-    row_chunks = frames // step_rows
-
-    def kv_step(i, carry):
-        at = pl.ds(pl.multiple_of(i * step_rows, step_rows), step_rows)
-        group = jnp.zeros((1, width), jnp.int32) + rate_groups[i // row_chunks]
-        rate_row = jnp.where(group == 1, rate_table[pl.ds(1, 1), :], rate_table[pl.ds(0, 1), :])
-        low = (mem_low[at, :].astype(F32) + rate_row).astype(BF16)
-        mem_low[at, :] = low
-        kv[at, :] = dot_nn(low, w_kv[...]).astype(BF16)
-        return carry
-
-    lax.fori_loop(0, utterances * row_chunks, kv_step, 0)
-
     edge = jnp.zeros((8, width), F32)
     for u in range(utterances):
         padded[u, pl.ds(0, 8), :] = edge
         padded[u, pl.ds(8 + slots, 8), :] = edge
 
-    pl.semaphore_wait(barrier, n_dp)
-    load_query.wait()
-    load_out.wait()
+    step_rows = 256
+    row_chunks = frames // step_rows
 
     def key_of(u, h):
         return kv[pl.ds(u * frames, frames), pl.ds(h * HD, HD)]
@@ -329,28 +311,35 @@
         local = target_column.astype(jnp.int32) - core * vocab_here
         return jnp.where((local >= 0) & (local < vocab_here), local, -1)
 
-    def vocab_tile(tile, first, col, target, top_m, picked):
-        ids = col + lax.broadcasted_iota(jnp.int32, (1, 128), 1)
-        tile = jnp.where(ids < vocab_here, tile, NEG)
-        logits[first] = tile
-        return jnp.maximum(top_m, tile), picked + jnp.where(ids == target, tile, 0.0)
-
     def vocab_stats(target):
-        start = (jnp.full((tokens, 128), NEG, F32), jnp.zeros((tokens, 128), F32))
+        tiles = main // 128
+        step_tiles = 4
 
         def step(j, carry):
-            col = pl.multiple_of(j * 256, 256)
-            product = dot_nt(top[0], w_vocab[pl.ds(col, 256), :])
-            carry = vocab_tile(product[:, :128], 2 * j, col, target, *carry)
-            return vocab_tile(product[:, 128:], 2 * j + 1, col + 128, target, *carry)
-
-        top_m, picked = lax.fori_loop(0, w_vocab.shape[0] // 256, step, start)
+            top_m, picked = carry
+            col = pl.multiple_of(j * (step_tiles * 128), step_tiles * 128)
+            product = dot_nt(top[0], w_vocab[pl.ds(col, step_tiles * 128), :])
+            for i in range(step_tiles):
+                tile = product[:, i * 128 : (i + 1) * 128]
+                ids = col + i * 128 + lax.broadcasted_iota(jnp.int32, (1, 128), 1)
+                logits[j * step_tiles + i] = tile
+                top_m = jnp.maximum(top_m, tile)
+                picked = picked + jnp.where(ids == target, tile, 0.0)
+            return top_m, picked
+
+        ids = main + lax.broadcasted_iota(jnp.int32, (1, 128), 1)
+        last = jnp.where(ids < vocab_here, dot_nt(top[0], w_rest[...]), NEG)
+        logits[tiles] = last
+        picked = jnp.where(ids == target, last, 0.0)
+        top_m, picked = lax.fori_loop(0, tiles // step_tiles, step, (last, picked))
         top_row = jnp.max(top_m, axis=1, keepdims=True)
 
         def add(j, total):
-            return total + jnp.exp(logits[j] - top_row)
-
-        total = lax.fori_loop(0, w_vocab.shape[0] // 128, add, jnp.zeros((tokens, 128), F32))
+            for i in range(3):
+                total = total + jnp.exp(logits[3 * j + i] - top_row)
+            return total
+
+        total = lax.fori_loop(0, (tiles + 1) // 3, add, jnp.zeros((tokens, 128), F32))
         return (
             top_row,
             jnp.sum(total, axis=1, keepdims=True),
@@ -367,23 +356,28 @@
             picked = picked + b[2:3]
         return top_value + jnp.log(total), picked
 
+    def memory_block(u):
+        at = rows(u)
+        valid = own_valid[u * slots : (u + 1) * slots]
+        hat, _ = normalise(stream_in[at, :])
+        padded[u, pl.ds(8, slots), :] = (hat * gain_1 + bias_1) * valid
+        for j in range(width // 128):
+            cols = pl.ds(j * 128, 128)
+            total = jnp.zeros((slots, 128), F32)
+            for k in range(kernel_rows.shape[0]):
+                shift = 8 + k - kernel_rows.shape[0] // 2
+                total = total + kernel_rows[pl.ds(k, 1), cols] * padded[u, pl.ds(shift, slots), cols]
+            stream_one[at, cols] = stream_in[at, cols] + total * valid
+        low = stream_one[at, :].astype(BF16)
+        one_low[at, :] = low
+        queries[at, :] = dot_nn(low, w_query[...]).astype(BF16)
+
     def forward(second, beside_one=None, beside_two=None):
         copies = []
         for u in range(utterances):
             at = rows(u)
-            valid = own_valid[u * slots : (u + 1) * slots]
-            hat, _ = normalise(stream_in[at, :])
-            padded[u, pl.ds(8, slots), :] = (hat * gain_1 + bias_1) * valid
-            for j in range(width // 128):
-                cols = pl.ds(j * 128, 128)
-                total = jnp.zeros((slots, 128), F32)
-                for k in range(kernel_rows.shape[0]):
-                    shift = 8 + k - kernel_rows.shape[0] // 2
-                    total = total + kernel_rows[pl.ds(k, 1), cols] * padded[u, pl.ds(shift, slots), cols]
-                stream_one[at, cols] = stream_in[at, cols] + total * valid
-            low = stream_one[at, :].astype(BF16)
-            one_low[at, :] = low
-            queries[at, :] = dot_nn(low, w_query[...]).astype(BF16)
+            if second:
+                memory_block(u)
             frame_ok = frame_lane < memory_lengths[u]
             for h in range(heads):
                 cols = pl.ds(h * HD, HD)
@@ -438,9 +432,32 @@
             look_up_block(k)
         look_up_rest()
 
+    load_query.wait()
+    for u in range(utterances):
+        memory_block(u)
+    load_memory.wait()
+    for copy in load_kv:
+        copy.wait()
+    kv_rows = 512
+    kv_chunks = frames // kv_rows
+
+    def kv_step(i, carry):
+        at = pl.ds(pl.multiple_of(i * kv_rows, kv_rows), kv_rows)
+        group = jnp.zeros((1, width), jnp.int32) + rate_groups[i // kv_chunks]
+        rate_row = jnp.where(group == 1, rate_table[pl.ds(1, 1), :], rate_table[pl.ds(0, 1), :])
+        low = (mem_low[at, :].astype(F32) + rate_row).astype(BF16)
+        mem_low[at, :] = low
+        kv[at, :] = dot_nn(low, w_kv[...]).astype(BF16)
+        return carry
+
+    lax.fori_loop(0, utterances * kv_chunks, kv_step, 0)
+
+    pl.semaphore_wait(barrier, n_dp)
+    load_out.wait()
     forward(False, beside_one, beside_two)
     table_swap = swap(taken_mine, taken_theirs, sibling)
     load_vocab.wait()
+    w_rest[pl.ds(0, vocab_here - main), :] = w_vocab[pl.ds(main, vocab_here - main), :]
     own_local = local_targets(own_target)
     stats[0] = to_rows(vocab_stats(own_local))
     first_swap = swap(stats.at[0], stats_arrived.at[0], sibling)
@@ -482,10 +499,12 @@
         grad_logits[:, pl.ds(col, 128)] = grad.astype(BF16)
         return carry
 
-    lax.fori_loop(0, w_vocab.shape[0] // 128, slope, 0)
+    lax.fori_loop(0, main // 128 + 1, slope, 0)
     three_copies = []
     for u in range(utterances):
-        sent[u] = dot_nn(grad_logits[rows(u), :], w_vocab[...])
+        sent[u] = dot_nn(grad_logits[rows(u), pl.ds(0, main)], w_vocab[pl.ds(0, main), :]) + dot_nn(
+            grad_logits[rows(u), pl.ds(main, 128)], w_rest[...]
+        )
         three_copies.append(swap(sent.at[u], arrived.at[u], sibling))
 
     plan = Planner()
@@ -495,7 +514,11 @@
     def make_chunk(index):
         name, start, cols, order = chunk_list(part_cols, width, bits, low_bits, r)[index]
         source, landing = getattr(r, "src_" + name), r.landing[index]
-        out = r.vocab_sum if name == "vocab" and not low_bits else getattr(r, name + "_out")
+        if name == "kv":
+            out, out_start = (r.key_out, r.value_out)[start // cols], 0
+        else:
+            out = r.vocab_sum if name == "vocab" and not low_bits else getattr(r, name + "_out")
+            out_start = start
         rows_here = source.shape[-2]
 
         def pick(step, which):
@@ -523,7 +546,7 @@
             copy.wait_recv()
             ref, where = pick(step, bit_of[order[step]])
             got = landing[step]
-            at = pl.ds(start, cols)
+            at = pl.ds(out_start, cols)
             if step < len(order) - 1:
                 got[...] = got[...] + ref[where]
             elif name == "vocab":
@@ -561,8 +584,10 @@
         def take(step, copies):
             copies.wait_recv()
             for j in range(1, 4):
-                r.vocab_out[lax.rem(mate[j], 4), :, at] = traded[j - 1, :, at]
-            r.vocab_out[quarter, :, at] = summed[quarter // 2, lax.rem(quarter, 2), :, at]
+                there = pl.multiple_of(lax.rem(mate[j], 4) * part_cols + start, 128)
+                r.vocab_out[:, pl.ds(there, cols)] = traded[j - 1, :, at]
+            here = pl.multiple_of(base + start, 128)
+            r.vocab_out[:, pl.ds(here, cols)] = summed[quarter // 2, lax.rem(quarter, 2), :, at]
 
         return Chunk([(0, 2 * r.src_vocab.shape[-2] * cols * 4)], send, take)
 
@@ -604,12 +629,8 @@
         token_swaps[j - 1].wait()
         share_swaps.append(swap(gathered.at[j - 1, 0], gathered.at[j - 1, 1], sibling))
         top[j, at_core, :] = gathered[j - 1, 0].astype(BF16)
-    base = pl.multiple_of(
-        quarter * part_cols - quarter // 3 * (4 * part_cols - w_vocab.shape[0]), 128
-    )
-    pieces = [(c, 256) for c in range(0, part_cols // 256 * 256, 256)]
-    if part_cols % 256:
-        pieces.append((part_cols // 256 * 256, part_cols % 256))
+    base = pl.multiple_of(quarter * part_cols, part_cols)
+    pieces = [(c, 256) for c in range(0, part_cols, 256)]
     for j in range(1, 4):
         meta_swaps[j - 1].wait()
         columns = to_columns(meta[j])
@@ -619,13 +640,13 @@
         for col, cols in pieces:
             ids = base + col + lax.broadcasted_iota(jnp.int32, (1, cols), 1)
             tile = dot_nt(top[j], w_vocab[pl.ds(base + col, cols), :])
-            tile = jnp.where(ids < vocab_here, tile, NEG)
             grad = (jnp.exp(tile - log_total) - jnp.where(ids == target, 1.0, 0.0)) * valid
             grad_others[pl.ds((j - 1) * tokens, tokens), pl.ds(col, cols)] = grad.astype(BF16)
         plan.run_until(plan.now + 0.8)
     top_turned = r.top_turned
     for j in range(4):
         top_turned[:, pl.ds(j * tokens, tokens)] = top[j].T
+    put("rest", slice(None), dot_nn(top_turned[:, pl.ds(0, tokens)], grad_logits[:, pl.ds(main, 128)]))
     starts = sorted(start for name, start in chunks if name == "vocab")
     for start, stop in zip(starts, starts[1:] + [part_cols]):
         for col in range(start, stop, 256):
@@ -637,6 +658,7 @@
             put("vocab", pl.ds(col, cols), product)
         plan.run_until(plan.now + 0.7)
         plan.post(chunks["vocab", start])
+    plan.post(chunks["rest", 0])
 
     one_copies = []
     gain_2_total, bias_2_total = 0.0, 0.0
@@ -864,9 +886,15 @@
     table_swap = swap(table_out, table_theirs, sibling)
     plan.run_until(plan.now + 3.0)
     table_swap.wait()
-    table_out[...] = table_out[...] + table_theirs[...]
-    store(table_out, r.table_out)
+    whole_table = r.whole_table
+    whole_table[...] = (
+        table_out[pl.ds(0, whole_table.shape[0]), :] + table_theirs[pl.ds(0, whole_table.shape[0]), :]
+    )[:, :table_rows]
+    store(whole_table, r.table_out)
     plan.finish()
+    if not low_bits:
+        rest = vocab_here - main
+        r.vocab_out[:, pl.ds(main, rest)] = r.rest_out[...][:, :rest]
     for copy in stores:
         copy.wait()
 
@@ -880,13 +908,13 @@
 def chunk_list(part_cols, width, bits, low_bits, sizes):
     turned = [bits[1], bits[0]] + bits[2:]
     listing = []
-    tiles = part_cols // 128
-    edges = [tiles * k // 3 * 128 for k in range(4)]
-    for k in range(3):
-        order = [b for b in bits if b > 1]
-        listing.append(("vocab", edges[k], edges[k + 1] - edges[k], order))
+    for start in range(0, part_cols, 512):
+        listing.append(("vocab", start, 512, [b for b in bits if b > 1]))
+    listing.append(("rest", 0, 128, bits))
     for name, order in (("back", turned), ("in", bits)):
         for start in range(0, sizes.units, 512):
+            if name == "in" and start:
+                order = [bits[2], bits[0], bits[1]] + bits[3:]
             listing.append((name, start, 512, order))
     listing.append(("out", 0, sizes.half, turned))
     listing.append(("query", 0, sizes.half, bits))
@@ -909,10 +937,9 @@
     units = w_in.shape[1]
     vocab_here = w_vocab.shape[1]
     table_rows = embedding.shape[0]
-    part_cols = ((vocab_here + 127) // 128 + 3) // 4 * 128
-    all_cols = (vocab_here + 255) // 256 * 256
+    part_cols = vocab_here // 512 * 128
+    all_cols = 4 * part_cols + 128
     w_turned = w_vocab.T
-    main = vocab_here // 256 * 256
     mains = table_rows // 2048 * 2048
     nbits = n_dp.bit_length() - 1
     steps = nbits
@@ -935,7 +962,6 @@
     dma = lambda *shape: pltpu.SemaphoreType.DMA(shape)
     inputs = dict(
         acoustic=(VMEM, acoustic),
-        w_tail=(VMEM, w_turned[main:]),
         table_tail=(VMEM, embedding[mains:]),
         memory=(ANY, memory),
         table=(ANY, embedding),
@@ -961,15 +987,17 @@
     outputs = dict(
         loss_out=f32(utterances, slots),
         small_out=f32(24, width),
-        vocab_out=f32(*((2,) * len(plane) if low_bits else (4,)), rows, part_cols),
+        vocab_out=f32(2, rows, part_cols) if low_bits else f32(rows, vocab_here),
+        rest_out=f32(rows, 128),
         in_out=f32(rows, units),
         back_out=f32(rows, units),
         query_out=f32(rows, half),
         out_out=f32(rows, half),
-        kv_out=f32(rows, 2 * half),
+        key_out=f32(rows, half),
+        value_out=f32(rows, half),
         acoustic_out=f32(tokens, width),
         memory_out=f32(mem_rows, width // 2),
-        table_out=f32(feature_rows, blocks_hi * 256),
+        table_out=f32(features, table_rows),
     )
     shape = (2,) * steps + (rows,)
     scratch = dict(
@@ -978,7 +1006,8 @@
         w_out=v16(half, width),
         w_in=v16(width, units),
         w_back=v16(units, width),
-        w_vocab=v16(all_cols, width),
+        w_vocab=v16(vocab_here, width),
+        w_rest=v16(128, width),
         mem_low=v16(mem_rows, width),
         kv=v16(mem_rows, 2 * half),
         spare=v16(mem_rows, 2 * half),
@@ -1023,6 +1052,8 @@
         table_theirs=v32(feature_rows, blocks_hi * 256),
         table_mine=v32(feature_rows, blocks_hi * 256),
         src_vocab=v32(*shape, part_cols),
+        src_rest=v32(*shape, 128),
+        whole_table=v32(features, table_rows),
         src_back=v32(*shape, units),
         vocab_sum=v32(*(2,) * len(plane), rows, part_cols),
         vocab_traded=v32(3, rows, part_cols),
@@ -1071,23 +1102,22 @@
     return SimpleNamespace(**dict(zip(outputs, out))), low_bits
 
 
-def deliver_kernel(n_dp, *refs):
-    sources, targets, held, sem_in, sem_out = refs[:11], refs[11:28], refs[28:39], refs[39], refs[40]
-    loss, small, table, vocab, kv = held[:5]
-    (
-        loss_to, gain_one_to, bias_one_to, gain_two_to, bias_two_to, taps_to, rate_to,
-        table_to, vocab_to, key_to, value_to,
-    ) = targets[:11]
+def deliver_kernel(n_dp, n_passed, *refs):
+    n = n_passed + 2
+    sources, targets, held = refs[:n], refs[n : 2 * n + 5], refs[2 * n + 5 : 3 * n + 5]
+    sem_in, sem_out = refs[3 * n + 5 :]
     reads, writes = [], []
     for i, (source, buffer) in enumerate(zip(sources, held)):
         reads.append(pltpu.make_async_copy(source, buffer, sem_in.at[i]))
         reads[-1].start()
-    for i in range(5, 11):
+    for i in range(n_passed):
         reads[i].wait()
-        writes.append(pltpu.make_async_copy(held[i], targets[6 + i], sem_out.at[i]))
+        writes.append(pltpu.make_async_copy(held[i], targets[i], sem_out.at[i]))
         writes[-1].start()
-    for i in range(5):
-        reads[i].wait()
+    reads[n_passed].wait()
+    reads[n_passed + 1].wait()
+    loss, small = held[n_passed:]
+    loss_to, gain_one_to, bias_one_to, gain_two_to, bias_two_to, taps_to, rate_to = targets[n_passed:]
     slots = loss.shape[1]
     for u in range(loss.shape[0]):
         loss_to[:, pl.ds(u * slots, slots)] = loss[pl.ds(u, 1), :]
@@ -1100,18 +1130,6 @@
     for i, target in enumerate((gain_one_to, bias_one_to, gain_two_to, bias_two_to)):
         target[...] = mine[12 + i : 13 + i]
     rate_to[...] = small[pl.ds(16, 2), :]
-    table_to[...] = table[pl.ds(0, table_to.shape[0]), :][:, : table_to.shape[1]]
-    part_cols = vocab.shape[2]
-    vocab_here = vocab_to.shape[1]
-    last = (vocab_here + 255) // 256 * 256 - part_cols
-    for k in range(3):
-        vocab_to[:, pl.ds(k * part_cols, part_cols)] = vocab[k]
-    rest = vocab_here - 3 * part_cols
-    skip = 3 * part_cols - last
-    vocab_to[:, pl.ds(3 * part_cols, rest)] = vocab[3][:, skip : skip + rest]
-    half = key_to.shape[1]
-    key_to[...] = kv[:, pl.ds(0, half)]
-    value_to[...] = kv[:, pl.ds(half, half)]
     for copy in writes:
         copy.wait()
 
@@ -1148,48 +1166,43 @@
         token_lengths, memory_lengths, rate_groups, glance_mask, targets, n_dp,
     )
     vocab = result.vocab_out
-    summed = [result.query_out, result.kv_out, result.out_out, result.in_out, result.back_out]
+    summed = [
+        result.query_out, result.key_out, result.value_out, result.out_out, result.in_out,
+        result.back_out,
+    ]
     if low_bits:
         size = 1 << len(low_bits)
         groups = [list(range(g * size, (g + 1) * size)) for g in range(n_dp // size)]
         planes = [list(range(4 * g, 4 * g + 4)) for g in range(n_dp // 4)]
-        own_rows = model_width // n_dp
         vocab = lax.all_to_all(
-            vocab.reshape(4, own_rows, -1), "dp", 0, 0, axis_index_groups=planes, tiled=True
+            vocab.reshape(4, model_width // n_dp, -1), "dp", 0, 0, axis_index_groups=planes, tiled=True
         )
-        summed = [
+        *summed, rest = [
             lax.psum_scatter(s, "dp", scatter_dimension=0, axis_index_groups=groups, tiled=True)
-            for s in summed
+            for s in (*summed, result.rest_out)
         ]
-    grad_query, grad_kv, grad_out, grad_in, grad_back = summed
+        vocab = jnp.concatenate([*vocab, rest], axis=1)[:, : w_vocab.shape[1]]
     own = model_width // n_dp
     f32 = lambda *shape: jax.ShapeDtypeStruct(shape, F32)
     like = lambda x: jax.ShapeDtypeStruct(x.shape, F32)
-    handed = (
-        result.loss_out, result.small_out, result.table_out, vocab, grad_kv, grad_query, grad_out,
-        grad_in, grad_back, result.acoustic_out, result.memory_out,
-    )
+    passed = (result.memory_out, result.table_out, result.acoustic_out, vocab, *summed)
+    handed = (*passed, result.loss_out, result.small_out)
     (
-        token_loss, gain_1, bias_1, gain_2, bias_2, grad_taps, grad_rate, grad_table, grad_vocab,
-        grad_key, grad_value, grad_query, grad_out, grad_in, grad_back, grad_acoustic, grad_memory,
+        grad_memory, grad_table, grad_acoustic, grad_vocab, grad_query, grad_key, grad_value,
+        grad_out, grad_in, grad_back, token_loss, gain_1, bias_1, gain_2, bias_2, grad_taps, grad_rate,
     ) = pl.pallas_call(
-        partial(deliver_kernel, n_dp),
+        partial(deliver_kernel, n_dp, len(passed)),
         out_shape=[
+            *[like(x) for x in passed],
             f32(1, tok_rows),
             *[f32(1, own)] * 4,
             f32(fsmn_kernel.shape[0], own),
             f32(2, model_width),
-            f32(own, embedding.shape[0]),
-            f32(own, w_vocab.shape[1]),
-            *[f32(own, half)] * 2,
-            *[like(x) for x in (grad_query, grad_out, grad_in, grad_back)],
-            like(result.acoustic_out),
-            like(result.memory_out),
         ],
-        in_specs=[ANY] * 11,
-        out_specs=[VMEM] * 11 + [ANY] * 6,
+        in_specs=[ANY] * len(handed),
+        out_specs=[ANY] * len(passed) + [VMEM] * 7,
         scratch_shapes=[pltpu.VMEM(x.shape, F32) for x in handed]
-        + [pltpu.SemaphoreType.DMA((11,)), pltpu.SemaphoreType.DMA((11,))],
+        + [pltpu.SemaphoreType.DMA((len(handed),)), pltpu.SemaphoreType.DMA((len(handed),))],
         compiler_params=pltpu.CompilerParams(vmem_limit_bytes=60 << 20),
     )(*handed)
     return (

time: 140 us -> 133 us (0.950)
  Pallas kernels: 136 us -> 131 us
  local copies, waits for them, and re-layouts: 3.19 us -> 1.64 us
    pallas_call x1, Pallas kernels: 131 us -> 126 us  [decoder_call(): pl.pallas_call(kernel, out_shape=list(outputs.values()), in_specs=[spec f...]
    slice x1 -> x0, local copies, waits for them, and re-layouts: 1.55 us -> none  [decoder_call(): w_turned[main:]]
where the time goes in v7:
time: 133 us
  Pallas kernels  131 us (98%)
  local copies, waits for them, and re-layouts  1.64 us (1%)
    pallas_call x1, Pallas kernels, decoder_call(): pl.pallas_call(kernel, out_shape=list(outputs.values()), in_specs=[spec f...  126 us
    pallas_call x1, Pallas kernels, per_device(): pl.pallas_call(partial(deliver_kernel, n_dp, len(passed)), out_shape=[*[l...  4.57 us

profile of v7, /device:TPU:0, one launch (start us, length us, event | category | flops | bytes accessed | tf_op | source)
XLA Modules:
  0.0 133.0 jit_solution(15589498228326898950)
XLA Ops:
  0.7 1.6 %slice.3.refs_1_ = bf16[212,512]{1,0:T(8,128)(2,1)} slice(bf16[8404,512]{1,0:T(8,128)(2,1)} %refs_3_.1), slice={[8192:8404], [0:512]} | slice | bytes 434176 | tf_op jit(solution)/shard_map/slice | solution.py:965
  2.3 126.0 %shard_map.332 = (f32[2,128]{1,0:T(2,128)}, f32[24,512]{1,0:T(8,128)}, f32[32,4202]{1,0:T(8,128)}, f32[32,128]{1,0:T(8,128)}, f32[32,1024]{1,0:T(8,128)}, /*inde...) custom-call(bf16[256,512]{1,0:T(8,128)(2,1)} %refs_0_.1, ...), custom_call_target="tpu_custom_call" | custom-call | tf_op jit(solution)/shard_map/pallas_call | solution.py:1092
  128.3 4.6 %shard_map.333 = (f32[2048,256]{1,0:T(8,128)}, f32[32,8404]{1,0:T(8,128)}, f32[256,512]{1,0:T(8,128)}, f32[32,4202]{1,0:T(8,128)}, f32[32,256]{1,0:T(8,128)}, /*...) custom-call(f32[2048,256]{1,0:T(8,128)} %get-tuple-element.46.refs_0, ...), custom_call_target="tpu_custom_call" | custom-call | tf_op jit(solution)/shard_map/pallas_call | solution.py:1193

commit v8 on v7

--- a/solution.py
+++ b/solution.py
@@ -50,12 +50,16 @@
     return scale * (grad_hat - first - hat * second)
 
 
-def to_rows(columns):
+def side_by_side(columns):
     lane = lax.broadcasted_iota(jnp.int32, (columns[0].shape[0], 128), 1)
     tile = jnp.zeros(lane.shape, F32)
     for i, column in enumerate(columns):
         tile = jnp.where(lane == i, column, tile)
-    return tile.T[:8]
+    return tile
+
+
+def to_rows(columns):
+    return side_by_side(columns).T[:8]
 
 
 def to_columns(rows):
@@ -315,9 +319,12 @@
         tiles = main // 128
         step_tiles = 4
 
-        def step(j, carry):
-            top_m, picked = carry
-            col = pl.multiple_of(j * (step_tiles * 128), step_tiles * 128)
+        ids = main + lax.broadcasted_iota(jnp.int32, (1, 128), 1)
+        last = jnp.where(ids < vocab_here, dot_nt(top[0], w_rest[...]), NEG)
+        logits[tiles] = last
+        top_m, picked = last, jnp.where(ids == target, last, 0.0)
+        for j in range(tiles // step_tiles):
+            col = j * step_tiles * 128
             product = dot_nt(top[0], w_vocab[pl.ds(col, step_tiles * 128), :])
             for i in range(step_tiles):
                 tile = product[:, i * 128 : (i + 1) * 128]
@@ -325,13 +332,6 @@
                 logits[j * step_tiles + i] = tile
                 top_m = jnp.maximum(top_m, tile)
                 picked = picked + jnp.where(ids == target, tile, 0.0)
-            return top_m, picked
-
-        ids = main + lax.broadcasted_iota(jnp.int32, (1, 128), 1)
-        last = jnp.where(ids < vocab_here, dot_nt(top[0], w_rest[...]), NEG)
-        logits[tiles] = last
-        picked = jnp.where(ids == target, last, 0.0)
-        top_m, picked = lax.fori_loop(0, tiles // step_tiles, step, (last, picked))
         top_row = jnp.max(top_m, axis=1, keepdims=True)
 
         def add(j, total):
@@ -346,15 +346,10 @@
             jnp.sum(picked, axis=1, keepdims=True),
         )
 
-    def join(blocks):
-        top_value = blocks[0][0:1]
-        for b in blocks[1:]:
-            top_value = jnp.maximum(top_value, b[0:1])
-        total, picked = 0.0, 0.0
-        for b in blocks:
-            total = total + b[1:2] * jnp.exp(b[0:1] - top_value)
-            picked = picked + b[2:3]
-        return top_value + jnp.log(total), picked
+    def join(mine, theirs):
+        top_value = jnp.maximum(mine[0], theirs[0])
+        total = mine[1] * jnp.exp(mine[0] - top_value) + theirs[1] * jnp.exp(theirs[0] - top_value)
+        return top_value + jnp.log(total), mine[2] + theirs[2]
 
     def memory_block(u):
         at = rows(u)
@@ -459,14 +454,14 @@
     load_vocab.wait()
     w_rest[pl.ds(0, vocab_here - main), :] = w_vocab[pl.ds(main, vocab_here - main), :]
     own_local = local_targets(own_target)
-    stats[0] = to_rows(vocab_stats(own_local))
+    mine = vocab_stats(own_local)
+    stats[0] = side_by_side(mine)
     first_swap = swap(stats.at[0], stats_arrived.at[0], sibling)
     table_swap.wait()
     first_swap.wait()
-    log_total, picked = join([stats[0], stats_arrived[0]])
-    first_loss = (log_total - picked) * meta[0, 1:2, :]
-    blend_row = meta[0, 2:3, :] * meta[0, 1:2, :] / (1.0 + jnp.exp(math.log(V) - first_loss))
-    blend = to_columns(jnp.concatenate([blend_row] * 8, axis=0))[:, 0:1]
+    log_total, picked = join(mine, [stats_arrived[0, :, i : i + 1] for i in range(3)])
+    first_loss = (log_total - picked) * own_valid
+    blend = own_columns[:, 2:3] * own_valid / (1.0 + jnp.exp(math.log(V) - first_loss))
     for u in range(utterances):
         at = rows(u)
         wide_acoustic = acoustic[at, :].astype(F32)
@@ -475,21 +470,21 @@
 
     forward(True)
     token_swaps = [
-        swap(stream_three.at[core], gathered.at[j - 1, 0], {"dp": mate[j]}) for j in range(1, 4)
+        swap(stream_three.at[core], gathered.at[j - 1, 0], {"dp": mate[j]}) for j in (1, 2)
     ]
-    stats[1] = to_rows(vocab_stats(own_local))
+    mine = vocab_stats(own_local)
+    stats[1] = side_by_side(mine)
     stat_swap = swap(stats.at[1], stats_arrived.at[1], sibling)
+    for copy in token_swaps:
+        copy.wait()
+    part = slots // 2
+    relays = [
+        swap(gathered.at[0, 0, pl.ds(0, part)], gathered.at[2, 0, pl.ds(0, part)], {"dp": mate[2]}),
+        swap(gathered.at[1, 0, pl.ds(part, part)], gathered.at[2, 0, pl.ds(part, part)], {"dp": mate[1]}),
+    ]
+    share_swaps = [swap(gathered.at[j, 0], gathered.at[j, 1], sibling) for j in range(2)]
     stat_swap.wait()
-    log_total, picked = join([stats[1], stats_arrived[1]])
-    loss = (log_total - picked) * meta[0, 1:2, :]
-    for u in range(utterances):
-        r.loss_out[pl.ds(u, 1), :] = loss[:, u * slots : (u + 1) * slots]
-    meta[0] = jnp.where(
-        lax.broadcasted_iota(jnp.int32, (8, tokens), 0) == 3, log_total, meta[0]
-    )
-    meta_swaps = [swap(meta.at[0], meta.at[j], {"dp": mate[j]}) for j in range(1, 4)]
-
-    log_column = to_columns(meta[0])[:, 3:4]
+    log_column, picked = join(mine, [stats_arrived[1, :, i : i + 1] for i in range(3)])
 
     def slope(j, carry):
         col = pl.multiple_of(j * 128, 128)
@@ -499,13 +494,17 @@
         grad_logits[:, pl.ds(col, 128)] = grad.astype(BF16)
         return carry
 
-    lax.fori_loop(0, main // 128 + 1, slope, 0)
+    lax.fori_loop(0, main // 128 + 1, slope, 0, unroll=3)
     three_copies = []
     for u in range(utterances):
         sent[u] = dot_nn(grad_logits[rows(u), pl.ds(0, main)], w_vocab[pl.ds(0, main), :]) + dot_nn(
             grad_logits[rows(u), pl.ds(main, 128)], w_rest[...]
         )
         three_copies.append(swap(sent.at[u], arrived.at[u], sibling))
+    meta[0] = to_rows([own_target, own_valid, log_column, (log_column - picked) * own_valid])
+    meta_swaps = [swap(meta.at[0], meta.at[j], {"dp": mate[j]}) for j in range(1, 4)]
+    for u in range(utterances):
+        r.loss_out[pl.ds(u, 1), :] = meta[0, 3:4, u * slots : (u + 1) * slots]
 
     plan = Planner()
     steps_all = len(bits)
@@ -601,40 +600,19 @@
         source = getattr(r, "src_" + name)
         source[..., at] = product.reshape(source.shape[:-1] + (product.shape[1],))
 
-    copies = []
-    for u in range(utterances):
-        at = rows(u)
-        three_copies[u].wait()
-        three = sent[u] + arrived[u]
-        grad_three[u] = three
-        low = three.astype(BF16)
-        branch_low[at, :] = low
-        pre = (dot_nt(low, w_back[...]) * gelu_slope[at, :]).astype(BF16)
-        grad_pre[at, :] = pre
-        sent[utterances + u] = dot_nt(pre, w_in[...])
-        copies.append(swap(sent.at[utterances + u], arrived.at[utterances + u], sibling))
-    plan.run_until(4.0)
-    for name, left, right in (("back", branch_low, hidden), ("in", norm_low, grad_pre)):
-        left_turned = left[...].T
-        for start in sorted(s for n, s in chunks if n == name):
-            at = pl.ds(start, 512)
-            put(name, at, dot_nn(left_turned, right[:, at]))
-            plan.run_until(plan.now + 0.5)
-            plan.post(chunks[name, start])
-
     at_core = pl.ds(pl.multiple_of(core * slots, slots), slots)
     at_other = pl.ds(pl.multiple_of((1 - core) * slots, slots), slots)
-    share_swaps = []
-    for j in range(1, 4):
-        token_swaps[j - 1].wait()
-        share_swaps.append(swap(gathered.at[j - 1, 0], gathered.at[j - 1, 1], sibling))
-        top[j, at_core, :] = gathered[j - 1, 0].astype(BF16)
     base = pl.multiple_of(quarter * part_cols, part_cols)
     pieces = [(c, 256) for c in range(0, part_cols, 256)]
     for j in range(1, 4):
+        if j == 2:
+            for copy in relays:
+                copy.wait()
+            share_swaps.append(swap(gathered.at[2, 0], gathered.at[2, 1], sibling))
         meta_swaps[j - 1].wait()
         columns = to_columns(meta[j])
-        target, valid, log_total = local_targets(columns[:, 0:1]), columns[:, 1:2], columns[:, 3:4]
+        target, valid, log_total = local_targets(columns[:, 0:1]), columns[:, 1:2], columns[:, 2:3]
+        top[j, at_core, :] = gathered[j - 1, 0].astype(BF16)
         share_swaps[j - 1].wait()
         top[j, at_other, :] = gathered[j - 1, 1].astype(BF16)
         for col, cols in pieces:
@@ -642,10 +620,10 @@
             tile = dot_nt(top[j], w_vocab[pl.ds(base + col, cols), :])
             grad = (jnp.exp(tile - log_total) - jnp.where(ids == target, 1.0, 0.0)) * valid
             grad_others[pl.ds((j - 1) * tokens, tokens), pl.ds(col, cols)] = grad.astype(BF16)
-        plan.run_until(plan.now + 0.8)
     top_turned = r.top_turned
     for j in range(4):
         top_turned[:, pl.ds(j * tokens, tokens)] = top[j].T
+    plan.run_until(9.0)
     put("rest", slice(None), dot_nn(top_turned[:, pl.ds(0, tokens)], grad_logits[:, pl.ds(main, 128)]))
     starts = sorted(start for name, start in chunks if name == "vocab")
     for start, stop in zip(starts, starts[1:] + [part_cols]):
@@ -659,6 +637,27 @@
         plan.run_until(plan.now + 0.7)
         plan.post(chunks["vocab", start])
     plan.post(chunks["rest", 0])
+
+    copies = []
+    for u in range(utterances):
+        at = rows(u)
+        three_copies[u].wait()
+        three = sent[u] + arrived[u]
+        grad_three[u] = three
+        low = three.astype(BF16)
+        branch_low[at, :] = low
+        pre = (dot_nt(low, w_back[...]) * gelu_slope[at, :]).astype(BF16)
+        grad_pre[at, :] = pre
+        sent[utterances + u] = dot_nt(pre, w_in[...])
+        copies.append(swap(sent.at[utterances + u], arrived.at[utterances + u], sibling))
+    plan.run_until(plan.now + 3.0)
+    for name, left, right in (("back", branch_low, hidden), ("in", norm_low, grad_pre)):
+        left_turned = left[...].T
+        for start in sorted(s for n, s in chunks if n == name):
+            at = pl.ds(start, 512)
+            put(name, at, dot_nn(left_turned, right[:, at]))
+            plan.run_until(plan.now + 0.5)
+            plan.post(chunks[name, start])
 
     one_copies = []
     gain_2_total, bias_2_total = 0.0, 0.0
@@ -1038,8 +1037,8 @@
         grad_queries=v16(tokens, half),
         mem_arrived=v32(mem_rows // 256 * (width // 256), 256, 128),
         meta=v32(4, 8, tokens),
-        stats=v32(2, 8, tokens),
-        stats_arrived=v32(2, 8, tokens),
+        stats=v32(2, tokens, 128),
+        stats_arrived=v32(2, tokens, 128),
         sent=v32(2 * utterances, slots, width),
         arrived=v32(2 * utterances, slots, width),
         gathered=v32(3, 2, slots, width),
@@ -1107,15 +1106,23 @@
     sources, targets, held = refs[:n], refs[n : 2 * n + 5], refs[2 * n + 5 : 3 * n + 5]
     sem_in, sem_out = refs[3 * n + 5 :]
     reads, writes = [], []
-    for i, (source, buffer) in enumerate(zip(sources, held)):
-        reads.append(pltpu.make_async_copy(source, buffer, sem_in.at[i]))
+    pieces = []
+    for i in range(n):
+        rows = sources[i].shape[0]
+        count = 4 if rows >= 1024 else 1
+        for k in range(count):
+            at = pl.ds(k * (rows // count), rows // count)
+            pieces.append((i, at) if count > 1 else (i, None))
+    for k, (i, at) in enumerate(pieces):
+        source, buffer = (sources[i], held[i]) if at is None else (sources[i].at[at], held[i].at[at])
+        reads.append(pltpu.make_async_copy(source, buffer, sem_in.at[k]))
         reads[-1].start()
-    for i in range(n_passed):
-        reads[i].wait()
-        writes.append(pltpu.make_async_copy(held[i], targets[i], sem_out.at[i]))
-        writes[-1].start()
-    reads[n_passed].wait()
-    reads[n_passed + 1].wait()
+    for k, (i, at) in enumerate(pieces):
+        reads[k].wait()
+        if i < n_passed:
+            buffer, target = (held[i], targets[i]) if at is None else (held[i].at[at], targets[i].at[at])
+            writes.append(pltpu.make_async_copy(buffer, target, sem_out.at[k]))
+            writes[-1].start()
     loss, small = held[n_passed:]
     loss_to, gain_one_to, bias_one_to, gain_two_to, bias_two_to, taps_to, rate_to = targets[n_passed:]
     slots = loss.shape[1]
@@ -1202,7 +1209,7 @@
         in_specs=[ANY] * len(handed),
         out_specs=[ANY] * len(passed) + [VMEM] * 7,
         scratch_shapes=[pltpu.VMEM(x.shape, F32) for x in handed]
-        + [pltpu.SemaphoreType.DMA((len(handed),)), pltpu.SemaphoreType.DMA((len(handed),))],
+        + [pltpu.SemaphoreType.DMA((len(handed) + 3,)), pltpu.SemaphoreType.DMA((len(handed) + 3,))],
         compiler_params=pltpu.CompilerParams(vmem_limit_bytes=60 << 20),
     )(*handed)
     return (

time: 133 us -> 141 us (1.060)
  Pallas kernels: 131 us -> 139 us
    pallas_call x1, Pallas kernels: 126 us -> 134 us  [decoder_call(): pl.pallas_call(kernel, out_shape=list(outputs.values()), in_specs=[spec f...]
where the time goes in v8:
time: 141 us
  Pallas kernels  139 us (99%)
  local copies, waits for them, and re-layouts  1.64 us (1%)
    pallas_call x1, Pallas kernels, decoder_call(): pl.pallas_call(kernel, out_shape=list(outputs.values()), in_specs=[spec f...  134 us
    pallas_call x1, Pallas kernels, per_device(): pl.pallas_call(partial(deliver_kernel, n_dp, len(passed)), out_shape=[*[l...  5.14 us

profile of v8, /device:TPU:0, one launch (start us, length us, event | category | flops | bytes accessed | tf_op | source)
XLA Modules:
  0.0 141.3 jit_solution(3044359313368562299)
XLA Ops:
  0.7 1.6 %slice.3.refs_1_ = bf16[212,512]{1,0:T(8,128)(2,1)} slice(bf16[8404,512]{1,0:T(8,128)(2,1)} %refs_3_.1), slice={[8192:8404], [0:512]} | slice | bytes 434176 | tf_op jit(solution)/shard_map/slice | solution.py:964
  2.3 133.7 %shard_map.332 = (f32[2,128]{1,0:T(2,128)}, f32[24,512]{1,0:T(8,128)}, f32[32,4202]{1,0:T(8,128)}, f32[32,128]{1,0:T(8,128)}, f32[32,1024]{1,0:T(8,128)}, /*inde...) custom-call(bf16[256,512]{1,0:T(8,128)(2,1)} %refs_0_.1, ...), custom_call_target="tpu_custom_call" | custom-call | tf_op jit(solution)/shard_map/pallas_call | solution.py:1091
  136.0 5.1 %shard_map.333 = (f32[2048,256]{1,0:T(8,128)}, f32[32,8404]{1,0:T(8,128)}, f32[256,512]{1,0:T(8,128)}, f32[32,4202]{1,0:T(8,128)}, f32[32,256]{1,0:T(8,128)}, /*...) custom-call(f32[2048,256]{1,0:T(8,128)} %get-tuple-element.46.refs_0, ...), custom_call_target="tpu_custom_call" | custom-call | tf_op jit(solution)/shard_map/pallas_call | solution.py:1200

commit v9 on v8

--- a/solution.py
+++ b/solution.py
@@ -475,6 +475,24 @@
     mine = vocab_stats(own_local)
     stats[1] = side_by_side(mine)
     stat_swap = swap(stats.at[1], stats_arrived.at[1], sibling)
+    stat_swap.wait()
+    log_column, picked = join(mine, [stats_arrived[1, :, i : i + 1] for i in range(3)])
+
+    def slope(j, carry):
+        col = pl.multiple_of(j * 128, 128)
+        ids = col + lax.broadcasted_iota(jnp.int32, (1, 128), 1)
+        onehot = jnp.where(ids == own_local, 1.0, 0.0)
+        grad = (jnp.exp(logits[j] - log_column) - onehot) * own_valid
+        grad_logits[:, pl.ds(col, 128)] = grad.astype(BF16)
+        return carry
+
+    lax.fori_loop(0, main // 128 + 1, slope, 0, unroll=3)
+    three_copies = []
+    for u in range(utterances):
+        sent[u] = dot_nn(grad_logits[rows(u), pl.ds(0, main)], w_vocab[pl.ds(0, main), :]) + dot_nn(
+            grad_logits[rows(u), pl.ds(main, 128)], w_rest[...]
+        )
+        three_copies.append(swap(sent.at[u], arrived.at[u], sibling))
     for copy in token_swaps:
         copy.wait()
     part = slots // 2
@@ -483,24 +501,6 @@
         swap(gathered.at[1, 0, pl.ds(part, part)], gathered.at[2, 0, pl.ds(part, part)], {"dp": mate[1]}),
     ]
     share_swaps = [swap(gathered.at[j, 0], gathered.at[j, 1], sibling) for j in range(2)]
-    stat_swap.wait()
-    log_column, picked = join(mine, [stats_arrived[1, :, i : i + 1] for i in range(3)])
-
-    def slope(j, carry):
-        col = pl.multiple_of(j * 128, 128)
-        ids = col + lax.broadcasted_iota(jnp.int32, (1, 128), 1)
-        onehot = jnp.where(ids == own_local, 1.0, 0.0)
-        grad = (jnp.exp(logits[j] - log_column) - onehot) * own_valid
-        grad_logits[:, pl.ds(col, 128)] = grad.astype(BF16)
-        return carry
-
-    lax.fori_loop(0, main // 128 + 1, slope, 0, unroll=3)
-    three_copies = []
-    for u in range(utterances):
-        sent[u] = dot_nn(grad_logits[rows(u), pl.ds(0, main)], w_vocab[pl.ds(0, main), :]) + dot_nn(
-            grad_logits[rows(u), pl.ds(main, 128)], w_rest[...]
-        )
-        three_copies.append(swap(sent.at[u], arrived.at[u], sibling))
     meta[0] = to_rows([own_target, own_valid, log_column, (log_column - picked) * own_valid])
     meta_swaps = [swap(meta.at[0], meta.at[j], {"dp": mate[j]}) for j in range(1, 4)]
     for u in range(utterances):
@@ -599,6 +599,27 @@
     def put(name, at, product):
         source = getattr(r, "src_" + name)
         source[..., at] = product.reshape(source.shape[:-1] + (product.shape[1],))
+
+    copies = []
+    for u in range(utterances):
+        at = rows(u)
+        three_copies[u].wait()
+        three = sent[u] + arrived[u]
+        grad_three[u] = three
+        low = three.astype(BF16)
+        branch_low[at, :] = low
+        pre = (dot_nt(low, w_back[...]) * gelu_slope[at, :]).astype(BF16)
+        grad_pre[at, :] = pre
+        sent[utterances + u] = dot_nt(pre, w_in[...])
+        copies.append(swap(sent.at[utterances + u], arrived.at[utterances + u], sibling))
+    plan.run_until(plan.now + 8.0)
+    for name, left, right in (("back", branch_low, hidden), ("in", norm_low, grad_pre)):
+        left_turned = left[...].T
+        for start in sorted(s for n, s in chunks if n == name):
+            at = pl.ds(start, 512)
+            put(name, at, dot_nn(left_turned, right[:, at]))
+            plan.run_until(plan.now + 0.5)
+            plan.post(chunks[name, start])
 
     at_core = pl.ds(pl.multiple_of(core * slots, slots), slots)
     at_other = pl.ds(pl.multiple_of((1 - core) * slots, slots), slots)
@@ -623,7 +644,7 @@
     top_turned = r.top_turned
     for j in range(4):
         top_turned[:, pl.ds(j * tokens, tokens)] = top[j].T
-    plan.run_until(9.0)
+    plan.run_until(plan.now + 4.0)
     put("rest", slice(None), dot_nn(top_turned[:, pl.ds(0, tokens)], grad_logits[:, pl.ds(main, 128)]))
     starts = sorted(start for name, start in chunks if name == "vocab")
     for start, stop in zip(starts, starts[1:] + [part_cols]):
@@ -637,27 +658,6 @@
         plan.run_until(plan.now + 0.7)
         plan.post(chunks["vocab", start])
     plan.post(chunks["rest", 0])
-
-    copies = []
-    for u in range(utterances):
-        at = rows(u)
-        three_copies[u].wait()
-        three = sent[u] + arrived[u]
-        grad_three[u] = three
-        low = three.astype(BF16)
-        branch_low[at, :] = low
-        pre = (dot_nt(low, w_back[...]) * gelu_slope[at, :]).astype(BF16)
-        grad_pre[at, :] = pre
-        sent[utterances + u] = dot_nt(pre, w_in[...])
-        copies.append(swap(sent.at[utterances + u], arrived.at[utterances + u], sibling))
-    plan.run_until(plan.now + 3.0)
-    for name, left, right in (("back", branch_low, hidden), ("in", norm_low, grad_pre)):
-        left_turned = left[...].T
-        for start in sorted(s for n, s in chunks if n == name):
-            at = pl.ds(start, 512)
-            put(name, at, dot_nn(left_turned, right[:, at]))
-            plan.run_until(plan.now + 0.5)
-            plan.post(chunks[name, start])
 
     one_copies = []
     gain_2_total, bias_2_total = 0.0, 0.0
@@ -883,7 +883,7 @@
     else:
         lax.fori_loop(1, pieces, lambda p, c: (table_piece(p, False), c)[1], 0)
     table_swap = swap(table_out, table_theirs, sibling)
-    plan.run_until(plan.now + 3.0)
+    plan.run_until(plan.now + 8.0)
     table_swap.wait()
     whole_table = r.whole_table
     whole_table[...] = (
@@ -1106,23 +1106,15 @@
     sources, targets, held = refs[:n], refs[n : 2 * n + 5], refs[2 * n + 5 : 3 * n + 5]
     sem_in, sem_out = refs[3 * n + 5 :]
     reads, writes = [], []
-    pieces = []
-    for i in range(n):
-        rows = sources[i].shape[0]
-        count = 4 if rows >= 1024 else 1
-        for k in range(count):
-            at = pl.ds(k * (rows // count), rows // count)
-            pieces.append((i, at) if count > 1 else (i, None))
-    for k, (i, at) in enumerate(pieces):
-        source, buffer = (sources[i], held[i]) if at is None else (sources[i].at[at], held[i].at[at])
-        reads.append(pltpu.make_async_copy(source, buffer, sem_in.at[k]))
+    for i, (source, buffer) in enumerate(zip(sources, held)):
+        reads.append(pltpu.make_async_copy(source, buffer, sem_in.at[i]))
         reads[-1].start()
-    for k, (i, at) in enumerate(pieces):
-        reads[k].wait()
-        if i < n_passed:
-            buffer, target = (held[i], targets[i]) if at is None else (held[i].at[at], targets[i].at[at])
-            writes.append(pltpu.make_async_copy(buffer, target, sem_out.at[k]))
-            writes[-1].start()
+    for i in range(n_passed):
+        reads[i].wait()
+        writes.append(pltpu.make_async_copy(held[i], targets[i], sem_out.at[i]))
+        writes[-1].start()
+    reads[n_passed].wait()
+    reads[n_passed + 1].wait()
     loss, small = held[n_passed:]
     loss_to, gain_one_to, bias_one_to, gain_two_to, bias_two_to, taps_to, rate_to = targets[n_passed:]
     slots = loss.shape[1]
@@ -1209,7 +1201,7 @@
         in_specs=[ANY] * len(handed),
         out_specs=[ANY] * len(passed) + [VMEM] * 7,
         scratch_shapes=[pltpu.VMEM(x.shape, F32) for x in handed]
-        + [pltpu.SemaphoreType.DMA((len(handed) + 3,)), pltpu.SemaphoreType.DMA((len(handed) + 3,))],
+        + [pltpu.SemaphoreType.DMA((len(handed),)), pltpu.SemaphoreType.DMA((len(handed),))],
         compiler_params=pltpu.CompilerParams(vmem_limit_bytes=60 << 20),
     )(*handed)
     return (

time: 141 us -> 129 us (0.915); the launches traced: 141 us -> 127 us
  Pallas kernels: 139 us -> 125 us
    pallas_call x1, Pallas kernels: 134 us -> 120 us  [decoder_call(): pl.pallas_call(kernel, out_shape=list(outputs.values()), in_specs=[spec f...]
where the time goes in v9:
time: 129 us; the launch traced here: 127 us
  Pallas kernels  125 us (97%)
  local copies, waits for them, and re-layouts  1.64 us (1%)
    pallas_call x1, Pallas kernels, decoder_call(): pl.pallas_call(kernel, out_shape=list(outputs.values()), in_specs=[spec f...  120 us
    pallas_call x1, Pallas kernels, per_device(): pl.pallas_call(partial(deliver_kernel, n_dp, len(passed)), out_shape=[*[l...  4.57 us

profile of v9, /device:TPU:0, one launch (start us, length us, event | category | flops | bytes accessed | tf_op | source)
XLA Modules:
  0.0 127.3 jit_solution(16707268198454689025)
XLA Ops:
  0.7 1.6 %slice.3.refs_1_ = bf16[212,512]{1,0:T(8,128)(2,1)} slice(bf16[8404,512]{1,0:T(8,128)(2,1)} %refs_3_.1), slice={[8192:8404], [0:512]} | slice | bytes 434176 | tf_op jit(solution)/shard_map/slice | solution.py:964
  2.3 120.3 %shard_map.332 = (f32[2,128]{1,0:T(2,128)}, f32[24,512]{1,0:T(8,128)}, f32[32,4202]{1,0:T(8,128)}, f32[32,128]{1,0:T(8,128)}, f32[32,1024]{1,0:T(8,128)}, /*inde...) custom-call(bf16[256,512]{1,0:T(8,128)(2,1)} %refs_0_.1, ...), custom_call_target="tpu_custom_call" | custom-call | tf_op jit(solution)/shard_map/pallas_call | solution.py:1091
  122.6 4.6 %shard_map.333 = (f32[2048,256]{1,0:T(8,128)}, f32[32,8404]{1,0:T(8,128)}, f32[256,512]{1,0:T(8,128)}, f32[32,4202]{1,0:T(8,128)}, f32[32,256]{1,0:T(8,128)}, /*...) custom-call(f32[2048,256]{1,0:T(8,128)} %get-tuple-element.46.refs_0, ...), custom_call_target="tpu_custom_call" | custom-call | tf_op jit(solution)/shard_map/pallas_call | solution.py:1192

commit v10 on v9

--- a/solution.py
+++ b/solution.py
@@ -69,15 +69,20 @@
 class Planner:
     RATE = 0.045e6
     HOP = 1.5
-    BACKLOG = 3.0
+    AHEAD = 4.0
+    LINK_MOST = 2
+    MOST = 6
 
     def __init__(self):
         self.now = 0.0
         self.free = {}
         self.flying = []
-        self.waiting = []
+        self.ready = []
         self.started = []
         self.count = 0
+
+    def way_left(self, item, step):
+        return sum(size for _, size in item.steps[step:]) / self.RATE + self.HOP * len(item.steps[step:])
 
     def launch(self, item, step):
         link, size = item.steps[step]
@@ -86,43 +91,51 @@
         copy = item.send(step)
         self.started.append(copy)
         self.count += 1
-        self.flying.append((self.free[link] + self.HOP, self.count, item, step, copy))
-
-    def release(self):
-        kept = []
-        for item in self.waiting:
-            link = item.steps[0][0]
-            if self.free.get(link, 0.0) - self.now < self.BACKLOG:
-                self.launch(item, 0)
-            else:
-                kept.append(item)
-        self.waiting = kept
+        self.flying.append((self.free[link] + self.HOP, self.count, item, step, copy, link))
+
+    def pump(self):
+        while True:
+            live = [f[5] for f in self.flying if f[0] - self.HOP > self.now]
+            if len(live) >= self.MOST:
+                return
+            best = None
+            for item, step in self.ready:
+                link = item.steps[step][0]
+                if live.count(link) >= self.LINK_MOST or self.free.get(link, 0.0) - self.now > self.AHEAD:
+                    continue
+                key = (live.count(link), -self.way_left(item, step))
+                if best is None or key < best[0]:
+                    best = (key, item, step)
+            if best is None:
+                return
+            self.ready.remove(best[1:])
+            self.launch(*best[1:])
 
     def post(self, *items):
-        self.waiting += items
-        self.release()
+        self.ready += [(item, 0) for item in items]
+        self.pump()
 
     def run_until(self, time):
-        while self.flying or self.waiting:
+        while self.flying or self.ready:
             if not self.flying:
-                self.now = max(self.now, min(self.free[i.steps[0][0]] for i in self.waiting))
-                self.release()
+                self.now = max(self.now, min(self.free[i.steps[k][0]] for i, k in self.ready))
+                self.pump()
                 continue
             first = min(self.flying, key=lambda f: f[:2])
             if first[0] > time:
                 break
             self.flying.remove(first)
             self.now = max(self.now, first[0])
-            _, _, item, step, copy = first
+            _, _, item, step, copy, _ = first
             item.take(step, copy)
             if step + 1 < len(item.steps):
-                self.launch(item, step + 1)
+                self.ready.append((item, step + 1))
             elif item.follow is not None:
-                self.launch(item.follow, 0)
-            self.release()
+                self.ready.append((item.follow, 0))
+            self.pump()
         if time != math.inf:
             self.now = max(self.now, time)
-        self.release()
+        self.pump()
 
     def finish(self):
         self.run_until(math.inf)
@@ -655,7 +668,7 @@
                 top_turned[:, pl.ds(tokens, 3 * tokens)], grad_others[:, pl.ds(col, cols)]
             )
             put("vocab", pl.ds(col, cols), product)
-        plan.run_until(plan.now + 0.7)
+        plan.run_until(plan.now + 0.4)
         plan.post(chunks["vocab", start])
     plan.post(chunks["rest", 0])
 
@@ -907,14 +920,13 @@
 def chunk_list(part_cols, width, bits, low_bits, sizes):
     turned = [bits[1], bits[0]] + bits[2:]
     listing = []
-    for start in range(0, part_cols, 512):
-        listing.append(("vocab", start, 512, [b for b in bits if b > 1]))
-    listing.append(("rest", 0, 128, bits))
-    for name, order in (("back", turned), ("in", bits)):
-        for start in range(0, sizes.units, 512):
-            if name == "in" and start:
-                order = [bits[2], bits[0], bits[1]] + bits[3:]
-            listing.append((name, start, 512, order))
+    for start in range(0, part_cols, 256):
+        listing.append(("vocab", start, 256, [b for b in bits if b > 1]))
+    for start in range(0, sizes.units, 512):
+        listing.append(("back", start, 512, turned))
+    for start in range(0, sizes.units, 512):
+        listing.append(("in", start, 512, bits))
+    listing.append(("rest", 0, 128, turned))
     listing.append(("out", 0, sizes.half, turned))
     listing.append(("query", 0, sizes.half, bits))
     for k, start in enumerate(range(0, 2 * sizes.half, 256)):

time: 129 us -> 139 us (1.078)
  Pallas kernels: 125 us -> 135 us
    pallas_call x1, Pallas kernels: 120 us -> 130 us  [decoder_call(): pl.pallas_call(kernel, out_shape=list(outputs.values()), in_specs=[spec f...]
where the time goes in v10:
time: 139 us; the launch traced here: 137 us
  Pallas kernels  135 us (97%)
  local copies, waits for them, and re-layouts  1.64 us (1%)
    pallas_call x1, Pallas kernels, decoder_call(): pl.pallas_call(kernel, out_shape=list(outputs.values()), in_specs=[spec f...  130 us
    pallas_call x1, Pallas kernels, per_device(): pl.pallas_call(partial(deliver_kernel, n_dp, len(passed)), out_shape=[*[l...  4.57 us

profile of v10, /device:TPU:0, one launch (start us, length us, event | category | flops | bytes accessed | tf_op | source)
XLA Modules:
  0.0 137.3 jit_solution(5567837544304445642)
XLA Ops:
  0.7 1.6 %slice.3.refs_1_ = bf16[212,512]{1,0:T(8,128)(2,1)} slice(bf16[8404,512]{1,0:T(8,128)(2,1)} %refs_3_.1), slice={[8192:8404], [0:512]} | slice | bytes 434176 | tf_op jit(solution)/shard_map/slice | solution.py:976
  2.3 130.2 %shard_map.332 = (f32[2,128]{1,0:T(2,128)}, f32[24,512]{1,0:T(8,128)}, f32[32,4202]{1,0:T(8,128)}, f32[32,128]{1,0:T(8,128)}, f32[32,1024]{1,0:T(8,128)}, /*inde...) custom-call(bf16[256,512]{1,0:T(8,128)(2,1)} %refs_0_.1, ...), custom_call_target="tpu_custom_call" | custom-call | tf_op jit(solution)/shard_map/pallas_call | solution.py:1103
  132.5 4.6 %shard_map.333 = (f32[2048,256]{1,0:T(8,128)}, f32[32,8404]{1,0:T(8,128)}, f32[256,512]{1,0:T(8,128)}, f32[32,4202]{1,0:T(8,128)}, f32[32,256]{1,0:T(8,128)}, /*...) custom-call(f32[2048,256]{1,0:T(8,128)} %get-tuple-element.46.refs_0, ...), custom_call_target="tpu_custom_call" | custom-call | tf_op jit(solution)/shard_map/pallas_call | solution.py:1204

commit v11 on v9

--- a/solution.py
+++ b/solution.py
@@ -69,7 +69,7 @@
 class Planner:
     RATE = 0.045e6
     HOP = 1.5
-    BACKLOG = 3.0
+    BACKLOG = 6.0
 
     def __init__(self):
         self.now = 0.0
@@ -909,16 +909,14 @@
     listing = []
     for start in range(0, part_cols, 512):
         listing.append(("vocab", start, 512, [b for b in bits if b > 1]))
-    listing.append(("rest", 0, 128, bits))
-    for name, order in (("back", turned), ("in", bits)):
-        for start in range(0, sizes.units, 512):
-            if name == "in" and start:
-                order = [bits[2], bits[0], bits[1]] + bits[3:]
-            listing.append((name, start, 512, order))
-    listing.append(("out", 0, sizes.half, turned))
+    for name in ("back", "in"):
+        for k, start in enumerate(range(0, sizes.units, 512)):
+            listing.append((name, start, 512, [bits, turned][k % 2]))
+    listing.append(("rest", 0, 128, turned))
+    listing.append(("out", 0, sizes.half, bits))
     listing.append(("query", 0, sizes.half, bits))
-    for k, start in enumerate(range(0, 2 * sizes.half, 256)):
-        listing.append(("kv", start, 256, [bits, turned][k % 2]))
+    for start in range(0, 2 * sizes.half, 256):
+        listing.append(("kv", start, 256, turned))
     return listing
 
 

time: 129 us -> 131 us (1.016); the launches traced: 127 us -> 131 us
  Pallas kernels: 125 us -> 128 us
    pallas_call x1, Pallas kernels: 120 us -> 124 us  [decoder_call(): pl.pallas_call(kernel, out_shape=list(outputs.values()), in_specs=[spec f...]
where the time goes in v11:
time: 131 us
  Pallas kernels  128 us (98%)
  local copies, waits for them, and re-layouts  1.64 us (1%)
    pallas_call x1, Pallas kernels, decoder_call(): pl.pallas_call(kernel, out_shape=list(outputs.values()), in_specs=[spec f...  124 us
    pallas_call x1, Pallas kernels, per_device(): pl.pallas_call(partial(deliver_kernel, n_dp, len(passed)), out_shape=[*[l...  4.57 us

profile of v11, /device:TPU:0, one launch (start us, length us, event | category | flops | bytes accessed | tf_op | source)
XLA Modules:
  0.0 130.7 jit_solution(1974182743950328257)
XLA Ops:
  0.7 1.6 %slice.3.refs_1_ = bf16[212,512]{1,0:T(8,128)(2,1)} slice(bf16[8404,512]{1,0:T(8,128)(2,1)} %refs_3_.1), slice={[8192:8404], [0:512]} | slice | bytes 434176 | tf_op jit(solution)/shard_map/slice | solution.py:962
  2.3 123.6 %shard_map.332 = (f32[2,128]{1,0:T(2,128)}, f32[24,512]{1,0:T(8,128)}, f32[32,4202]{1,0:T(8,128)}, f32[32,128]{1,0:T(8,128)}, f32[32,1024]{1,0:T(8,128)}, /*inde...) custom-call(bf16[256,512]{1,0:T(8,128)(2,1)} %refs_0_.1, ...), custom_call_target="tpu_custom_call" | custom-call | tf_op jit(solution)/shard_map/pallas_call | solution.py:1089
  125.9 4.6 %shard_map.333 = (f32[2048,256]{1,0:T(8,128)}, f32[32,8404]{1,0:T(8,128)}, f32[256,512]{1,0:T(8,128)}, f32[32,4202]{1,0:T(8,128)}, f32[32,256]{1,0:T(8,128)}, /*...) custom-call(f32[2048,256]{1,0:T(8,128)} %get-tuple-element.46.refs_0, ...), custom_call_target="tpu_custom_call" | custom-call | tf_op jit(solution)/shard_map/pallas_call | solution.py:1190

commit v12 on v9

--- a/solution.py
+++ b/solution.py
@@ -171,14 +171,14 @@
     one_low, queries, probs, mixed = r.one_low, r.queries, r.probs, r.mixed
     norm_low, hidden, gelu_slope, top = r.norm_low, r.hidden, r.gelu_slope, r.top
     logits, grad_logits, grad_others = r.logits, r.grad_logits, r.grad_others
-    taken_mine, taken_theirs = r.taken_mine, r.taken_theirs
+    taken_mine, taken_theirs = r.grad_three, r.taken_theirs
     grad_three, grad_two, branch_low = r.grad_three, r.grad_two, r.branch_low
     grad_pre, att_low, grad_queries = r.grad_pre, r.att_low, r.grad_queries
     mem_arrived, meta, stats, stats_arrived = r.mem_arrived, r.meta, r.stats, r.stats_arrived
     sent, arrived, gathered = r.sent, r.arrived, r.gathered
     small_sent, small_arrived = r.small_sent, r.small_arrived
     terms, term_blocks, term_arrived = grad_three, r.term_blocks, r.term_arrived
-    onehot_lo, table_theirs, table_out = r.onehot_lo, r.table_theirs, r.table_mine
+    onehot_lo, table_theirs, whole_table = r.onehot_lo, r.table_theirs, r.whole_table
     swap_send, swap_recv, load_sem = r.swap_send, r.swap_recv, r.load_sem
 
     utterances, slots = targets.shape
@@ -238,8 +238,17 @@
     load_vocab = load(r.w_vocab_hbm, w_vocab)
     w_rest = r.w_rest
     w_rest[...] = jnp.zeros(w_rest.shape, BF16)
+    rest_rows = (table_rows - mains) // 16 * 16
     r.table_rest[...] = jnp.zeros(r.table_rest.shape, BF16)
-    r.table_rest[pl.ds(0, table_rows - mains), :] = r.table_tail[...]
+    load_rest = load(table.at[pl.ds(mains, rest_rows), :], r.table_rest.at[pl.ds(0, rest_rows), :])
+    r.table_rest[pl.ds(rest_rows, table_rows - mains - rest_rows), :] = r.table_tail[...]
+
+    stores = []
+
+    def store(source, target):
+        copy = pltpu.make_async_copy(source, target, r.store_sem.at[len(stores)])
+        copy.start()
+        stores.append(copy)
 
     swaps = []
 
@@ -307,6 +316,7 @@
             table_loads.append(load_table(k + 2))
 
     def look_up_rest():
+        load_rest.wait()
         part = look_up(mains, r.table_rest.shape[0], core == 0, r.table_rest[...])
         for u in range(utterances):
             taken_mine[u] = taken_mine[u] + part[u * slots : (u + 1) * slots]
@@ -315,7 +325,7 @@
         local = target_column.astype(jnp.int32) - core * vocab_here
         return jnp.where((local >= 0) & (local < vocab_here), local, -1)
 
-    def vocab_stats(target):
+    def vocab_stats(target, keep=False):
         tiles = main // 128
         step_tiles = 4
 
@@ -336,7 +346,10 @@
 
         def add(j, total):
             for i in range(3):
-                total = total + jnp.exp(logits[3 * j + i] - top_row)
+                raised = jnp.exp(logits[3 * j + i] - top_row)
+                if keep:
+                    logits[3 * j + i] = raised
+                total = total + raised
             return total
 
         total = lax.fori_loop(0, (tiles + 1) // 3, add, jnp.zeros((tokens, 128), F32))
@@ -472,17 +485,19 @@
     token_swaps = [
         swap(stream_three.at[core], gathered.at[j - 1, 0], {"dp": mate[j]}) for j in (1, 2)
     ]
-    mine = vocab_stats(own_local)
+    mine = vocab_stats(own_local, keep=True)
     stats[1] = side_by_side(mine)
     stat_swap = swap(stats.at[1], stats_arrived.at[1], sibling)
     stat_swap.wait()
     log_column, picked = join(mine, [stats_arrived[1, :, i : i + 1] for i in range(3)])
 
+    factor = jnp.exp(mine[0] - log_column) * own_valid
+    valid_local = jnp.where(own_valid > 0.0, own_local, -1)
+
     def slope(j, carry):
         col = pl.multiple_of(j * 128, 128)
         ids = col + lax.broadcasted_iota(jnp.int32, (1, 128), 1)
-        onehot = jnp.where(ids == own_local, 1.0, 0.0)
-        grad = (jnp.exp(logits[j] - log_column) - onehot) * own_valid
+        grad = logits[j] * factor - jnp.where(ids == valid_local, 1.0, 0.0)
         grad_logits[:, pl.ds(col, 128)] = grad.astype(BF16)
         return carry
 
@@ -504,20 +519,29 @@
     meta[0] = to_rows([own_target, own_valid, log_column, (log_column - picked) * own_valid])
     meta_swaps = [swap(meta.at[0], meta.at[j], {"dp": mate[j]}) for j in range(1, 4)]
     for u in range(utterances):
-        r.loss_out[pl.ds(u, 1), :] = meta[0, 3:4, u * slots : (u + 1) * slots]
+        r.loss_sum[pl.ds(u, 1), :] = meta[0, 3:4, u * slots : (u + 1) * slots]
+    store(r.loss_sum, r.loss_out)
 
     plan = Planner()
     steps_all = len(bits)
     scatter_send, scatter_recv = r.scatter_send, r.scatter_recv
 
+    vocab_parts = []
+
+    def vocab_done():
+        vocab_parts.append(1)
+        if len(vocab_parts) == 1 + part_cols // 512:
+            store(r.vocab_whole, r.vocab_out)
+
     def make_chunk(index):
         name, start, cols, order = chunk_list(part_cols, width, bits, low_bits, r)[index]
         source, landing = getattr(r, "src_" + name), r.landing[index]
+        out_start = start
         if name == "kv":
-            out, out_start = (r.key_out, r.value_out)[start // cols], 0
+            out, final = ((r.key_sum, r.key_out), (r.value_sum, r.value_out))[start // cols]
+            out_start = 0
         else:
-            out = r.vocab_sum if name == "vocab" and not low_bits else getattr(r, name + "_out")
-            out_start = start
+            out, final = getattr(r, name + "_sum"), getattr(r, name + "_out")
         rows_here = source.shape[-2]
 
         def pick(step, which):
@@ -548,10 +572,14 @@
             at = pl.ds(out_start, cols)
             if step < len(order) - 1:
                 got[...] = got[...] + ref[where]
-            elif name == "vocab":
-                out[..., at] = got[...] + ref[where]
-            else:
-                out[:, at] = got[...] + ref[where]
+                return
+            out[..., at] = got[...] + ref[where]
+            if low_bits or name not in ("vocab", "rest"):
+                store(out.at[..., at], final.at[..., at])
+            elif name == "rest":
+                rest = vocab_here - main
+                r.vocab_whole[:, pl.ds(main, rest)] = out[...][:, :rest]
+                vocab_done()
 
         steps = [
             (link_of(b, bits), rows_here * cols * 4 * 2 ** (steps_all - 1 - s))
@@ -584,9 +612,10 @@
             copies.wait_recv()
             for j in range(1, 4):
                 there = pl.multiple_of(lax.rem(mate[j], 4) * part_cols + start, 128)
-                r.vocab_out[:, pl.ds(there, cols)] = traded[j - 1, :, at]
+                r.vocab_whole[:, pl.ds(there, cols)] = traded[j - 1, :, at]
             here = pl.multiple_of(base + start, 128)
-            r.vocab_out[:, pl.ds(here, cols)] = summed[quarter // 2, lax.rem(quarter, 2), :, at]
+            r.vocab_whole[:, pl.ds(here, cols)] = summed[quarter // 2, lax.rem(quarter, 2), :, at]
+            vocab_done()
 
         return Chunk([(0, 2 * r.src_vocab.shape[-2] * cols * 4)], send, take)
 
@@ -632,14 +661,16 @@
             share_swaps.append(swap(gathered.at[2, 0], gathered.at[2, 1], sibling))
         meta_swaps[j - 1].wait()
         columns = to_columns(meta[j])
-        target, valid, log_total = local_targets(columns[:, 0:1]), columns[:, 1:2], columns[:, 2:3]
+        valid = columns[:, 1:2] > 0.0
+        target = jnp.where(valid, local_targets(columns[:, 0:1]), -1)
+        log_total = jnp.where(valid, columns[:, 2:3], -NEG)
         top[j, at_core, :] = gathered[j - 1, 0].astype(BF16)
         share_swaps[j - 1].wait()
         top[j, at_other, :] = gathered[j - 1, 1].astype(BF16)
         for col, cols in pieces:
             ids = base + col + lax.broadcasted_iota(jnp.int32, (1, cols), 1)
             tile = dot_nt(top[j], w_vocab[pl.ds(base + col, cols), :])
-            grad = (jnp.exp(tile - log_total) - jnp.where(ids == target, 1.0, 0.0)) * valid
+            grad = jnp.exp(tile - log_total) - jnp.where(ids == target, 1.0, 0.0)
             grad_others[pl.ds((j - 1) * tokens, tokens), pl.ds(col, cols)] = grad.astype(BF16)
     top_turned = r.top_turned
     for j in range(4):
@@ -785,13 +816,16 @@
 
     def small_take(step, copy):
         copy.wait_recv()
+        if step + 1 == len(small_peers):
+            copy.wait_send()
+            plan.started = [c for c in plan.started if c is not copy]
         if step + 1 < len(small_peers):
             small_sent[step + 1] = small_sent[step] + small_arrived[step]
         else:
-            r.small_out[pl.ds(0, 16), :] = small_sent[step, pl.ds(0, 16), :]
-            r.small_out[pl.ds(16, 8), :] = (
+            small_sent[step, pl.ds(16, 8), :] = (
                 small_sent[step, pl.ds(16, 8), :] + small_arrived[step, pl.ds(16, 8), :]
             )
+            store(small_sent.at[step], r.small_out)
 
     small_links = [link_of(b, bits) for b in low_bits + bits] + ["core"]
     plan.post(Chunk([(l, 24 * width * 4) for l in small_links], small_send, small_take))
@@ -828,13 +862,6 @@
 
     term_arrived[me] = term_blocks[me]
     lax.fori_loop(1, n_dp, term_start, 0)
-    stores = []
-
-    def store(source, target):
-        copy = pltpu.make_async_copy(source, target, r.store_sem.at[len(stores)])
-        copy.start()
-        stores.append(copy)
-
     store(stream_one, r.acoustic_out)
     for u in range(utterances):
         mem_copies[u].wait()
@@ -848,7 +875,7 @@
     plan.run_until(plan.now + 8.0)
     lax.fori_loop(1, n_dp, term_wait, 0)
     per_piece = 512 // slots
-    blocks_hi = table_out.shape[1] // 256
+    blocks_hi = (table_rows + 255) // 256
     batch = 4
 
     def table_piece(p, fresh):
@@ -868,11 +895,10 @@
             for i, hi in enumerate(here):
                 top_part = product[2 * i * feature_rows : (2 * i + 1) * feature_rows]
                 low_part = product[(2 * i + 1) * feature_rows : (2 * i + 2) * feature_rows]
-                at = pl.ds(hi * 256, 256)
-                if fresh:
-                    table_out[:, at] = top_part + low_part
-                else:
-                    table_out[:, at] = table_out[:, at] + (top_part + low_part)
+                cols = min(256, table_rows - hi * 256)
+                at = pl.ds(hi * 256, cols)
+                found = (top_part + low_part)[:features, :cols]
+                whole_table[:, at] = found if fresh else whole_table[:, at] + found
 
     pieces = n_dp // per_piece
     table_piece(0, True)
@@ -882,18 +908,12 @@
             table_piece(p, False)
     else:
         lax.fori_loop(1, pieces, lambda p, c: (table_piece(p, False), c)[1], 0)
-    table_swap = swap(table_out, table_theirs, sibling)
+    table_swap = swap(whole_table, table_theirs, sibling)
     plan.run_until(plan.now + 8.0)
     table_swap.wait()
-    whole_table = r.whole_table
-    whole_table[...] = (
-        table_out[pl.ds(0, whole_table.shape[0]), :] + table_theirs[pl.ds(0, whole_table.shape[0]), :]
-    )[:, :table_rows]
+    whole_table[...] = whole_table[...] + table_theirs[...]
     store(whole_table, r.table_out)
     plan.finish()
-    if not low_bits:
-        rest = vocab_here - main
-        r.vocab_out[:, pl.ds(main, rest)] = r.rest_out[...][:, :rest]
     for copy in stores:
         copy.wait()
 
@@ -961,7 +981,7 @@
     dma = lambda *shape: pltpu.SemaphoreType.DMA(shape)
     inputs = dict(
         acoustic=(VMEM, acoustic),
-        table_tail=(VMEM, embedding[mains:]),
+        table_tail=(VMEM, embedding[mains + (table_rows - mains) // 16 * 16 :]),
         memory=(ANY, memory),
         table=(ANY, embedding),
         w_query_hbm=(ANY, w_query),
@@ -1027,7 +1047,6 @@
         grad_logits=v16(tokens, all_cols),
         grad_others=v16(3 * tokens, part_cols),
         top_turned=v16(width, 4 * tokens),
-        taken_mine=v32(utterances, slots, width),
         taken_theirs=v32(utterances, slots, width),
         grad_three=v32(utterances, slots, width),
         grad_two=v32(tokens, width),
@@ -1048,20 +1067,28 @@
         term_arrived=v32(n_dp, block_rows, slots),
         onehot_lo=v16(256, 512),
         table_rest=v16((table_rows - mains + 127) // 128 * 128, width),
-        table_theirs=v32(feature_rows, blocks_hi * 256),
-        table_mine=v32(feature_rows, blocks_hi * 256),
+        table_theirs=v32(features, table_rows),
         src_vocab=v32(*shape, part_cols),
         src_rest=v32(*shape, 128),
         whole_table=v32(features, table_rows),
         src_back=v32(*shape, units),
         vocab_sum=v32(*(2,) * len(plane), rows, part_cols),
+        rest_sum=v32(rows, 128),
+        vocab_whole=v32(rows, vocab_here),
+        in_sum=v32(rows, units),
+        back_sum=v32(rows, units),
+        query_sum=v32(rows, half),
+        out_sum=v32(rows, half),
+        key_sum=v32(rows, half),
+        value_sum=v32(rows, half),
+        loss_sum=v32(utterances, slots),
         vocab_traded=v32(3, rows, part_cols),
         src_in=v32(*shape, units),
         src_out=v32(*shape, half),
         src_query=v32(*shape, half),
         src_kv=v32(*shape, 2 * half),
         load_sem=dma(24),
-        store_sem=dma(24),
+        store_sem=dma(48),
         trade_send=dma(part_cols // 128, 3),
         trade_recv=dma(part_cols // 128, 3),
         swap_send=dma(40),
@@ -1092,7 +1119,7 @@
         kernel,
         out_shape=list(outputs.values()),
         in_specs=[spec for spec, _ in inputs.values()],
-        out_specs=[VMEM] * (len(outputs) - 3) + [ANY] * 3,
+        out_specs=[ANY] * len(outputs),
         scratch_shapes=list(scratch.values()) + flat,
         compiler_params=pltpu.CompilerParams(
             collective_id=1, has_side_effects=True, vmem_limit_bytes=64 << 20
@@ -1104,7 +1131,7 @@
 def deliver_kernel(n_dp, n_passed, *refs):
     n = n_passed + 2
     sources, targets, held = refs[:n], refs[n : 2 * n + 5], refs[2 * n + 5 : 3 * n + 5]
-    sem_in, sem_out = refs[3 * n + 5 :]
+    shaped, (sem_in, sem_out) = refs[3 * n + 5 : 3 * n + 12], refs[3 * n + 12 :]
     reads, writes = [], []
     for i, (source, buffer) in enumerate(zip(sources, held)):
         reads.append(pltpu.make_async_copy(source, buffer, sem_in.at[i]))
@@ -1116,19 +1143,22 @@
     reads[n_passed].wait()
     reads[n_passed + 1].wait()
     loss, small = held[n_passed:]
-    loss_to, gain_one_to, bias_one_to, gain_two_to, bias_two_to, taps_to, rate_to = targets[n_passed:]
+    loss_at, gain_one_at, bias_one_at, gain_two_at, bias_two_at, taps_at, rate_at = shaped
     slots = loss.shape[1]
     for u in range(loss.shape[0]):
-        loss_to[:, pl.ds(u * slots, slots)] = loss[pl.ds(u, 1), :]
+        loss_at[:, pl.ds(u * slots, slots)] = loss[pl.ds(u, 1), :]
     me = lax.axis_index("dp")
     own = small.shape[1] // n_dp
     mine = jnp.zeros((16, own), F32)
     for p in range(n_dp):
         mine = jnp.where(me == p, small[pl.ds(0, 16), p * own : (p + 1) * own], mine)
-    taps_to[...] = mine[: taps_to.shape[0]]
-    for i, target in enumerate((gain_one_to, bias_one_to, gain_two_to, bias_two_to)):
+    taps_at[...] = mine[: taps_at.shape[0]]
+    for i, target in enumerate((gain_one_at, bias_one_at, gain_two_at, bias_two_at)):
         target[...] = mine[12 + i : 13 + i]
-    rate_to[...] = small[pl.ds(16, 2), :]
+    rate_at[...] = small[pl.ds(16, 2), :]
+    for i, source in enumerate(shaped):
+        writes.append(pltpu.make_async_copy(source, targets[n_passed + i], sem_out.at[n_passed + i]))
+        writes[-1].start()
     for copy in writes:
         copy.wait()
 
@@ -1186,22 +1216,19 @@
     like = lambda x: jax.ShapeDtypeStruct(x.shape, F32)
     passed = (result.memory_out, result.table_out, result.acoustic_out, vocab, *summed)
     handed = (*passed, result.loss_out, result.small_out)
+    small_shapes = [
+        f32(1, tok_rows), *[f32(1, own)] * 4, f32(fsmn_kernel.shape[0], own), f32(2, model_width)
+    ]
     (
         grad_memory, grad_table, grad_acoustic, grad_vocab, grad_query, grad_key, grad_value,
         grad_out, grad_in, grad_back, token_loss, gain_1, bias_1, gain_2, bias_2, grad_taps, grad_rate,
     ) = pl.pallas_call(
         partial(deliver_kernel, n_dp, len(passed)),
-        out_shape=[
-            *[like(x) for x in passed],
-            f32(1, tok_rows),
-            *[f32(1, own)] * 4,
-            f32(fsmn_kernel.shape[0], own),
-            f32(2, model_width),
-        ],
+        out_shape=[*[like(x) for x in passed], *small_shapes],
         in_specs=[ANY] * len(handed),
-        out_specs=[ANY] * len(passed) + [VMEM] * 7,
-        scratch_shapes=[pltpu.VMEM(x.shape, F32) for x in handed]
-        + [pltpu.SemaphoreType.DMA((len(handed),)), pltpu.SemaphoreType.DMA((len(handed),))],
+        out_specs=[ANY] * (len(passed) + 7),
+        scratch_shapes=[pltpu.VMEM(x.shape, F32) for x in (*handed, *small_shapes)]
+        + [pltpu.SemaphoreType.DMA((len(handed),)), pltpu.SemaphoreType.DMA((len(passed) + 7,))],
         compiler_params=pltpu.CompilerParams(vmem_limit_bytes=60 << 20),
     )(*handed)
     return (

time: 129 us -> 129 us (level); the launches traced: 127 us -> 129 us
  Pallas kernels: 125 us -> 127 us
    pallas_call x1, Pallas kernels: 120 us -> 123 us  [decoder_call(): pl.pallas_call(kernel, out_shape=list(outputs.values()), in_specs=[spec f...]
where the time goes in v12:
time: 129 us
  Pallas kernels  127 us (98%)
  local copies, waits for them, and re-layouts  1.3 us (1%)
    pallas_call x1, Pallas kernels, decoder_call(): pl.pallas_call(kernel, out_shape=list(outputs.values()), in_specs=[spec f...  123 us
    pallas_call x1, Pallas kernels, per_device(): pl.pallas_call(partial(deliver_kernel, n_dp, len(passed)), out_shape=[*[l...  4.26 us

profile of v12, /device:TPU:0, one launch (start us, length us, event | category | flops | bytes accessed | tf_op | source)
XLA Modules:
  0.0 129.0 jit_solution(9876273695051063206)
XLA Ops:
  0.7 1.3 %slice.3.refs_1_ = bf16[4,512]{1,0:T(4,128)(2,1)} slice(bf16[8404,512]{1,0:T(8,128)(2,1)} %refs_3_.1), slice={[8400:8404], [0:512]} | slice | bytes 8192 | tf_op jit(solution)/shard_map/slice | solution.py:984
  2.0 122.6 %shard_map.332 = (f32[2,128]{1,0:T(2,128)}, f32[24,512]{1,0:T(8,128)}, f32[32,4202]{1,0:T(8,128)}, f32[32,128]{1,0:T(8,128)}, f32[32,1024]{1,0:T(8,128)}, /*inde...) custom-call(bf16[256,512]{1,0:T(8,128)(2,1)} %refs_0_.1, ...), custom_call_target="tpu_custom_call" | custom-call | tf_op jit(solution)/shard_map/pallas_call | solution.py:1118
  124.6 4.3 %shard_map.333 = (f32[2048,256]{1,0:T(8,128)}, f32[32,8404]{1,0:T(8,128)}, f32[256,512]{1,0:T(8,128)}, f32[32,4202]{1,0:T(8,128)}, f32[32,256]{1,0:T(8,128)}, /*...) custom-call(f32[2048,256]{1,0:T(8,128)} %get-tuple-element.46.refs_0, ...), custom_call_target="tpu_custom_call" | custom-call | tf_op jit(solution)/shard_map/pallas_call | solution.py:1225

commit v13 on v12

--- a/solution.py
+++ b/solution.py
@@ -69,7 +69,7 @@
 class Planner:
     RATE = 0.045e6
     HOP = 1.5
-    BACKLOG = 3.0
+    BACKLOG = 4.0
 
     def __init__(self):
         self.now = 0.0
@@ -190,6 +190,7 @@
     me, core = lax.axis_index("dp"), lax.axis_index("mp")
     sibling = {"mp": 1 - core}
     quarter = lax.rem(me, 4)
+    bit_0 = lax.rem(me, 2)
     flips = [1 - 2 * lax.rem(me, 2), 2 - 4 * lax.rem(me // 2, 2)]
     mate = [me + flips[0] * (j % 2) + flips[1] * (j // 2) for j in range(4)]
     bit_of = {b: lax.rem(me // (1 << b), 2) for b in low_bits + bits}
@@ -409,8 +410,13 @@
             two = stream_one[at, :] + (sent[u] + arrived[u])
             stream_two[at, :] = two
             hat, _ = normalise(two)
-            low = (hat * gain_2 + bias_2).astype(BF16)
+            norm = hat * gain_2 + bias_2
+            low = norm.astype(BF16)
             norm_low[at, :] = low
+            if second:
+                r.norm_wide[u] = norm
+                if u == utterances - 1:
+                    norm_swap = swap(r.norm_wide.at[core], r.norm_got.at[0], {"dp": mate[1]})
             pre = dot_nn(low, w_in[...])
             phi = 0.5 * (1.0 + lax.erf(pre * math.sqrt(0.5)))
             hidden[at, :] = (pre * phi).astype(BF16)
@@ -428,6 +434,7 @@
             three = stream_two[at, :] + (sent[utterances + u] + arrived[utterances + u])
             stream_three[u] = three
             top[0, at, :] = three.astype(BF16)
+        return norm_swap if second else None
 
     stream_in[...] = acoustic[...].astype(F32)
 
@@ -481,7 +488,7 @@
         taken = taken_mine[u] + taken_theirs[u]
         stream_in[at, :] = wide_acoustic + blend[u * slots : (u + 1) * slots] * (taken - wide_acoustic)
 
-    forward(True)
+    norm_swap = forward(True)
     token_swaps = [
         swap(stream_three.at[core], gathered.at[j - 1, 0], {"dp": mate[j]}) for j in (1, 2)
     ]
@@ -573,6 +580,13 @@
             if step < len(order) - 1:
                 got[...] = got[...] + ref[where]
                 return
+            if name in ("back", "in") and not low_bits:
+                here = pl.multiple_of(bit_0 * cols, cols)
+                there = pl.multiple_of((1 - bit_0) * cols, cols)
+                out[:, pl.ds(here, cols)] = ref[where]
+                out[:, pl.ds(there, cols)] = got[...]
+                store(out, final)
+                return
             out[..., at] = got[...] + ref[where]
             if low_bits or name not in ("vocab", "rest"):
                 store(out.at[..., at], final.at[..., at])
@@ -629,26 +643,14 @@
         source = getattr(r, "src_" + name)
         source[..., at] = product.reshape(source.shape[:-1] + (product.shape[1],))
 
-    copies = []
     for u in range(utterances):
-        at = rows(u)
         three_copies[u].wait()
         three = sent[u] + arrived[u]
         grad_three[u] = three
-        low = three.astype(BF16)
-        branch_low[at, :] = low
-        pre = (dot_nt(low, w_back[...]) * gelu_slope[at, :]).astype(BF16)
-        grad_pre[at, :] = pre
-        sent[utterances + u] = dot_nt(pre, w_in[...])
-        copies.append(swap(sent.at[utterances + u], arrived.at[utterances + u], sibling))
-    plan.run_until(plan.now + 8.0)
-    for name, left, right in (("back", branch_low, hidden), ("in", norm_low, grad_pre)):
-        left_turned = left[...].T
-        for start in sorted(s for n, s in chunks if n == name):
-            at = pl.ds(start, 512)
-            put(name, at, dot_nn(left_turned, right[:, at]))
-            plan.run_until(plan.now + 0.5)
-            plan.post(chunks[name, start])
+        branch_low[rows(u), :] = three.astype(BF16)
+    pair_swap = swap(grad_three.at[core], r.three_got.at[0], {"dp": mate[1]})
+    norm_swap.wait()
+    share_norm = swap(r.norm_got.at[0], r.norm_got.at[1], sibling)
 
     at_core = pl.ds(pl.multiple_of(core * slots, slots), slots)
     at_other = pl.ds(pl.multiple_of((1 - core) * slots, slots), slots)
@@ -675,7 +677,9 @@
     top_turned = r.top_turned
     for j in range(4):
         top_turned[:, pl.ds(j * tokens, tokens)] = top[j].T
-    plan.run_until(plan.now + 4.0)
+    plan.free[link_of(0, bits)] = 11.0
+    plan.free[link_of(1, bits)] = 6.0
+    plan.run_until(9.0)
     put("rest", slice(None), dot_nn(top_turned[:, pl.ds(0, tokens)], grad_logits[:, pl.ds(main, 128)]))
     starts = sorted(start for name, start in chunks if name == "vocab")
     for start, stop in zip(starts, starts[1:] + [part_cols]):
@@ -689,6 +693,44 @@
         plan.run_until(plan.now + 0.7)
         plan.post(chunks["vocab", start])
     plan.post(chunks["rest", 0])
+
+    copies = []
+    for u in range(utterances):
+        at = rows(u)
+        low = branch_low[at, :]
+        pre = (dot_nt(low, w_back[...]) * gelu_slope[at, :]).astype(BF16)
+        grad_pre[at, :] = pre
+        sent[utterances + u] = dot_nt(pre, w_in[...])
+        copies.append(swap(sent.at[utterances + u], arrived.at[utterances + u], sibling))
+    plan.run_until(plan.now + 3.0)
+    pair_swap.wait()
+    share_three = swap(r.three_got.at[0], r.three_got.at[1], sibling)
+    units_half = w_in.shape[1] // 2
+    mine = pl.ds(pl.multiple_of(bit_0 * units_half, units_half), units_half)
+    norm_mate, three_mate = r.norm_mate, r.three_mate
+    share_norm.wait()
+    norm_mate[at_core, :] = r.norm_got[0].astype(BF16)
+    norm_mate[at_other, :] = r.norm_got[1].astype(BF16)
+    pre = dot_nn(norm_mate[...], w_in[:, mine])
+    phi = 0.5 * (1.0 + lax.erf(pre * math.sqrt(0.5)))
+    r.hidden_mate[...] = (pre * phi).astype(BF16)
+    slope_mate = phi + pre * (jnp.exp(-0.5 * pre * pre) * (1.0 / math.sqrt(2.0 * math.pi)))
+    three_mate[at_core, :] = r.three_got[0].astype(BF16)
+    share_three.wait()
+    three_mate[at_other, :] = r.three_got[1].astype(BF16)
+    r.pre_mate[...] = (dot_nt(three_mate[...], w_back[mine, :]) * slope_mate).astype(BF16)
+    plan.run_until(plan.now + 2.0)
+    for name, left, right, left_mate, right_mate in (
+        ("back", branch_low, hidden, three_mate, r.hidden_mate),
+        ("in", norm_low, grad_pre, norm_mate, r.pre_mate),
+    ):
+        put(
+            name,
+            slice(None),
+            dot_nn(left[...].T, right[:, mine]) + dot_nn(left_mate[...].T, right_mate[...]),
+        )
+        plan.run_until(plan.now + 0.8)
+        plan.post(chunks[name, 0])
 
     one_copies = []
     gain_2_total, bias_2_total = 0.0, 0.0
@@ -929,13 +971,11 @@
     listing = []
     for start in range(0, part_cols, 512):
         listing.append(("vocab", start, 512, [b for b in bits if b > 1]))
+    last = [] if low_bits else [0]
+    for name in ("back", "in"):
+        listing.append((name, 0, sizes.units // 2, [b for b in bits if b > 0] + last))
     listing.append(("rest", 0, 128, bits))
-    for name, order in (("back", turned), ("in", bits)):
-        for start in range(0, sizes.units, 512):
-            if name == "in" and start:
-                order = [bits[2], bits[0], bits[1]] + bits[3:]
-            listing.append((name, start, 512, order))
-    listing.append(("out", 0, sizes.half, turned))
+    listing.append(("out", 0, sizes.half, bits))
     listing.append(("query", 0, sizes.half, bits))
     for k, start in enumerate(range(0, 2 * sizes.half, 256)):
         listing.append(("kv", start, 256, [bits, turned][k % 2]))
@@ -966,6 +1006,7 @@
         steps -= 1
     low_bits, bits = list(range(nbits - steps)), list(range(nbits - steps, nbits))
     rows = width >> steps
+    unit_cols = units // 2 if low_bits else units
     features = width // n_dp
     feature_rows = max(features, 8)
     block_rows = feature_rows + 8 if features >= 8 else 8
@@ -1008,8 +1049,8 @@
         small_out=f32(24, width),
         vocab_out=f32(2, rows, part_cols) if low_bits else f32(rows, vocab_here),
         rest_out=f32(rows, 128),
-        in_out=f32(rows, units),
-        back_out=f32(rows, units),
+        in_out=f32(rows, unit_cols),
+        back_out=f32(rows, unit_cols),
         query_out=f32(rows, half),
         out_out=f32(rows, half),
         key_out=f32(rows, half),
@@ -1071,19 +1112,26 @@
         src_vocab=v32(*shape, part_cols),
         src_rest=v32(*shape, 128),
         whole_table=v32(features, table_rows),
-        src_back=v32(*shape, units),
+        src_back=v32(*shape, units // 2),
         vocab_sum=v32(*(2,) * len(plane), rows, part_cols),
         rest_sum=v32(rows, 128),
         vocab_whole=v32(rows, vocab_here),
-        in_sum=v32(rows, units),
-        back_sum=v32(rows, units),
+        in_sum=v32(rows, unit_cols),
+        back_sum=v32(rows, unit_cols),
         query_sum=v32(rows, half),
         out_sum=v32(rows, half),
         key_sum=v32(rows, half),
         value_sum=v32(rows, half),
         loss_sum=v32(utterances, slots),
         vocab_traded=v32(3, rows, part_cols),
-        src_in=v32(*shape, units),
+        src_in=v32(*shape, units // 2),
+        norm_wide=v32(utterances, slots, width),
+        norm_got=v32(2, slots, width),
+        three_got=v32(2, slots, width),
+        norm_mate=v16(tokens, width),
+        three_mate=v16(tokens, width),
+        hidden_mate=v16(tokens, units // 2),
+        pre_mate=v16(tokens, units // 2),
         src_out=v32(*shape, half),
         src_query=v32(*shape, half),
         src_kv=v32(*shape, 2 * half),
@@ -1195,10 +1243,8 @@
         token_lengths, memory_lengths, rate_groups, glance_mask, targets, n_dp,
     )
     vocab = result.vocab_out
-    summed = [
-        result.query_out, result.key_out, result.value_out, result.out_out, result.in_out,
-        result.back_out,
-    ]
+    summed = [result.query_out, result.key_out, result.value_out, result.out_out]
+    halves = [result.in_out, result.back_out]
     if low_bits:
         size = 1 << len(low_bits)
         groups = [list(range(g * size, (g + 1) * size)) for g in range(n_dp // size)]
@@ -1211,10 +1257,23 @@
             for s in (*summed, result.rest_out)
         ]
         vocab = jnp.concatenate([*vocab, rest], axis=1)[:, : w_vocab.shape[1]]
+        pairs = [[2 * g, 2 * g + 1] for g in range(n_dp // 2)]
+        halves = [
+            jnp.concatenate(
+                [
+                    *lax.all_to_all(
+                        h.reshape(2, model_width // n_dp, -1), "dp", 0, 0, axis_index_groups=pairs,
+                        tiled=True,
+                    )
+                ],
+                axis=1,
+            )
+            for h in halves
+        ]
     own = model_width // n_dp
     f32 = lambda *shape: jax.ShapeDtypeStruct(shape, F32)
     like = lambda x: jax.ShapeDtypeStruct(x.shape, F32)
-    passed = (result.memory_out, result.table_out, result.acoustic_out, vocab, *summed)
+    passed = (result.memory_out, result.table_out, result.acoustic_out, vocab, *summed, *halves)
     handed = (*passed, result.loss_out, result.small_out)
     small_shapes = [
         f32(1, tok_rows), *[f32(1, own)] * 4, f32(fsmn_kernel.shape[0], own), f32(2, model_width)

time: 129 us -> 138 us (1.070)
  Pallas kernels: 127 us -> 135 us
    pallas_call x1, Pallas kernels: 123 us -> 131 us  [decoder_call(): pl.pallas_call(kernel, out_shape=list(outputs.values()), in_specs=[spec f...]
where the time goes in v13:
time: 138 us
  Pallas kernels  135 us (98%)
    pallas_call x1, Pallas kernels, decoder_call(): pl.pallas_call(kernel, out_shape=list(outputs.values()), in_specs=[spec f...  131 us
    pallas_call x1, Pallas kernels, per_device(): pl.pallas_call(partial(deliver_kernel, n_dp, len(passed)), out_shape=[*[l...  4.26 us

profile of v13, /device:TPU:0, one launch (start us, length us, event | category | flops | bytes accessed | tf_op | source)
XLA Modules:
  0.0 137.6 jit_solution(466656064976208193)
XLA Ops:
  0.7 1.3 slice.3.refs_1_
  2.0 131.2 %shard_map.332 = (f32[2,128]{1,0:T(2,128)}, f32[24,512]{1,0:T(8,128)}, f32[32,4202]{1,0:T(8,128)}, f32[32,128]{1,0:T(8,128)}, f32[32,1024]{1,0:T(8,128)}, /*inde...) custom-call(bf16[256,512]{1,0:T(8,128)(2,1)} %refs_0_.1, ...), custom_call_target="tpu_custom_call" | custom-call | tf_op jit(solution)/shard_map/pallas_call | solution.py:1166
  133.1 4.3 %shard_map.333 = (f32[2048,256]{1,0:T(8,128)}, f32[32,8404]{1,0:T(8,128)}, f32[256,512]{1,0:T(8,128)}, f32[32,4202]{1,0:T(8,128)}, f32[32,256]{1,0:T(8,128)}, /*...) custom-call(f32[2048,256]{1,0:T(8,128)} %get-tuple-element.46.refs_0, ...), custom_call_target="tpu_custom_call" | custom-call | tf_op jit(solution)/shard_map/pallas_call | solution.py:1284

commit v14 on v12

--- a/solution.py
+++ b/solution.py
@@ -68,8 +68,8 @@
 
 class Planner:
     RATE = 0.045e6
-    HOP = 1.5
-    BACKLOG = 3.0
+    HOP = 4.0
+    BACKLOG = 6.0
 
     def __init__(self):
         self.now = 0.0

time: 129 us -> 132 us (1.023)
  Pallas kernels: 127 us -> 130 us
    pallas_call x1, Pallas kernels: 123 us -> 126 us  [decoder_call(): pl.pallas_call(kernel, out_shape=list(outputs.values()), in_specs=[spec f...]
where the time goes in v14:
time: 132 us
  Pallas kernels  130 us (98%)
    pallas_call x1, Pallas kernels, decoder_call(): pl.pallas_call(kernel, out_shape=list(outputs.values()), in_specs=[spec f...  126 us
    pallas_call x1, Pallas kernels, per_device(): pl.pallas_call(partial(deliver_kernel, n_dp, len(passed)), out_shape=[*[l...  4.26 us

profile of v14, /device:TPU:0, one launch (start us, length us, event | category | flops | bytes accessed | tf_op | source)
XLA Modules:
  0.0 132.1 jit_solution(4479327070887243430)
XLA Ops:
  0.7 1.3 slice.3.refs_1_
  2.0 125.6 %shard_map.332 = (f32[2,128]{1,0:T(2,128)}, f32[24,512]{1,0:T(8,128)}, f32[32,4202]{1,0:T(8,128)}, f32[32,128]{1,0:T(8,128)}, f32[32,1024]{1,0:T(8,128)}, /*inde...) custom-call(bf16[256,512]{1,0:T(8,128)(2,1)} %refs_0_.1, ...), custom_call_target="tpu_custom_call" | custom-call | tf_op jit(solution)/shard_map/pallas_call | solution.py:1118
  127.6 4.3 %shard_map.333 = (f32[2048,256]{1,0:T(8,128)}, f32[32,8404]{1,0:T(8,128)}, f32[256,512]{1,0:T(8,128)}, f32[32,4202]{1,0:T(8,128)}, f32[32,256]{1,0:T(8,128)}, /*...) custom-call(f32[2048,256]{1,0:T(8,128)} %get-tuple-element.46.refs_0, ...), custom_call_target="tpu_custom_call" | custom-call | tf_op jit(solution)/shard_map/pallas_call | solution.py:1225

commit v15 on v12

--- a/solution.py
+++ b/solution.py
@@ -69,7 +69,7 @@
 class Planner:
     RATE = 0.045e6
     HOP = 1.5
-    BACKLOG = 3.0
+    BACKLOG = 1.0
 
     def __init__(self):
         self.now = 0.0

time: 129 us -> 139 us (1.078)
  Pallas kernels: 127 us -> 136 us
    pallas_call x1, Pallas kernels: 123 us -> 132 us  [decoder_call(): pl.pallas_call(kernel, out_shape=list(outputs.values()), in_specs=[spec f...]
where the time goes in v15:
time: 139 us; the launch traced here: 138 us
  Pallas kernels  136 us (98%)
    pallas_call x1, Pallas kernels, decoder_call(): pl.pallas_call(kernel, out_shape=list(outputs.values()), in_specs=[spec f...  132 us
    pallas_call x1, Pallas kernels, per_device(): pl.pallas_call(partial(deliver_kernel, n_dp, len(passed)), out_shape=[*[l...  4.26 us

profile of v15, /device:TPU:0, one launch (start us, length us, event | category | flops | bytes accessed | tf_op | source)
XLA Modules:
  0.0 138.4 jit_solution(16545828765192316179)
XLA Ops:
  0.7 1.3 slice.3.refs_1_
  2.0 132.0 %shard_map.332 = (f32[2,128]{1,0:T(2,128)}, f32[24,512]{1,0:T(8,128)}, f32[32,4202]{1,0:T(8,128)}, f32[32,128]{1,0:T(8,128)}, f32[32,1024]{1,0:T(8,128)}, /*inde...) custom-call(bf16[256,512]{1,0:T(8,128)(2,1)} %refs_0_.1, ...), custom_call_target="tpu_custom_call" | custom-call | tf_op jit(solution)/shard_map/pallas_call | solution.py:1118
  134.0 4.3 %shard_map.333 = (f32[2048,256]{1,0:T(8,128)}, f32[32,8404]{1,0:T(8,128)}, f32[256,512]{1,0:T(8,128)}, f32[32,4202]{1,0:T(8,128)}, f32[32,256]{1,0:T(8,128)}, /*...) custom-call(f32[2048,256]{1,0:T(8,128)} %get-tuple-element.46.refs_0, ...), custom_call_target="tpu_custom_call" | custom-call | tf_op jit(solution)/shard_map/pallas_call | solution.py:1225
